TPU v7x, 512 devices: a whole 4x4x16 slice. The times are simulated.
512 devices in a mesh: row: 32 (over y, x, core), col: 16 (over z).
Axes of the slice: x: 4, y: 4, z: 16, core: 2. Of those that a mesh axis runs over, the one named last changes fastest.
Arguments:
- hidden_in: bfloat16 [512, 8192], P('col', 'row'), may hold values from -6 to 6
- norm_mixer: float32 [8192], P('row'), may hold values from 0.5 to 1.5
- mixer_in: bfloat16 [8192, 4, 32, 128], P('row', None, 'col'), may hold values from -0.0625 to 0.0625
- bc_proj: bfloat16 [8192, 4, 512], P('row', None, 'col'), may hold values from -0.0625 to 0.0625
- dt_proj: bfloat16 [8192, 4, 32], P('row', None, 'col'), may hold values from -0.0625 to 0.0625
- dt_bias: float32 [4, 32], P(None, 'col'), may hold values from -5 to -1
- a_log: float32 [4, 32], P(None, 'col'), may hold values from -4 to 1
- skip_d: float32 [4, 32], P(None, 'col'), may hold values from 0.5 to 1.5
- conv_x: bfloat16 [4, 4, 2048], P(None, None, 'col'), may hold values from -3 to 3
- conv_bc: bfloat16 [4, 4, 512], replicated, may hold values from -3 to 3
- x_cache: bfloat16 [32, 4, 3, 2048], P('row', None, None, 'col'), may hold values from -6 to 6
- bc_cache: bfloat16 [32, 4, 3, 512], P('row'), may hold values from -6 to 6
- ssm_cache: float32 [32, 4, 32, 64, 256], P('row', None, 'col'), may hold values from -2 to 2
- slot_ids: int32 [8], replicated, may hold values from 0 to 3, as said below
- parents: int32 [8, 64], replicated, may hold values from -1 to 62, as said below
- ancestors: int32 [8, 64, 64], replicated, may hold values from 0 to 1, as said below
- norm_gated: float32 [4, 2048], P(None, 'col'), may hold values from 0.5 to 1.5
- out_proj: bfloat16 [4, 2048, 8192], P(None, 'col', 'row'), may hold values from -0.0625 to 0.0625
- norm_ffn: float32 [8192], P('row'), may hold values from 0.5 to 1.5
- ffn_up: bfloat16 [8192, 32768], P('row', 'col'), may hold values from -0.0625 to 0.0625
- ffn_down: bfloat16 [32768, 8192], P('col', 'row'), may hold values from -0.03125 to 0.03125
Outputs:
- hidden_out: bfloat16 [512, 8192], P('col', 'row')
Inputs may be any that keep to these rules, and one draw needn't show every extreme that they name: `parents`: node 0 of every tree is its root, with parent -1; every other node i has its parent among nodes max(i - 4, 0) to i - 1. ancestors[q, i, j] is 1 exactly when node j is node i or an ancestor of node i in request q's tree under parents, else 0. `slot_ids`: the first 4 requests hold 4 different slots (so one of them holds slot 3); the other requests may hold any slot.
All inputs are finite; a program needn't handle non-finite values.
Results may differ from a plain program's by a relative error of at most 0.04.
Values may be sent and summed in bfloat16 or wider, within the bound.
No kernel may reach another device: no remote copies, remote signals or barrier semaphores. Data moves between devices by JAX's collectives and lax.ppermute only.
A program may use at most 64 MiB of HBM per device.

v0:
```python
import jax
import jax.numpy as jnp
from jax import lax
from jax.sharding import PartitionSpec as P

D = 8192
H = 128
P_SIZE = 64
N = 256
G = 4


EPSILON = 1e-05
HIGHEST = lax.Precision.HIGHEST


def tree_conv(values, history, kernel, tree_parents, tree_anc):
    node_count = values.shape[0]
    tap_count = kernel.shape[0]
    positions = jnp.arange(node_count, dtype=jnp.int32)
    parent_hop = (tree_parents[:, None] == positions[None, :]).astype(jnp.float32)
    node_depth = jnp.sum(tree_anc, axis=1) - 1
    history_pos = jnp.arange(tap_count - 1, dtype=jnp.int32)
    running = kernel[tap_count - 1][None, :] * values
    ancestor_hop = parent_hop
    for distance in range(1, tap_count):
        from_tree = jnp.dot(ancestor_hop, values, precision=HIGHEST)
        cache_pick = (
            (distance > node_depth)[:, None]
            & (history_pos[None, :] == (tap_count - 1 - distance + node_depth)[:, None])
        ).astype(jnp.float32)
        from_cache = jnp.dot(cache_pick, history, precision=HIGHEST)
        running = running + kernel[tap_count - 1 - distance][None, :] * (from_tree + from_cache)
        ancestor_hop = jnp.dot(ancestor_hop, parent_hop, precision=HIGHEST)
    return jax.nn.silu(running)


def mixer_group(
    values,
    history,
    kernel,
    dt_raw,
    dt_offset,
    rate_log,
    skip_gain,
    start_state,
    gate_in,
    tree_parents,
    tree_anc,
):
    head_count = dt_raw.shape[1]
    head_width = head_count * P_SIZE
    conv_out = tree_conv(values, history, kernel, tree_parents, tree_anc)
    x_conv = conv_out[:, :head_width].reshape(-1, head_count, P_SIZE)
    b_matrix = conv_out[:, head_width : head_width + N]
    c_matrix = conv_out[:, head_width + N :]
    dt_step = jax.nn.softplus(dt_raw + dt_offset[None, :])
    log_decay = dt_step * (-jnp.exp(rate_log))[None, :]
    anc_float = tree_anc.astype(jnp.float32)
    cum_decay = jnp.dot(anc_float, log_decay, precision=HIGHEST)
    scores = jnp.dot(c_matrix, b_matrix.T, precision=HIGHEST)
    is_ancestor = tree_anc[:, :, None] > 0
    gaps_log = jnp.where(is_ancestor, cum_decay[:, None, :] - cum_decay[None, :, :], 0.0)
    weights = jnp.where(is_ancestor, jnp.exp(gaps_log), 0.0) * scores[:, :, None]
    inner_sum = jnp.einsum("ijh,jhp->ihp", weights, dt_step[:, :, None] * x_conv, precision=HIGHEST)
    carried = jnp.exp(cum_decay)[:, :, None] * jnp.einsum(
        "in,hpn->ihp", c_matrix, start_state, precision=HIGHEST
    )
    mixed_out = inner_sum + carried + skip_gain[None, :, None] * x_conv
    return mixed_out * jax.nn.silu(gate_in)


def local(
    hidden_in,
    norm_mixer,
    mixer_in,
    bc_proj,
    dt_proj,
    dt_bias,
    a_log,
    skip_d,
    conv_x,
    conv_bc,
    x_cache,
    bc_cache,
    ssm_cache,
    slot_ids,
    parents,
    ancestors,
    norm_gated,
    out_proj,
    norm_ffn,
    ffn_up,
    ffn_down,
):
    groups = mixer_in.shape[1]
    requests = slot_ids.shape[0]
    node_count = parents.shape[1]
    row_index = lax.axis_index("row")
    request = row_index // groups
    group_index = row_index % groups
    residual = hidden_in.astype(jnp.float32)
    mixer_sq = lax.psum(jnp.sum(residual * residual, axis=1), "row")
    mixer_normed = (
        residual * lax.rsqrt(mixer_sq[:, None] / D + EPSILON) * norm_mixer[None, :]
    ).astype(jnp.bfloat16)
    gathered = lax.all_gather(mixer_normed, "col", axis=0, tiled=True)
    tokens = gathered.reshape(requests, node_count, gathered.shape[1])
    xz_term = jnp.einsum("qtd,dghe->qgthe", tokens, mixer_in, preferred_element_type=jnp.float32)
    xz_term = xz_term.reshape(requests * groups, node_count, -1)
    dt_term = jnp.einsum("qtd,dgh->qgth", tokens, dt_proj, preferred_element_type=jnp.float32)
    dt_term = dt_term.reshape(requests * groups, node_count, -1)
    bc_term = jnp.einsum("qtd,dge->qgte", tokens, bc_proj, preferred_element_type=jnp.float32)
    bc_term = bc_term.reshape(requests * groups, node_count, -1)
    xz_sum, dt_sum, bc_sum = (
        lax.psum_scatter(
            xz_term.astype(jnp.bfloat16), "row", scatter_dimension=0, tiled=True
        ).astype(jnp.float32),
        lax.psum_scatter(
            dt_term.astype(jnp.bfloat16), "row", scatter_dimension=0, tiled=True
        ).astype(jnp.float32),
        lax.psum_scatter(
            bc_term.astype(jnp.bfloat16), "row", scatter_dimension=0, tiled=True
        ).astype(jnp.float32),
    )
    head_count = dt_sum.shape[2]
    xz_local = xz_sum[0].reshape(node_count, head_count, 2 * P_SIZE)
    x_new = xz_local[:, :, :P_SIZE].reshape(node_count, head_count * P_SIZE)
    gate_in = xz_local[:, :, P_SIZE:]
    bc_new = lax.all_gather(bc_sum[0], "col", axis=1, tiled=True)
    slot_index = lax.dynamic_index_in_dim(slot_ids, request, 0, keepdims=False)
    tree_parents = lax.dynamic_index_in_dim(parents, request, 0, keepdims=False)
    tree_anc = lax.dynamic_index_in_dim(ancestors, request, 0, keepdims=False)
    x_hist = lax.dynamic_index_in_dim(x_cache[0], slot_index, 0, keepdims=False)
    bc_hist = lax.dynamic_index_in_dim(bc_cache[0], slot_index, 0, keepdims=False)
    start_state = lax.dynamic_index_in_dim(ssm_cache[0], slot_index, 0, keepdims=False)
    history = jnp.concatenate([x_hist, bc_hist], axis=1).astype(jnp.float32)
    kernel = jnp.concatenate(
        [
            lax.dynamic_index_in_dim(conv_x, group_index, 1, keepdims=False),
            lax.dynamic_index_in_dim(conv_bc, group_index, 1, keepdims=False),
        ],
        axis=1,
    ).astype(jnp.float32)
    values = jnp.concatenate([x_new, bc_new], axis=1)

    def pick_group(table):
        return lax.dynamic_index_in_dim(table, group_index, 0, keepdims=False)

    gated = mixer_group(
        values,
        history,
        kernel,
        dt_sum[0],
        pick_group(dt_bias),
        pick_group(a_log),
        pick_group(skip_d),
        start_state,
        gate_in,
        tree_parents,
        tree_anc,
    )
    group_sq = lax.psum(jnp.sum(gated * gated, axis=(1, 2)), "col")
    gated_flat = gated.reshape(node_count, -1)
    mixed_heads = (
        gated_flat
        * lax.rsqrt(group_sq[:, None] / (H // G * P_SIZE) + EPSILON)
        * pick_group(norm_gated)[None, :]
    ).astype(jnp.bfloat16)
    all_heads = lax.all_gather(mixed_heads[None], "row", axis=0, tiled=True)
    all_heads = all_heads.reshape(requests, groups, node_count, -1)
    mixer_term = jnp.einsum(
        "qgtc,gcd->qtd", all_heads, out_proj, preferred_element_type=jnp.float32
    )
    mixer_out = lax.psum_scatter(
        mixer_term.reshape(requests * node_count, -1).astype(jnp.bfloat16),
        "col",
        scatter_dimension=0,
        tiled=True,
    ).astype(jnp.float32)
    after = (residual + mixer_out).astype(jnp.bfloat16)
    after_wide = after.astype(jnp.float32)
    ffn_sq = lax.psum(jnp.sum(after_wide * after_wide, axis=1), "row")
    ffn_normed = (after_wide * lax.rsqrt(ffn_sq[:, None] / D + EPSILON) * norm_ffn[None, :]).astype(
        jnp.bfloat16
    )
    up_term = jnp.dot(
        lax.all_gather(ffn_normed, "col", axis=0, tiled=True),
        ffn_up,
        preferred_element_type=jnp.float32,
    )
    up_share = lax.psum_scatter(
        up_term.astype(jnp.bfloat16), "row", scatter_dimension=0, tiled=True
    ).astype(jnp.float32)
    act_share = jnp.square(jax.nn.relu(up_share)).astype(jnp.bfloat16)
    act_all = lax.all_gather(act_share, "row", axis=0, tiled=True)
    ffn_out = lax.psum_scatter(
        jnp.dot(act_all, ffn_down, preferred_element_type=jnp.float32).astype(jnp.bfloat16),
        "col",
        scatter_dimension=0,
        tiled=True,
    ).astype(jnp.float32)
    return (after_wide + ffn_out).astype(jnp.bfloat16)


def solution(mesh):
    return jax.shard_map(
        local,
        mesh=mesh,
        in_specs=(
            P("col", "row"),
            P("row"),
            P("row", None, "col", None),
            P("row", None, "col"),
            P("row", None, "col"),
            P(None, "col"),
            P(None, "col"),
            P(None, "col"),
            P(None, None, "col"),
            P(),
            P("row", None, None, "col"),
            P("row", None, None, None),
            P("row", None, "col", None, None),
            P(),
            P(),
            P(),
            P(None, "col"),
            P(None, "col", "row"),
            P("row"),
            P("row", "col"),
            P("col", "row"),
        ),
        out_specs=P("col", "row"),
        check_vma=False,
    )
```

profile of v0, /device:TPU:4, one launch (start us, length us, event | category | flops | bytes accessed | tf_op | source)
XLA Modules:
  0.0 766.7 jit_solution(11946104521999442471)
XLA Ops:
  6.5 0.9 fusion.28
  7.5 57.9 %psum.21 = f32[32]{0:T(128)S(1)} all-reduce(f32[32]{0:T(128)S(1)} %fusion.28), channel_id=1, replica_groups=mesh['row'=32,'col'=16] {'row'}, use_global_device_ids=true, to_apply=%region_1.2 | all-reduce | flops 32 | bytes 256 | tf_op jit(solution)/shard_map/psum | solution.py:103
  65.4 0.8 fusion.30
  66.2 36.0 %all_gather.15 = bf16[512,256]{1,0:T(8,128)(2,1)S(1)} all-gather(bf16[32,256]{1,0:T(8,128)(2,1)S(1)} %fusion.30), channel_id=1, replica_groups=mesh['row'=32,'col'=16] {'col'}, dimensions={0}, use_global_device_ids=true | all-gather | bytes 278528 | tf_op jit(solution)/shard_map/all_gather | solution.py:107
  102.3 1.8 convolution_convert_fusion.3
  104.2 1.5 fusion
  105.6 1.1 copy.56
  106.8 1.5 convert_element_type.104
  108.4 0.9 dynamic-slice_reduce_fusion
  109.4 0.6 dynamic_slice.51
  111.3 0.8 compare_bitcast_fusion
  112.7 0.7 fusion.91
  113.5 0.2 fusion.11
  113.8 123.8 %all-reduce = bf16[32,64,2]{1,2,0:T(2,128)(2,1)S(1)} all-reduce(bf16[32,64,2]{1,2,0:T(2,128)(2,1)S(1)} %copy.54), channel_id=3, replica_groups=mesh['row'=32,'col'=16] {'row'}, use_global_device_ids=true, to_apply=%region_2.3.clone | all-reduce | flops 4096 | bytes 16384
  237.6 0.2 fusion.86
  237.9 1.3 dynamic-slice.3
  239.1 0.7 compare_select_fusion.1
  239.8 0.7 fusion.92
  240.8 1.6 fusion.101
  242.4 0.2 fusion.44
  242.6 0.2 fusion.43
  242.9 0.2 fusion.50
  243.1 0.2 fusion.53
  243.3 0.2 fusion.47
  243.6 0.7 squeeze.55
  244.3 27.3 %all-gather = f32[1,64,512]{1,0,2:T(1,128)S(1)} all-gather(f32[1,64,32]{1,0,2:T(1,128)S(1)} %bitcast.133), channel_id=2, replica_groups=mesh['row'=32,'col'=16] {'col'}, dimensions={2}, use_global_device_ids=true | all-gather | bytes 139264 | tf_op jit(solution)/shard_map/all_gather | solution.py:130
  271.7 37.7 %reduce-scatter.6.cloned.1.call-done = bf16[1,64,256]{2,1,0:T(8,128)(2,1)} async-done(((bf16[32,64,256]{2,1,0:T(8,128)(2,1)}), bf16[1,64,256]{2,1,0:T(8,128)(2,1)}) %reduce-scatter.6.cloned.1.call-update) | async-done | bytes 32784 | tf_op jit(solution)/shard_map/reduce_scatter | solution.py:116
  309.4 0.9 copy.57
  310.3 0.3 fusion.6
  310.6 0.3 fusion.7
  310.9 0.3 divide_multiply_fusion
  311.6 0.3 convolution_bitcast_fusion.1
  311.9 1.2 multiply_reduce_fusion
  313.2 31.3 %psum.22 = f32[64]{0:T(128)S(1)} all-reduce(f32[64]{0:T(128)S(1)} %get-tuple-element.16), channel_id=1, replica_groups=mesh['row'=32,'col'=16] {'col'}, use_global_device_ids=true, to_apply=%region_7.8 | all-reduce | flops 64 | bytes 512 | tf_op jit(solution)/shard_map/psum | solution.py:163
  344.6 22.9 %all_gather.17 = bf16[32,64,128]{2,1,0:T(8,128)(2,1)S(1)} all-gather(bf16[1,64,128]{2,1,0:T(8,128)(2,1)S(1)} %multiply_convert_fusion.1), channel_id=1, replica_groups=mesh['row'=32,'col'=16] {'row'}, dimensions={0}, use_global_device_ids=true | all-gather | bytes 540672 | tf_op jit(solution)/shard_map/all_gather | solution.py:170
  367.6 1.0 fusion.1
  368.6 65.6 %reduce-scatter.10.cloned.1.call-done = bf16[32,256]{1,0:T(8,128)(2,1)} async-done(((bf16[512,256]{1,0:T(8,128)(2,1)}), bf16[32,256]{1,0:T(8,128)(2,1)}) %reduce-scatter.10.cloned.1.call-update) | async-done | bytes 16400 | tf_op jit(solution)/shard_map/reduce_scatter | solution.py:175
  434.2 0.8 fusion.32
  435.1 52.6 %psum.23 = f32[32]{0:T(128)S(1)} all-reduce(f32[32]{0:T(128)S(1)} %fusion.32), channel_id=1, replica_groups=mesh['row'=32,'col'=16] {'row'}, use_global_device_ids=true, to_apply=%region_10.11 | all-reduce | flops 32 | bytes 256 | tf_op jit(solution)/shard_map/psum | solution.py:183
  487.7 0.8 fusion.34
  488.5 28.8 %all_gather.18 = bf16[512,256]{1,0:T(8,128)(2,1)S(1)} all-gather(bf16[32,256]{1,0:T(8,128)(2,1)S(1)} %fusion.34), channel_id=1, replica_groups=mesh['row'=32,'col'=16] {'col'}, dimensions={0}, use_global_device_ids=true | all-gather | bytes 278528 | tf_op jit(solution)/shard_map/all_gather | solution.py:188
  517.3 2.1 convolution_convert_fusion
  519.5 105.7 %reduce-scatter.12.cloned.1.call-done = bf16[16,2048]{1,0:T(8,128)(2,1)} async-done(((bf16[512,2048]{1,0:T(8,128)(2,1)}), bf16[16,2048]{1,0:T(8,128)(2,1)}) %reduce-scatter.12.cloned.1.call-update) | async-done | bytes 65552 | tf_op jit(solution)/shard_map/reduce_scatter | solution.py:192
  625.1 1.5 multiply_convert_fusion
  626.7 59.9 %all-gather.3.cloned.1.call-done = bf16[512,2048]{1,0:T(8,128)(2,1)} async-done(((bf16[16,2048]{1,0:T(8,128)(2,1)}), bf16[512,2048]{1,0:T(8,128)(2,1)}) %all-gather.3.cloned.1.call-update) | async-done | bytes 2097168 | tf_op jit(solution)/shard_map/all_gather | solution.py:196
  686.6 3.0 convolution_convert_fusion.2
  689.6 68.8 %reduce-scatter.14.cloned.1.call-done = bf16[32,256]{1,0:T(8,128)(2,1)} async-done(((bf16[512,256]{1,0:T(8,128)(2,1)}), bf16[32,256]{1,0:T(8,128)(2,1)}) %reduce-scatter.14.cloned.1.call-update) | async-done | bytes 16400 | tf_op jit(solution)/shard_map/reduce_scatter | solution.py:197
  758.5 1.3 fusion.35
  (70 shorter events, 1.4 us)
Async XLA Ops:
  6.5 510.8 %copy-start = (bf16[256,2048]{1,0:T(8,128)(2,1)S(1)}, bf16[256,2048]{1,0:T(8,128)(2,1)}, u32[]{:S(2)}) copy-start(bf16[256,2048]{1,0:T(8,128)(2,1)} %param.40) | copy-start | bytes 3145732
  6.5 237.0 %reduce-scatter.8.cloned.1.call-start = ((), (), s32[]{:S(2)}) async-start(), calls=%async_computation.6 | async-start | bytes 270336 | tf_op jit(solution)/shard_map/reduce_scatter | solution.py:122
  104.1 205.3 %reduce-scatter.6.cloned.1.call-start = ((), (), s32[]{:S(2)}) async-start(), calls=%async_computation.5 | async-start | bytes 1081344 | tf_op jit(solution)/shard_map/reduce_scatter | solution.py:116
  106.7 2.6 copy-start.14
  106.7 5.9 copy-start.6
  106.8 6.0 copy-start.12
  106.8 6.7 copy-start.5
  106.8 6.7 copy-start.10
  106.8 6.7 copy-start.4
  106.8 130.8 %copy-start.7 = (f32[4,2]{0,1:T(2,128)S(1)}, f32[4,2]{0,1:T(2,128)}, u32[]{:S(2)}) copy-start(f32[4,2]{0,1:T(2,128)} %param.26) | copy-start | bytes 100
  106.8 130.8 %copy-start.8 = (f32[4,2]{0,1:T(2,128)S(1)}, f32[4,2]{0,1:T(2,128)}, u32[]{:S(2)}) copy-start(f32[4,2]{0,1:T(2,128)} %param.27) | copy-start | bytes 100
  106.8 133.7 %copy-start.11 = (f32[4,2]{0,1:T(2,128)S(1)}, f32[4,2]{0,1:T(2,128)}, u32[]{:S(2)}) copy-start(f32[4,2]{0,1:T(2,128)} %param.28) | copy-start | bytes 100
  108.4 325.9 %reduce-scatter.10.cloned.1.call-start = ((), (), s32[]{:S(2)}) async-start(), calls=%async_computation.7 | async-start | bytes 278528 | tf_op jit(solution)/shard_map/reduce_scatter | solution.py:175
  310.6 56.9 %copy-start.2 = (bf16[4,128,256]{2,1,0:T(8,128)(2,1)S(1)}, bf16[4,128,256]{2,1,0:T(8,128)(2,1)}, u32[]{:S(2)}) copy-start(bf16[4,128,256]{2,1,0:T(8,128)(2,1)} %param.38) | copy-start | bytes 786436
  311.3 123.0 %copy-start.1 = (bf16[32,256]{1,0:T(8,128)(2,1)S(1)}, bf16[32,256]{1,0:T(8,128)(2,1)}, u32[]{:S(2)}) copy-start(bf16[32,256]{1,0:T(8,128)(2,1)} %param.21) | copy-start | bytes 49156
  311.3 176.4 %copy-start.9 = (f32[256]{0:T(256)S(1)}, f32[256]{0:T(256)}, u32[]{:S(2)}) copy-start(f32[256]{0:T(256)} %param.39) | copy-start | bytes 3076
  368.6 256.5 %reduce-scatter.12.cloned.1.call-start = ((), (), s32[]{:S(2)}) async-start(), calls=%async_computation.8 | async-start | bytes 2162688 | tf_op jit(solution)/shard_map/reduce_scatter | solution.py:192
  517.3 169.3 %copy-start.13 = (bf16[2048,256]{1,0:T(8,128)(2,1)S(1)}, bf16[2048,256]{1,0:T(8,128)(2,1)}, u32[]{:S(2)}) copy-start(bf16[2048,256]{1,0:T(8,128)(2,1)} %param.41) | copy-start | bytes 3145732
  519.4 167.2 %all-gather.3.cloned.1.call-start = ((), (), s32[]{:S(2)}) async-start(), calls=%async_computation.9 | async-start | bytes 2162688 | tf_op jit(solution)/shard_map/all_gather | solution.py:196
  626.6 131.9 %copy-start.3 = (bf16[32,256]{1,0:T(8,128)(2,1)S(1)}, bf16[32,256]{1,0:T(8,128)(2,1)}, u32[]{:S(2)}) copy-start(bf16[32,256]{1,0:T(8,128)(2,1)} %reduce-scatter.10.cloned.1.call-done) | copy-start | bytes 49156
  626.6 131.9 %reduce-scatter.14.cloned.1.call-start = ((), (), s32[]{:S(2)}) async-start(), calls=%async_computation.10 | async-start | bytes 278528 | tf_op jit(solution)/shard_map/reduce_scatter | solution.py:197
Sparse Core Ops, SparseCore 0:
  104.2 100.6 reduce-scatter.7
  209.3 100.0 reduce-scatter.5
  368.7 65.4 reduce-scatter.9
  519.5 105.5 reduce-scatter.11
  628.1 58.4 all-gather.2
  689.8 68.6 reduce-scatter.13
where the time goes:
time: 768 us; the launch traced here: 767 us
  blocking collectives  381 us (50%)
  waiting for transfers between devices  338 us (44%)
  between operations  15.8 us (2%)
  matrix products  15 us (2%)
  other arithmetic  9.54 us (1%)
    unnamed x1, blocking collectives  124 us
    reduce_scatter x1, waiting for transfers between devices, local(): lax.psum_scatter(up_term.astype(jnp.bfloat16), 'row', scatter_dimension=0...  106 us
    reduce_scatter x1, waiting for transfers between devices, local(): lax.psum_scatter(jnp.dot(act_all, ffn_down, preferred_element_type=jnp.fl...  68.8 us
    reduce_scatter x1, waiting for transfers between devices, local(): lax.psum_scatter(mixer_term.reshape(requests * node_count, -1).astype(jnp...  65.6 us
    all_gather x1, waiting for transfers between devices, local(): act_all = lax.all_gather(act_share, 'row', axis=0, tiled=True)  59.9 us
    psum x1, blocking collectives, local(): mixer_sq = lax.psum(jnp.sum(residual * residual, axis=1), 'row')  57.9 us
    psum x1, blocking collectives, local(): ffn_sq = lax.psum(jnp.sum(after_wide * after_wide, axis=1), 'row')  52.6 us
    reduce_scatter x1, waiting for transfers between devices, local(): lax.psum_scatter(xz_term.astype(jnp.bfloat16), 'row', scatter_dimension=0...  37.7 us
  transfers between devices with their start and end apart: 6, of which 5 were waited for; matrix products, arithmetic and copies ran while one was open for 2% of the time, Pallas kernels for 0%

commit v1 on v0

--- a/solution.py
+++ b/solution.py
@@ -70,6 +70,11 @@
     return mixed_out * jax.nn.silu(gate_in)
 
 
+def sum_parts(parts, axis):
+    received = lax.all_to_all(parts, axis, 0, 0, tiled=True)
+    return jnp.sum(received.astype(jnp.float32), axis=0)
+
+
 def local(
     hidden_in,
     norm_mixer,
@@ -99,30 +104,30 @@
     row_index = lax.axis_index("row")
     request = row_index // groups
     group_index = row_index % groups
+    rows = lax.axis_size("row")
+    cols = lax.axis_size("col")
     residual = hidden_in.astype(jnp.float32)
-    mixer_sq = lax.psum(jnp.sum(residual * residual, axis=1), "row")
-    mixer_normed = (
-        residual * lax.rsqrt(mixer_sq[:, None] / D + EPSILON) * norm_mixer[None, :]
-    ).astype(jnp.bfloat16)
-    gathered = lax.all_gather(mixer_normed, "col", axis=0, tiled=True)
-    tokens = gathered.reshape(requests, node_count, gathered.shape[1])
+    all_hidden = lax.all_gather(hidden_in, "col", axis=0, tiled=True).astype(jnp.float32)
+    mixer_part = jnp.sum(all_hidden * all_hidden, axis=1)
+    tokens = (all_hidden * norm_mixer[None, :]).astype(jnp.bfloat16)
+    tokens = tokens.reshape(requests, node_count, tokens.shape[1])
     xz_term = jnp.einsum("qtd,dghe->qgthe", tokens, mixer_in, preferred_element_type=jnp.float32)
-    xz_term = xz_term.reshape(requests * groups, node_count, -1)
+    xz_term = xz_term.reshape(rows, node_count, -1)
     dt_term = jnp.einsum("qtd,dgh->qgth", tokens, dt_proj, preferred_element_type=jnp.float32)
-    dt_term = dt_term.reshape(requests * groups, node_count, -1)
+    dt_term = dt_term.reshape(rows, node_count, -1)
     bc_term = jnp.einsum("qtd,dge->qgte", tokens, bc_proj, preferred_element_type=jnp.float32)
-    bc_term = bc_term.reshape(requests * groups, node_count, -1)
-    xz_sum, dt_sum, bc_sum = (
-        lax.psum_scatter(
-            xz_term.astype(jnp.bfloat16), "row", scatter_dimension=0, tiled=True
-        ).astype(jnp.float32),
-        lax.psum_scatter(
-            dt_term.astype(jnp.bfloat16), "row", scatter_dimension=0, tiled=True
-        ).astype(jnp.float32),
-        lax.psum_scatter(
-            bc_term.astype(jnp.bfloat16), "row", scatter_dimension=0, tiled=True
-        ).astype(jnp.float32),
-    )
+    bc_term = bc_term.reshape(rows, node_count, -1)
+    sq_term = jnp.broadcast_to(
+        mixer_part.reshape(requests, 1, node_count, 1), (requests, groups, node_count, 1)
+    ).reshape(rows, node_count, 1)
+    widths = [xz_term.shape[2], bc_term.shape[2], dt_term.shape[2]]
+    in_term = jnp.concatenate([xz_term, bc_term, dt_term, sq_term], axis=2).astype(jnp.bfloat16)
+    in_sum = sum_parts(in_term, "row")
+    scale = lax.rsqrt(in_sum[:, -1:] / D + EPSILON)
+    in_sum = in_sum[:, :-1] * scale
+    xz_sum = in_sum[None, :, : widths[0]]
+    bc_sum = in_sum[None, :, widths[0] : widths[0] + widths[1]]
+    dt_sum = in_sum[None, :, widths[0] + widths[1] :]
     head_count = dt_sum.shape[2]
     xz_local = xz_sum[0].reshape(node_count, head_count, 2 * P_SIZE)
     x_new = xz_local[:, :, :P_SIZE].reshape(node_count, head_count * P_SIZE)
@@ -172,35 +177,28 @@
     mixer_term = jnp.einsum(
         "qgtc,gcd->qtd", all_heads, out_proj, preferred_element_type=jnp.float32
     )
-    mixer_out = lax.psum_scatter(
-        mixer_term.reshape(requests * node_count, -1).astype(jnp.bfloat16),
-        "col",
-        scatter_dimension=0,
-        tiled=True,
-    ).astype(jnp.float32)
+    mixer_out = sum_parts(
+        mixer_term.reshape(cols, -1, mixer_term.shape[-1]).astype(jnp.bfloat16), "col"
+    )
     after = (residual + mixer_out).astype(jnp.bfloat16)
-    after_wide = after.astype(jnp.float32)
-    ffn_sq = lax.psum(jnp.sum(after_wide * after_wide, axis=1), "row")
-    ffn_normed = (after_wide * lax.rsqrt(ffn_sq[:, None] / D + EPSILON) * norm_ffn[None, :]).astype(
-        jnp.bfloat16
-    )
+    all_after = lax.all_gather(after, "col", axis=0, tiled=True).astype(jnp.float32)
+    ffn_part = jnp.sum(all_after * all_after, axis=1)
     up_term = jnp.dot(
-        lax.all_gather(ffn_normed, "col", axis=0, tiled=True),
+        (all_after * norm_ffn[None, :]).astype(jnp.bfloat16),
         ffn_up,
         preferred_element_type=jnp.float32,
     )
-    up_share = lax.psum_scatter(
-        up_term.astype(jnp.bfloat16), "row", scatter_dimension=0, tiled=True
-    ).astype(jnp.float32)
+    up_term = jnp.concatenate([up_term, ffn_part[:, None]], axis=1).astype(jnp.bfloat16)
+    up_sum = sum_parts(up_term.reshape(rows, -1, up_term.shape[1]), "row")
+    up_share = up_sum[:, :-1] * lax.rsqrt(up_sum[:, -1:] / D + EPSILON)
     act_share = jnp.square(jax.nn.relu(up_share)).astype(jnp.bfloat16)
-    act_all = lax.all_gather(act_share, "row", axis=0, tiled=True)
-    ffn_out = lax.psum_scatter(
-        jnp.dot(act_all, ffn_down, preferred_element_type=jnp.float32).astype(jnp.bfloat16),
-        "col",
-        scatter_dimension=0,
-        tiled=True,
-    ).astype(jnp.float32)
-    return (after_wide + ffn_out).astype(jnp.bfloat16)
+    act_all = lax.all_to_all(
+        jnp.broadcast_to(act_share[None], (rows,) + act_share.shape), "row", 0, 0, tiled=True
+    )
+    act_all = act_all.reshape(-1, act_all.shape[-1])
+    ffn_term = jnp.dot(act_all, ffn_down, preferred_element_type=jnp.float32).astype(jnp.bfloat16)
+    ffn_out = sum_parts(ffn_term.reshape(cols, -1, ffn_term.shape[1]), "col")
+    return (after.astype(jnp.float32) + ffn_out).astype(jnp.bfloat16)
 
 
 def solution(mesh):

time: 768 us -> 315 us (0.41)
  the two profiles are of different devices: /device:TPU:4 before, /device:TPU:32 now
where the time goes in v1:
time: 315 us; the launch traced here: 314 us
  blocking collectives  263 us (83%)
  waiting for transfers between devices  16.6 us (5%)
  matrix products  8.85 us (3%)
  other arithmetic  7.83 us (2%)
  local copies, waits for them, and re-layouts  7.73 us (2%)
  starting transfers between devices  7.47 us (2%)
    all_to_all x3, blocking collectives, sum_parts(): received = lax.all_to_all(parts, axis, 0, 0, tiled=True)  87.8 us
    all_gather x1, blocking collectives, local(): lax.all_gather(hidden_in, 'col', axis=0, tiled=True).astype(jnp.float32)  35 us
    all_to_all x1, blocking collectives, local(): lax.all_to_all(jnp.broadcast_to(act_share[None], (rows,) + act_share.shap...  32.2 us
    all_gather x1, blocking collectives, local(): bc_new = lax.all_gather(bc_sum[0], 'col', axis=1, tiled=True)  29.6 us
    all_gather x1, blocking collectives, local(): lax.all_gather(after, 'col', axis=0, tiled=True).astype(jnp.float32)  28.7 us
    psum x1, blocking collectives, local(): group_sq = lax.psum(jnp.sum(gated * gated, axis=(1, 2)), 'col')  27.2 us
    all_gather x1, blocking collectives, local(): all_heads = lax.all_gather(mixed_heads[None], 'row', axis=0, tiled=True)  22.4 us
    all_to_all x1, waiting for transfers between devices, sum_parts(): received = lax.all_to_all(parts, axis, 0, 0, tiled=True)  16.6 us
  transfers between devices with their start and end apart: 1, of which 1 were waited for; matrix products, arithmetic and copies ran while one was open for 2% of the time, Pallas kernels for 0%

profile of v1, /device:TPU:32, one launch (start us, length us, event | category | flops | bytes accessed | tf_op | source)
XLA Modules:
  0.0 313.7 jit_solution(13378187001837956240)
XLA Ops:
  0.0 35.0 %all_gather.12 = bf16[512,256]{1,0:T(8,128)(2,1)S(1)} all-gather(bf16[32,256]{1,0:T(8,128)(2,1)} %param.21), channel_id=1, replica_groups=mesh['row'=32,'col'=16] {'col'}, dimensions={0}, use_global_device_ids=true | all-gather | bytes 278528 | tf_op jit(solution)/shard_map/all_gather | solution.py:110
  35.0 0.8 fusion.12
  35.8 1.1 convolution_convert_fusion.3
  37.0 1.0 copy.108
  38.0 0.9 fusion.11
  38.9 1.1 copy.109
  40.0 0.4 fusion
  40.4 1.1 copy.105
  41.5 0.7 reshape.159
  42.3 0.3 copy.110
  42.7 2.9 pad_maximum_fusion.1
  45.7 7.5 %all-to-all-start = ((bf16[32,64,291]{2,1,0:T(8,128)(2,1)}), bf16[32,64,291]{2,1,0:T(8,128)(2,1)S(1)}, u32[]{:S(2)}, u32[]{:S(2)}) async-start(bf16[32,64,291]{2,1,0:T(8,128)(2,1)} %pad_maximum_fusion.1), calls=%async_computation | async-start | bytes 3145728 | tf_op jit(solution)/shard_map/all_to_all | solution.py:74
  53.2 0.6 dynamic_slice.51
  55.1 0.9 dynamic-slice_reduce_fusion
  56.0 0.8 compare_bitcast_fusion
  57.6 0.7 fusion.84
  58.3 0.7 fusion.85
  59.0 0.2 fusion.81
  59.2 0.2 fusion.78
  59.4 0.2 fusion.49
  59.6 0.2 fusion.48
  59.9 0.2 fusion.55
  60.1 0.2 fusion.58
  60.3 0.2 fusion.52
  60.5 16.6 %all-to-all-done = bf16[32,64,291]{2,1,0:T(8,128)(2,1)S(1)} async-done(((bf16[32,64,291]{2,1,0:T(8,128)(2,1)}), bf16[32,64,291]{2,1,0:T(8,128)(2,1)S(1)}, u32[]{:S(2)}, u32[]{:S(2)}) %all-to-all-start) | async-done | bytes 1191968 | tf_op jit(solution)/shard_map/all_to_all | solution.py:74
  77.1 0.3 convert_reduce_fusion.1
  77.8 29.6 %all_gather.13 = f32[64,512]{0,1:T(8,128)S(1)} all-gather(f32[64,32]{0,1:T(8,128)S(1)} %slice.70), channel_id=1, replica_groups=mesh['row'=32,'col'=16] {'col'}, dimensions={1}, use_global_device_ids=true | all-gather | bytes 139264 | tf_op jit(solution)/shard_map/all_gather | solution.py:135
  107.4 0.3 fusion.6
  107.8 0.3 fusion.7
  108.1 0.3 divide_multiply_fusion
  108.4 0.2 fusion.26
  108.8 1.0 fusion.91
  109.8 0.4 convolution_bitcast_fusion.1
  110.1 1.2 multiply_reduce_fusion
  111.4 27.2 %psum.7 = f32[64]{0:T(128)S(1)} all-reduce(f32[64]{0:T(128)S(1)} %get-tuple-element.18), channel_id=1, replica_groups=mesh['row'=32,'col'=16] {'col'}, use_global_device_ids=true, to_apply=%region_4.5 | all-reduce | flops 64 | bytes 512 | tf_op jit(solution)/shard_map/psum | solution.py:168
  138.6 22.4 %all_gather.14 = bf16[32,64,128]{2,1,0:T(8,128)(2,1)S(1)} all-gather(bf16[1,64,128]{2,1,0:T(8,128)(2,1)S(1)} %multiply_convert_fusion), channel_id=1, replica_groups=mesh['row'=32,'col'=16] {'row'}, dimensions={0}, use_global_device_ids=true | all-gather | bytes 540672 | tf_op jit(solution)/shard_map/all_gather | solution.py:175
  161.1 0.3 fusion.1
  161.4 26.9 %all_to_all.25 = bf16[16,32,256]{2,1,0:T(8,128)(2,1)S(1)} all-to-all(bf16[16,32,256]{2,1,0:T(8,128)(2,1)S(1)} %fusion.1), channel_id=1, replica_groups=mesh['row'=32,'col'=16] {'col'}, dimensions={0} | all-to-all | bytes 524288 | tf_op jit(solution)/shard_map/all_to_all | solution.py:74
  188.4 28.7 %all_gather.15 = bf16[512,256]{1,0:T(8,128)(2,1)S(1)} all-gather(bf16[32,256]{1,0:T(8,128)(2,1)S(1)} %add_convert_fusion.1), channel_id=1, replica_groups=mesh['row'=32,'col'=16] {'col'}, dimensions={0}, use_global_device_ids=true | all-gather | bytes 278528 | tf_op jit(solution)/shard_map/all_gather | solution.py:184
  217.2 0.3 concatenate.29
  217.5 0.7 convolution_convert_fusion
  218.5 35.2 %all_to_all.26 = bf16[32,16,2049]{2,1,0:T(8,128)(2,1)S(1)} all-to-all(bf16[32,16,2049]{2,1,0:T(8,128)(2,1)S(1)} %pad_maximum_fusion), channel_id=1, replica_groups=mesh['row'=32,'col'=16] {'row'}, dimensions={0} | all-to-all | bytes 4196352 | tf_op jit(solution)/shard_map/all_to_all | solution.py:74
  253.7 0.4 convert_reduce_fusion
  254.3 0.2 broadcast_in_dim.29
  254.5 32.2 %all_to_all.27 = bf16[32,16,2048]{2,1,0:T(8,128)(2,1)S(1)} all-to-all(bf16[32,16,2048]{2,1,0:T(8,128)(2,1)S(1)} %broadcast_in_dim.29), channel_id=1, replica_groups=mesh['row'=32,'col'=16] {'row'}, dimensions={0} | all-to-all | bytes 4194304 | tf_op jit(solution)/shard_map/all_to_all | solution.py:195
  286.7 0.7 convolution_convert_fusion.2
  287.4 25.7 %all_to_all.28 = bf16[16,32,256]{2,1,0:T(8,128)(2,1)S(1)} all-to-all(bf16[16,32,256]{2,1,0:T(8,128)(2,1)S(1)} %bitcast.105), channel_id=1, replica_groups=mesh['row'=32,'col'=16] {'col'}, dimensions={0} | all-to-all | bytes 524288 | tf_op jit(solution)/shard_map/all_to_all | solution.py:74
  313.1 0.6 add_convert_fusion
  (65 shorter events, 1.8 us)
Async XLA Ops:
  0.0 217.5 %copy-start = (bf16[256,2048]{1,0:T(8,128)(2,1)S(1)}, bf16[256,2048]{1,0:T(8,128)(2,1)}, u32[]{:S(2)}) copy-start(bf16[256,2048]{1,0:T(8,128)(2,1)} %param.40) | copy-start | bytes 3145732
  0.0 40.0 %copy-start.1 = (bf16[256,4,2,128]{3,2,1,0:T(2,128)(2,1)S(1)}, bf16[256,4,2,128]{3,2,1,0:T(2,128)(2,1)}, u32[]{:S(2)}) copy-start(bf16[256,4,2,128]{3,2,1,0:T(2,128)(2,1)} %param.23) | copy-start | bytes 1572868
  45.6 7.6 %copy-start.13 = (s32[8]{0:T(128)S(1)}, s32[8]{0:T(128)}, u32[]{:S(2)}) copy-start(s32[8]{0:T(128)} %param.34) | copy-start | bytes 100
  45.6 11.8 %copy-start.5 = (bf16[1,4,3,512]{3,1,2,0:T(4,128)(2,1)S(1)}, bf16[1,4,3,512]{3,1,2,0:T(4,128)(2,1)}, u32[]{:S(2)}) copy-start(bf16[1,4,3,512]{3,1,2,0:T(4,128)(2,1)} %param.32) | copy-start | bytes 36868
  45.6 11.8 %copy-start.11 = (bf16[1,4,3,128]{3,1,2,0:T(4,128)(2,1)S(1)}, bf16[1,4,3,128]{3,1,2,0:T(4,128)(2,1)}, u32[]{:S(2)}) copy-start(bf16[1,4,3,128]{3,1,2,0:T(4,128)(2,1)} %param.31) | copy-start | bytes 9220
  45.6 11.9 %copy-start.4 = (bf16[4,4,512]{2,1,0:T(4,128)(2,1)S(1)}, bf16[4,4,512]{2,1,0:T(4,128)(2,1)}, u32[]{:S(2)}) copy-start(bf16[4,4,512]{2,1,0:T(4,128)(2,1)} %param.30) | copy-start | bytes 49156
  45.6 11.9 %copy-start.9 = (bf16[4,4,128]{2,1,0:T(4,128)(2,1)S(1)}, bf16[4,4,128]{2,1,0:T(4,128)(2,1)}, u32[]{:S(2)}) copy-start(bf16[4,4,128]{2,1,0:T(4,128)(2,1)} %param.29) | copy-start | bytes 12292
  45.6 13.4 %copy-start.10 = (f32[4,2]{0,1:T(2,128)S(1)}, f32[4,2]{0,1:T(2,128)}, u32[]{:S(2)}) copy-start(f32[4,2]{0,1:T(2,128)} %param.27) | copy-start | bytes 100
  45.6 13.6 %copy-start.7 = (f32[4,2]{0,1:T(2,128)S(1)}, f32[4,2]{0,1:T(2,128)}, u32[]{:S(2)}) copy-start(f32[4,2]{0,1:T(2,128)} %param.26) | copy-start | bytes 100
  45.7 13.6 %copy-start.8 = (f32[4,2]{0,1:T(2,128)S(1)}, f32[4,2]{0,1:T(2,128)}, u32[]{:S(2)}) copy-start(f32[4,2]{0,1:T(2,128)} %param.28) | copy-start | bytes 100
  45.7 31.4 %all-to-all-start = ((bf16[32,64,291]{2,1,0:T(8,128)(2,1)}), bf16[32,64,291]{2,1,0:T(8,128)(2,1)S(1)}, u32[]{:S(2)}, u32[]{:S(2)}) async-start(bf16[32,64,291]{2,1,0:T(8,128)(2,1)} %pad_maximum_fusion.1), calls=%async_computation | async-start | bytes 3145728 | tf_op jit(solution)/shard_map/all_to_all | solution.py:74
  107.7 53.3 %copy-start.2 = (bf16[4,128,256]{2,1,0:T(8,128)(2,1)S(1)}, bf16[4,128,256]{2,1,0:T(8,128)(2,1)}, u32[]{:S(2)}) copy-start(bf16[4,128,256]{2,1,0:T(8,128)(2,1)} %param.38) | copy-start | bytes 786436
  108.6 79.7 %copy-start.3 = (bf16[32,256]{1,0:T(8,128)(2,1)S(1)}, bf16[32,256]{1,0:T(8,128)(2,1)}, u32[]{:S(2)}) copy-start(bf16[32,256]{1,0:T(8,128)(2,1)} %param.21) | copy-start | bytes 49156
  111.3 106.2 %copy-start.6 = (f32[256]{0:T(256)S(1)}, f32[256]{0:T(256)}, u32[]{:S(2)}) copy-start(f32[256]{0:T(256)} %param.39) | copy-start | bytes 3076
  254.5 32.2 %copy-start.12 = (bf16[2048,256]{1,0:T(8,128)(2,1)S(1)}, bf16[2048,256]{1,0:T(8,128)(2,1)}, u32[]{:S(2)}) copy-start(bf16[2048,256]{1,0:T(8,128)(2,1)} %param.41) | copy-start | bytes 3145732

commit v2 on v1

v2 whole, which is shorter than its diff:
```python
import jax
import jax.numpy as jnp
from jax import lax
from jax.experimental import pallas as pl
from jax.experimental.pallas import tpu as pltpu
from jax.sharding import PartitionSpec as P

D = 8192
H = 128
P_SIZE = 64
N = 256
G = 4

EPSILON = 1e-05
F32 = jnp.float32
BF16 = jnp.bfloat16
NT = (((1,), (1,)), ((), ()))
VMEM_LIMIT = 48 * 1024 * 1024


def spread(block, axis):
    size = lax.axis_size(axis)
    return lax.all_to_all(
        jnp.broadcast_to(block[None], (size,) + block.shape), axis, 0, 0, tiled=True
    )


def sum_parts(parts, axis):
    received = lax.all_to_all(parts, axis, 0, 0, tiled=True)
    return jnp.sum(received.astype(F32), axis=0)


def call(kernel, out_shape, *operands):
    return pl.pallas_call(
        kernel,
        out_shape=out_shape,
        compiler_params=pltpu.CompilerParams(vmem_limit_bytes=VMEM_LIMIT),
    )(*operands)


def two_halves(values):
    high = lax.reduce_precision(values, 8, 7)
    return high.astype(BF16), (values - high).astype(BF16)


def project_kernel(hidden_ref, gain_ref, main_ref, side_ref, out_ref):
    hidden = hidden_ref[...].astype(F32)
    normed = (hidden * gain_ref[...]).astype(BF16)
    squares = (hidden * hidden).astype(BF16)
    ones = jnp.ones((16, hidden.shape[1]), BF16)
    stat = lax.dot_general(ones, squares, NT, preferred_element_type=F32)
    for group in range(G):
        main = jnp.dot(
            normed, main_ref[:, group * 256 : (group + 1) * 256], preferred_element_type=F32
        ).astype(BF16)
        side = lax.dot_general(
            side_ref[group * 64 : (group + 1) * 64, :], normed, NT, preferred_element_type=F32
        )
        for request in range(8):
            nodes = slice(request * 64, (request + 1) * 64)
            out_ref[request, group, 0:64, :] = main[nodes, :]
            pieces = [side[0:16, nodes], side[16:32, nodes], side[32:48, nodes], stat[:, nodes]]
            out_ref[request, group, 64:80, :] = jnp.concatenate(pieces, axis=1).astype(BF16)


def combine_kernel(parts_ref, out_ref):
    total = parts_ref[0].astype(F32)
    for part in range(1, parts_ref.shape[0]):
        total = total + parts_ref[part].astype(F32)
    scale_row = lax.rsqrt(total[64:65, 192:256] / D + EPSILON)
    eye = lax.broadcasted_iota(jnp.int32, (64, 64), 0) == lax.broadcasted_iota(
        jnp.int32, (64, 64), 1
    )
    scale_col = jnp.sum(
        jnp.where(eye, jnp.broadcast_to(scale_row, (64, 64)), 0.0), axis=1, keepdims=True
    )
    main = total[0:64, :]
    main = jnp.concatenate(
        [main[:, 0:64], main[:, 128:192], main[:, 64:128], main[:, 192:256]], axis=1
    )
    out_ref[0:64, :] = (main * scale_col).astype(BF16)
    scale_all = jnp.concatenate([scale_row] * 4, axis=1)
    out_ref[64:80, :] = (total[64:80, :] * scale_all).astype(BF16)


def mixer_kernel(
    place_ref,
    new_ref,
    x_hist_ref,
    x_taps_ref,
    bc_hist_ref,
    bc_taps_ref,
    head_ref,
    gain_ref,
    state_ref,
    parents_ref,
    anc_ref,
    out_ref,
    x_ref,
    gate_ref,
    bc_ref,
    step_ref,
):
    cols = new_ref.shape[0]
    first = place_ref[0] * 4
    for col in range(cols):
        lanes = slice(col * 128, (col + 1) * 128)
        x_ref[0:64, lanes] = new_ref[col, 0:64, 0:128]
        gate_ref[:, lanes] = new_ref[col, 0:64, 128:256]
        tail = new_ref[col, 64:80, :].astype(F32)
        bc_ref[col * 32 : col * 32 + 16, 0:64] = tail[:, 0:64].astype(BF16)
        bc_ref[col * 32 + 16 : col * 32 + 32, 0:64] = tail[:, 64:128].astype(BF16)
        step_ref[col * 2 : col * 2 + 2, :] = tail[0:2, 128:192]
    x_ref[64:80, :] = x_hist_ref[...]
    bc_ref[:, 64:128] = bc_hist_ref[...]

    node_row = lax.broadcasted_iota(jnp.int32, (64, 64), 1)
    node_col = lax.broadcasted_iota(jnp.int32, (64, 64), 0)
    anc = anc_ref[...]
    anc_float = anc.astype(F32)
    depth = jnp.sum(anc, axis=1, keepdims=True) - 1
    hop = (parents_ref[...] == node_row).astype(BF16)
    hops = [None, hop]
    for _ in range(2):
        hops.append(jnp.dot(hops[-1], hop, preferred_element_type=F32).astype(BF16))

    def picks(distance, width):
        lane = lax.broadcasted_iota(jnp.int32, (64, width), 1)
        return ((distance > depth) & (lane == 3 - distance + depth)).astype(BF16)

    x_run = x_ref[0:64, :].astype(F32) * x_taps_ref[3:4, :]
    for distance in range(1, 4):
        mover = jnp.concatenate([hops[distance], picks(distance, 16)], axis=1)
        moved = jnp.dot(mover, x_ref[...], preferred_element_type=F32)
        x_run = x_run + moved * x_taps_ref[3 - distance : 4 - distance, :]
    x_conv = (x_run * jax.nn.sigmoid(x_run)).astype(BF16)
    bc_run = bc_ref[:, 0:64].astype(F32) * bc_taps_ref[:, 3:4]
    for distance in range(1, 4):
        mover = jnp.concatenate([hops[distance], picks(distance, 64)], axis=1)
        moved = lax.dot_general(bc_ref[...], mover, NT, preferred_element_type=F32)
        bc_run = bc_run + moved * bc_taps_ref[:, 3 - distance : 4 - distance]
    bc_conv = (bc_run * jax.nn.sigmoid(bc_run)).astype(BF16)

    raw = step_ref[...] + head_ref[:, 0:1]
    step = jnp.maximum(raw, 0.0) + jnp.log1p(jnp.exp(-jnp.abs(raw)))
    log_decay = -jnp.exp(head_ref[:, 1:2]) * step
    cum = lax.dot_general(
        log_decay,
        anc_float,
        NT,
        precision=lax.Precision.HIGHEST,
        preferred_element_type=F32,
    )

    own = (
        lax.broadcasted_iota(jnp.int32, (16, 64), 0) + first
        == lax.broadcasted_iota(jnp.int32, (16, 64), 1)
    ).astype(BF16)
    c_own = lax.dot_general(own, bc_conv[256:512, :], NT, preferred_element_type=F32).astype(BF16)
    scores = jnp.dot(c_own, bc_conv[0:256, :], preferred_element_type=F32)
    state = state_ref[...].reshape(-1, N)
    carried = lax.dot_general(c_own, state, NT, preferred_element_type=F32)
    x_own = jnp.dot(own, x_conv, preferred_element_type=F32)
    gate_own = jnp.dot(own, gate_ref[...], preferred_element_type=F32)

    weights = []
    starts = []
    for node in range(4):
        here = first + node
        mask = jnp.sum(jnp.where(node_col == here, anc, 0), axis=0, keepdims=True) > 0
        lane = lax.broadcasted_iota(jnp.int32, cum.shape, 1)
        cum_here = jnp.sum(jnp.where(lane == here, cum, 0.0), axis=1, keepdims=True)
        gap = jnp.where(mask, cum_here - cum, 0.0)
        weight = jnp.where(mask, jnp.exp(gap), 0.0) * scores[node : node + 1, :] * step
        weights.append(weight.astype(BF16))
        starts.append(jnp.exp(cum_here))
    mixed = jnp.dot(jnp.concatenate(weights, axis=0), x_conv, preferred_element_type=F32)
    heads = 2 * cols
    wide = (heads, heads * P_SIZE)
    own_head = (
        lax.broadcasted_iota(jnp.int32, wide, 1) // P_SIZE
        == lax.broadcasted_iota(jnp.int32, wide, 0)
    )
    skip = head_ref[:, 2:3]
    rows = []
    for node in range(4):
        term = (
            mixed[node * heads : (node + 1) * heads, :]
            + starts[node] * carried[node : node + 1, :]
            + skip * x_own[node : node + 1, :]
        )
        rows.append(jnp.sum(jnp.where(own_head, term, 0.0), axis=0, keepdims=True))
    mixed_own = jnp.concatenate(rows, axis=0)
    gate = gate_own[0:4, :]
    gated = mixed_own * (gate * jax.nn.sigmoid(gate))
    group_sq = jnp.sum(gated * gated, axis=1, keepdims=True)
    out = gated * lax.rsqrt(group_sq / (H // G * P_SIZE) + EPSILON) * gain_ref[...]
    out_ref[...] = out.astype(BF16)


def local(
    hidden_in,
    norm_mixer,
    mixer_in,
    bc_proj,
    dt_proj,
    dt_bias,
    a_log,
    skip_d,
    conv_x,
    conv_bc,
    x_cache,
    bc_cache,
    ssm_cache,
    slot_ids,
    parents,
    ancestors,
    norm_gated,
    out_proj,
    norm_ffn,
    ffn_up,
    ffn_down,
):
    rows = lax.axis_size("row")
    cols = lax.axis_size("col")
    row_index = lax.axis_index("row")
    col_index = lax.axis_index("col")
    request = row_index // G
    group_index = row_index % G

    def pick(table, index, axis=0):
        return lax.dynamic_index_in_dim(table, index, axis, keepdims=False)

    slot_index = pick(slot_ids, request)
    start_state = pick(ssm_cache[0], slot_index).astype(BF16).reshape(-1, N)
    early = jnp.concatenate([out_proj.reshape(-1, N), start_state], axis=0)
    early = lax.all_gather(early, "col", axis=0, tiled=False)
    out_weights = early[:, :512].reshape(cols, G, 128, 256)

    small = jnp.concatenate(
        [pick(dt_bias, group_index), pick(a_log, group_index), pick(skip_d, group_index)]
    )
    table = jnp.concatenate(
        [
            pick(conv_x, group_index, 1).astype(F32),
            pick(x_cache[0], slot_index).astype(F32),
            pick(norm_gated, group_index)[None],
            jnp.pad(small, (0, 128 - small.shape[0]))[None],
        ],
        axis=0,
    )
    high, low = two_halves(table)
    packed = jnp.concatenate([high, low[7:9], jnp.zeros((5, 128), BF16)], axis=0)
    sent = jnp.concatenate([hidden_in, packed.reshape(8, 256)], axis=0)
    spread_in = spread(sent, "col")
    hidden = spread_in[:, :32].reshape(512, 256)
    param = spread_in[:, 32:].reshape(cols, 16, 128).astype(F32)
    x_taps = param[:, 0:4].transpose(1, 0, 2).reshape(4, -1)
    x_hist = param[:, 4:7].astype(BF16).transpose(1, 0, 2).reshape(3, -1)
    x_hist = jnp.pad(x_hist, ((0, 13), (0, 0)))
    gain = (param[:, 7] + param[:, 9]).reshape(1, -1)
    head = (param[:, 8] + param[:, 10])[:, 0:6].reshape(cols, 3, 2).transpose(0, 2, 1)
    head = jnp.pad(head.reshape(2 * cols, 3), ((0, 0), (0, 125)))
    bc_hist = jnp.pad(pick(bc_cache[0], slot_index).T, ((0, 0), (0, 61)))
    bc_taps = jnp.pad(pick(conv_bc, group_index, 1).T.astype(F32), ((0, 0), (0, 124)))

    side = jnp.concatenate([bc_proj, dt_proj, jnp.zeros((256, G, 30), BF16)], axis=2)
    side = side.reshape(256, 256).T
    parts = call(
        project_kernel,
        jax.ShapeDtypeStruct((rows // G, G, 80, 256), BF16),
        hidden,
        norm_mixer[None, :],
        mixer_in.reshape(256, -1),
        side,
    )
    parts = lax.all_to_all(parts.reshape(rows, 80, 256), "row", 0, 0, tiled=True)
    combined = call(combine_kernel, jax.ShapeDtypeStruct((80, 256), BF16), parts)
    new = spread(combined, "col")
    operands = [
        x_hist,
        x_taps,
        bc_hist,
        bc_taps,
        head,
        gain,
        early,
        pick(parents, request)[:, None],
        pick(ancestors, request),
    ]

    def whole(shape):
        return pl.BlockSpec(shape, lambda step: (0,) * len(shape))

    specs = [whole(operand.shape) for operand in operands]
    specs[6] = pl.BlockSpec((cols, 128, N), lambda step: (0, 4, 0))
    mixed = pl.pallas_call(
        mixer_kernel,
        grid=(1,),
        out_shape=jax.ShapeDtypeStruct((4, 2048), BF16),
        in_specs=[pl.BlockSpec(memory_space=pltpu.SMEM), whole(new.shape)] + specs,
        out_specs=whole((4, 2048)),
        scratch_shapes=[
            pltpu.VMEM((80, 2048), BF16),
            pltpu.VMEM((64, 2048), BF16),
            pltpu.VMEM((512, 128), BF16),
            pltpu.VMEM((32, 64), F32),
        ],
        compiler_params=pltpu.CompilerParams(vmem_limit_bytes=VMEM_LIMIT),
    )(col_index.astype(jnp.int32)[None], new, *operands)

    heads = lax.all_gather(mixed, "row", axis=0, tiled=False)
    heads = heads.reshape(rows // G, G, 4, cols, 128)
    mixer_out = jnp.einsum("qgtck,cgkd->qtd", heads, out_weights, preferred_element_type=F32)
    residual = lax.dynamic_slice(
        hidden.reshape(8, 64, 256), (0, 4 * col_index, 0), (8, 4, 256)
    ).astype(F32)
    after = (residual + mixer_out).astype(BF16).reshape(32, 256)
    all_after = lax.all_gather(after, "col", axis=0, tiled=False)
    all_after = all_after.reshape(cols, 8, 4, 256).transpose(1, 0, 2, 3).reshape(512, 256)
    after_wide = all_after.astype(F32)
    ffn_part = jnp.sum(after_wide * after_wide, axis=1)
    up_term = jnp.dot(
        (after_wide * norm_ffn[None, :]).astype(BF16), ffn_up, preferred_element_type=F32
    )
    up_term = jnp.concatenate([up_term, ffn_part[:, None]], axis=1).astype(BF16)
    up_sum = sum_parts(up_term.reshape(rows, -1, up_term.shape[1]), "row")
    up_share = up_sum[:, :-1] * lax.rsqrt(up_sum[:, -1:] / D + EPSILON)
    act_share = jnp.square(jax.nn.relu(up_share)).astype(BF16)
    act_all = spread(act_share, "row").reshape(512, -1)
    ffn_term = jnp.dot(act_all, ffn_down, preferred_element_type=F32).astype(BF16)
    ffn_out = sum_parts(ffn_term.reshape(cols, -1, ffn_term.shape[1]), "col")
    own_after = lax.dynamic_slice(all_after, (32 * col_index, 0), (32, 256))
    return (own_after.astype(F32) + ffn_out).astype(BF16)


def solution(mesh):
    return jax.shard_map(
        local,
        mesh=mesh,
        in_specs=(
            P("col", "row"),
            P("row"),
            P("row", None, "col", None),
            P("row", None, "col"),
            P("row", None, "col"),
            P(None, "col"),
            P(None, "col"),
            P(None, "col"),
            P(None, None, "col"),
            P(),
            P("row", None, None, "col"),
            P("row", None, None, None),
            P("row", None, "col", None, None),
            P(),
            P(),
            P(),
            P(None, "col"),
            P(None, "col", "row"),
            P("row"),
            P("row", "col"),
            P("col", "row"),
        ),
        out_specs=P("col", "row"),
        check_vma=False,
    )
```

time: 315 us -> 310 us (0.984)
  blocking collectives: 263 us -> 148 us
  waiting for transfers between devices: 16.6 us -> 81 us
  starting transfers between devices: 7.47 us -> 31.3 us
  between operations: 2.48 us -> 15.7 us
  local copies, waits for them, and re-layouts: 7.73 us -> 16.8 us
  Pallas kernels: 0 us -> 3.92 us
  matrix products: 8.85 us -> 5.2 us
    all_gather x4 -> x2, blocking collectives: 116 us -> 53.5 us  [the longest x1 28.3 us: local(): all_after = lax.all_gather(after, 'col', axis=0, tiled=False)]
    all_to_all x3 -> x1, blocking collectives: 87.8 us -> 35.3 us  [sum_parts(): received = lax.all_to_all(parts, axis, 0, 0, tiled=True)]
    all_gather x0 -> x1, waiting for transfers between devices: none -> 39.6 us  [local(): early = lax.all_gather(early, 'col', axis=0, tiled=False)]
    all_to_all x1 -> x2, blocking collectives: 32.2 us -> 59.4 us  [the longest x1 32.2 us: spread(): lax.all_to_all(jnp.broadcast_to(block[None], (size,) + block.shape), axis...]
    psum x1 -> x0, blocking collectives: 27.2 us -> none  [local(): group_sq = lax.psum(jnp.sum(gated * gated, axis=(1, 2)), 'col')]
    all_to_all x0 -> x2, waiting for transfers between devices: none -> 23.2 us  [spread(): lax.all_to_all(jnp.broadcast_to(block[None], (size,) + block.shape), axis...]
    all_to_all x0 -> x2, starting transfers between devices: none -> 22.2 us  [spread(): lax.all_to_all(jnp.broadcast_to(block[None], (size,) + block.shape), axis...]
    slice x5, local copies, waits for them, and re-layouts: 0.06 us -> 4.61 us  [the longest x1 4.57 us: local(): out_weights = early[:, :512].reshape(cols, G, 128, 256)]
  transfers between devices with their start and end apart: 1 -> 4, of which waited for: 1 -> 3; matrix products, arithmetic and copies ran while one was open for 2% -> 5% of each run, Pallas kernels for 0% -> 0%
where the time goes in v2:
time: 310 us; the launch traced here: 309 us
  blocking collectives  148 us (48%)
  waiting for transfers between devices  81 us (26%)
  starting transfers between devices  31.3 us (10%)
  local copies, waits for them, and re-layouts  16.8 us (5%)
  between operations  15.7 us (5%)
  other arithmetic  6.9 us (2%)
  matrix products  5.2 us (2%)
  Pallas kernels  3.92 us (1%)
    all_gather x1, waiting for transfers between devices, local(): early = lax.all_gather(early, 'col', axis=0, tiled=False)  39.6 us
    all_to_all x1, blocking collectives, sum_parts(): received = lax.all_to_all(parts, axis, 0, 0, tiled=True)  35.3 us
    all_to_all x1, blocking collectives, spread(): lax.all_to_all(jnp.broadcast_to(block[None], (size,) + block.shape), axis...  32.2 us
    all_gather x1, blocking collectives, local(): all_after = lax.all_gather(after, 'col', axis=0, tiled=False)  28.3 us
    all_to_all x1, blocking collectives, local(): lax.all_to_all(parts.reshape(rows, 80, 256), 'row', 0, 0, tiled=True)  27.2 us
    all_gather x1, blocking collectives, local(): heads = lax.all_gather(mixed, 'row', axis=0, tiled=False)  25.2 us
    all_to_all x2, waiting for transfers between devices, spread(): lax.all_to_all(jnp.broadcast_to(block[None], (size,) + block.shape), axis...  23.2 us
    all_to_all x2, starting transfers between devices, spread(): lax.all_to_all(jnp.broadcast_to(block[None], (size,) + block.shape), axis...  22.2 us
  transfers between devices with their start and end apart: 4, of which 3 were waited for; matrix products, arithmetic and copies ran while one was open for 5% of the time, Pallas kernels for 0%

profile of v2, /device:TPU:32, one launch (start us, length us, event | category | flops | bytes accessed | tf_op | source)
XLA Modules:
  0.0 309.0 jit_solution(107678071926800726)
XLA Ops:
  6.6 1.3 dynamic_slice.53
  9.9 0.9 dynamic-slice_convert_fusion
  10.8 1.7 pad_maximum_fusion.1
  12.6 0.7 fusion.13
  13.3 0.9 fusion.16
  14.2 0.9 fusion.14
  15.1 0.7 constant_dynamic-slice_fusion.7
  15.9 0.7 fusion.12
  16.7 0.7 pad_maximum_fusion.2
  17.4 0.8 broadcast_in_dim.20
  18.2 15.2 %all-to-all-start = ((bf16[16,40,256]{2,1,0:T(8,128)(2,1)}), bf16[16,40,256]{2,1,0:T(8,128)(2,1)S(1)}, u32[]{:S(2)}, u32[]{:S(2)}) async-start(bf16[16,40,256]{2,1,0:T(8,128)(2,1)} %broadcast_in_dim.20), calls=%async_computation | async-start | bytes 655360 | tf_op jit(solution)/shard_map/all_to_all | solution.py:23
  33.5 0.4 reshape.108.main_ref
  33.9 23.2 %all-to-all-done = bf16[16,40,256]{2,1,0:T(8,128)(2,1)S(1)} async-done(((bf16[16,40,256]{2,1,0:T(8,128)(2,1)}), bf16[16,40,256]{2,1,0:T(8,128)(2,1)S(1)}, u32[]{:S(2)}, u32[]{:S(2)}) %all-to-all-start) | async-done | bytes 327712 | tf_op jit(solution)/shard_map/all_to_all | solution.py:23
  57.2 0.8 shard_map.199
  58.1 27.2 %all_to_all.30.parts_ref = bf16[32,80,256]{2,1,0:T(8,128)(2,1)S(1)} all-to-all(bf16[32,80,256]{2,1,0:T(8,128)(2,1)S(1)} %bitcast.72), channel_id=1, replica_groups=mesh['row'=32,'col'=16] {'row'}, dimensions={0} | all-to-all | bytes 2621440 | tf_op jit(solution)/shard_map/all_to_all | solution.py:277
  85.3 0.3 shard_map.200
  85.5 0.9 broadcast_in_dim.45
  86.4 7.0 %all-to-all-start.2 = ((bf16[16,80,256]{2,1,0:T(8,128)(2,1)}), bf16[16,80,256]{2,1,0:T(8,128)(2,1)S(1)}, u32[]{:S(2)}, u32[]{:S(2)}) async-start(bf16[16,80,256]{2,1,0:T(8,128)(2,1)} %broadcast_in_dim.45), calls=%async_computation.2 | async-start | bytes 1310720 | tf_op jit(solution)/shard_map/all_to_all | solution.py:23
  93.4 0.7 fusion.18
  94.2 0.2 copy.86
  94.5 0.2 copy.85
  94.7 0.8 dynamic-slice_bitcast_fusion.anc_ref
  95.5 0.3 copy.83
  96.0 1.0 copy-done.2
  97.2 1.0 slice_add_fusion
  98.3 39.6 %all-gather.5.cloned.1.call-done = bf16[10240,256]{1,0:T(8,128)(2,1)} async-done(((bf16[640,256]{1,0:T(8,128)(2,1)}), bf16[10240,256]{1,0:T(8,128)(2,1)}) %all-gather.5.cloned.1.call-update) | async-done | bytes 5242896 | tf_op jit(solution)/shard_map/all_gather | solution.py:237
  137.9 4.6 %slice.64 = bf16[16,512,256]{2,1,0:T(8,128)(2,1)} slice(bf16[16,640,256]{2,1,0:T(8,128)(2,1)} %bitcast.81), slice={[0:16], [0:512], [0:256]} | slice | bytes 8388608 | tf_op jit(solution)/shard_map/slice | solution.py:238
  142.5 2.8 shard_map.201
  145.3 25.2 %all-gather.2 = bf16[32,4,2048]{2,1,0:T(4,128)(2,1)S(1)} all-gather(bf16[1,4,2048]{2,1,0:T(4,128)(2,1)S(1)} %bitcast.77), channel_id=3, replica_groups=mesh['row'=32,'col'=16] {'row'}, dimensions={0}, use_global_device_ids=true | all-gather | bytes 540672 | tf_op jit(solution)/shard_map/all_gather | solution.py:312
  170.5 0.3 reshape.134
  170.8 3.1 fusion.1
  174.0 28.3 %all_gather.19 = bf16[16,32,256]{2,1,0:T(8,128)(2,1)S(1)} all-gather(bf16[1,32,256]{2,1,0:T(8,128)(2,1)S(1)} %all_gather_reshape.3), channel_id=1, replica_groups=mesh['row'=32,'col'=16] {'col'}, dimensions={0}, use_global_device_ids=true | all-gather | bytes 278528 | tf_op jit(solution)/shard_map/all_gather | solution.py:319
  202.2 0.2 bitcast_convert_fusion
  202.4 0.3 copy.96
  202.8 0.2 reshape.124
  203.0 0.2 multiply_reduce_fusion
  203.1 0.1 copy.97
  203.4 0.7 convolution_convert_fusion
  204.1 0.2 pad_maximum_fusion
  204.3 35.3 %all_to_all.31 = bf16[32,16,2049]{2,1,0:T(8,128)(2,1)S(1)} all-to-all(bf16[32,16,2049]{2,1,0:T(8,128)(2,1)S(1)} %pad_maximum_fusion), channel_id=1, replica_groups=mesh['row'=32,'col'=16] {'row'}, dimensions={0} | all-to-all | bytes 4196352 | tf_op jit(solution)/shard_map/all_to_all | solution.py:29
  239.7 0.4 convert_reduce_fusion
  240.2 0.2 broadcast_in_dim.47
  240.5 32.2 %all_to_all.32 = bf16[32,16,2048]{2,1,0:T(8,128)(2,1)S(1)} all-to-all(bf16[32,16,2048]{2,1,0:T(8,128)(2,1)S(1)} %broadcast_in_dim.47), channel_id=1, replica_groups=mesh['row'=32,'col'=16] {'row'}, dimensions={0} | all-to-all | bytes 4194304 | tf_op jit(solution)/shard_map/all_to_all | solution.py:23
  272.7 1.4 convolution_convert_fusion.1
  274.1 9.1 %all-to-all-start.5 = ((bf16[16,32,256]{2,1,0:T(8,128)(2,1)}), bf16[16,32,256]{2,1,0:T(8,128)(2,1)S(1)}, u32[]{:S(2)}, u32[]{:S(2)}) async-start(bf16[16,32,256]{2,1,0:T(8,128)(2,1)} %bitcast.35), calls=%async_computation.5 | async-start | bytes 524288 | tf_op jit(solution)/shard_map/all_to_all | solution.py:29
  283.2 0.1 copy.95
  283.4 18.1 %all-to-all-done.5 = bf16[16,32,256]{2,1,0:T(8,128)(2,1)S(1)} async-done(((bf16[16,32,256]{2,1,0:T(8,128)(2,1)}), bf16[16,32,256]{2,1,0:T(8,128)(2,1)S(1)}, u32[]{:S(2)}, u32[]{:S(2)}) %all-to-all-start.5) | async-done | bytes 262176 | tf_op jit(solution)/shard_map/all_to_all | solution.py:29
  301.6 0.6 add_convert_fusion
  (62 shorter events, 1.7 us)
Async XLA Ops:
  6.5 196.9 %copy-start = (bf16[256,2048]{1,0:T(8,128)(2,1)S(1)}, bf16[256,2048]{1,0:T(8,128)(2,1)}, u32[]{:S(2)}) copy-start(bf16[256,2048]{1,0:T(8,128)(2,1)} %param.40) | copy-start | bytes 3145732
  6.5 26.9 %copy-start.3 = (bf16[256,4,2,128]{3,2,1,0:T(2,128)(2,1)S(1)}, bf16[256,4,2,128]{3,2,1,0:T(2,128)(2,1)}, u32[]{:S(2)}) copy-start(bf16[256,4,2,128]{3,2,1,0:T(2,128)(2,1)} %param.23) | copy-start | bytes 1572868
  6.5 27.3 %copy-start.5 = (bf16[256,4,2]{0,2,1:T(2,128)(2,1)S(1)}, bf16[256,4,2]{0,2,1:T(2,128)(2,1)}, u32[]{:S(2)}) copy-start(bf16[256,4,2]{0,2,1:T(2,128)(2,1)} %param.25) | copy-start | bytes 12292
  6.5 27.3 %copy-start.4 = (bf16[256,4,32]{0,2,1:T(8,128)(2,1)S(1)}, bf16[256,4,32]{0,2,1:T(8,128)(2,1)}, u32[]{:S(2)}) copy-start(bf16[256,4,32]{0,2,1:T(8,128)(2,1)} %param.24) | copy-start | bytes 196612
  6.5 50.7 %copy-start.1 = (f32[256]{0:T(256)S(1)}, f32[256]{0:T(256)}, u32[]{:S(2)}) copy-start(f32[256]{0:T(256)} %param.22) | copy-start | bytes 3076
  6.5 131.4 %all-gather.5.cloned.1.call-start = ((), (), s32[]{:S(2)}) async-start(), calls=%async_computation.6 | async-start | bytes 5570560 | tf_op jit(solution)/shard_map/all_gather | solution.py:237
  18.2 39.0 %all-to-all-start = ((bf16[16,40,256]{2,1,0:T(8,128)(2,1)}), bf16[16,40,256]{2,1,0:T(8,128)(2,1)S(1)}, u32[]{:S(2)}, u32[]{:S(2)}) async-start(bf16[16,40,256]{2,1,0:T(8,128)(2,1)} %broadcast_in_dim.20), calls=%async_computation | async-start | bytes 655360 | tf_op jit(solution)/shard_map/all_to_all | solution.py:23
  85.3 8.9 %copy-start.6 = (bf16[4,4,512]{2,1,0:T(4,128)(2,1)S(1)}, bf16[4,4,512]{2,1,0:T(4,128)(2,1)}, u32[]{:S(2)}) copy-start(bf16[4,4,512]{2,1,0:T(4,128)(2,1)} %param.30) | copy-start | bytes 49156
  85.3 9.2 %copy-start.7 = (bf16[1,4,3,512]{3,1,2,0:T(4,128)(2,1)S(1)}, bf16[1,4,3,512]{3,1,2,0:T(4,128)(2,1)}, u32[]{:S(2)}) copy-start(bf16[1,4,3,512]{3,1,2,0:T(4,128)(2,1)} %param.32) | copy-start | bytes 36868
  86.4 56.1 %all-to-all-start.2 = ((bf16[16,80,256]{2,1,0:T(8,128)(2,1)}), bf16[16,80,256]{2,1,0:T(8,128)(2,1)S(1)}, u32[]{:S(2)}, u32[]{:S(2)}) async-start(bf16[16,80,256]{2,1,0:T(8,128)(2,1)} %broadcast_in_dim.45), calls=%async_computation.2 | async-start | bytes 1310720 | tf_op jit(solution)/shard_map/all_to_all | solution.py:23
  96.0 1.0 copy-start.2
  173.9 29.5 %copy-start.8 = (f32[256]{0:T(256)S(1)}, f32[256]{0:T(256)}, u32[]{:S(2)}) copy-start(f32[256]{0:T(256)} %param.39) | copy-start | bytes 3076
  240.5 32.2 %copy-start.9 = (bf16[2048,256]{1,0:T(8,128)(2,1)S(1)}, bf16[2048,256]{1,0:T(8,128)(2,1)}, u32[]{:S(2)}) copy-start(bf16[2048,256]{1,0:T(8,128)(2,1)} %param.41) | copy-start | bytes 3145732
  274.1 27.5 %all-to-all-start.5 = ((bf16[16,32,256]{2,1,0:T(8,128)(2,1)}), bf16[16,32,256]{2,1,0:T(8,128)(2,1)S(1)}, u32[]{:S(2)}, u32[]{:S(2)}) async-start(bf16[16,32,256]{2,1,0:T(8,128)(2,1)} %bitcast.35), calls=%async_computation.5 | async-start | bytes 524288 | tf_op jit(solution)/shard_map/all_to_all | solution.py:29
Sparse Core Ops, SparseCore 0:
  12.7 125.1 all-gather.4

commit v3 on v2

v3 whole, which is shorter than its diff:
```python
import jax
import jax.numpy as jnp
from jax import lax
from jax.experimental import pallas as pl
from jax.experimental.pallas import tpu as pltpu
from jax.sharding import PartitionSpec as P

D = 8192
H = 128
P_SIZE = 64
N = 256
G = 4

EPSILON = 1e-05
F32 = jnp.float32
BF16 = jnp.bfloat16
NT = (((1,), (1,)), ((), ()))
VMEM_LIMIT = 48 * 1024 * 1024


def spread(block, axis):
    size = lax.axis_size(axis)
    return lax.all_to_all(
        jnp.broadcast_to(block[None], (size,) + block.shape), axis, 0, 0, tiled=True
    )


def sum_parts(parts, axis):
    received = lax.all_to_all(parts, axis, 0, 0, tiled=True)
    return jnp.sum(received.astype(F32), axis=0)


def call(kernel, out_shape, *operands):
    return pl.pallas_call(
        kernel,
        out_shape=out_shape,
        compiler_params=pltpu.CompilerParams(vmem_limit_bytes=VMEM_LIMIT),
    )(*operands)


def project_side_kernel(hidden_ref, gain_ref, side_ref, out_ref):
    hidden = hidden_ref[...].astype(F32)
    normed = (hidden * gain_ref[...]).astype(BF16)
    squares = (hidden * hidden).astype(BF16)
    ones = jnp.ones((16, hidden.shape[1]), BF16)
    stat = lax.dot_general(ones, squares, NT, preferred_element_type=F32)
    for group in range(G):
        side = lax.dot_general(
            side_ref[group * 64 : (group + 1) * 64, :], normed, NT, preferred_element_type=F32
        )
        for request in range(8):
            nodes = slice(request * 64, (request + 1) * 64)
            pieces = [side[0:16, nodes], side[16:32, nodes], side[32:48, nodes], stat[:, nodes]]
            out_ref[request, group, :, :] = jnp.concatenate(pieces, axis=1).astype(BF16)


def project_main_kernel(hidden_ref, gain_ref, main_ref, out_ref):
    normed = (hidden_ref[...].astype(F32) * gain_ref[...]).astype(BF16)
    for group in range(G):
        main = jnp.dot(
            normed, main_ref[:, group * 256 : (group + 1) * 256], preferred_element_type=F32
        ).astype(BF16)
        for request in range(8):
            out_ref[request, group, :, :] = main[request * 64 : (request + 1) * 64, :]


def combine_side_kernel(parts_ref, bc_ref, local_ref):
    total = parts_ref[0].astype(F32)
    for part in range(1, parts_ref.shape[0]):
        total = total + parts_ref[part].astype(F32)
    scale = lax.rsqrt(total[0:1, 192:256] / D + EPSILON)
    bc_ref[...] = (total[:, 0:128] * jnp.concatenate([scale, scale], axis=1)).astype(BF16)
    local_ref[0:2, :] = total[0:2, 128:192] * scale
    local_ref[2:3, :] = scale
    local_ref[3:8, :] = jnp.zeros((5, 64), F32)


def column_of(row, size):
    eye = lax.broadcasted_iota(jnp.int32, (size, size), 0) == lax.broadcasted_iota(
        jnp.int32, (size, size), 1
    )
    wide = jnp.broadcast_to(row, (size, size))
    return jnp.sum(jnp.where(eye, wide, jnp.zeros_like(wide)), axis=1, keepdims=True)


def mixer_kernel(
    place_ref,
    slot_ref,
    parts_ref,
    bc_new_ref,
    local_ref,
    x_hist_ref,
    bc_hist_ref,
    state_ref,
    x_taps_ref,
    bc_taps_ref,
    head_ref,
    gain_ref,
    parents_ref,
    anc_ref,
    out_ref,
    bc_ref,
):
    request = place_ref[0]
    group = place_ref[1]
    total = parts_ref[0].astype(F32)
    for part in range(1, parts_ref.shape[0]):
        total = total + parts_ref[part].astype(F32)
    total = total * column_of(local_ref[2:3, :], 64)
    x_new = jnp.concatenate([total[:, 0:64], total[:, 128:192]], axis=1)
    gate = jnp.concatenate([total[:, 64:128], total[:, 192:256]], axis=1)

    for col in range(bc_new_ref.shape[0]):
        piece = bc_new_ref[col].astype(F32)
        bc_ref[col * 32 : col * 32 + 16, 0:64] = piece[:, 0:64].astype(BF16)
        bc_ref[col * 32 + 16 : col * 32 + 32, 0:64] = piece[:, 64:128].astype(BF16)
    bc_ref[:, 64:128] = bc_hist_ref[...]

    x_taps = jnp.zeros((4, 128), F32)
    gain = jnp.zeros((1, 128), F32)
    for index in range(G):
        x_taps = jnp.where(group == index, x_taps_ref[:, index, :].astype(F32), x_taps)
        gain = jnp.where(group == index, gain_ref[index : index + 1, :], gain)

    lane = lax.broadcasted_iota(jnp.int32, (64, 64), 1)
    row = lax.broadcasted_iota(jnp.int32, (64, 64), 0)
    anc = anc_ref[0]
    depth = jnp.sum(anc, axis=1, keepdims=True) - 1
    all_parents = parents_ref[...]
    this = lax.broadcasted_iota(jnp.int32, all_parents.shape, 0) == request
    parent_row = jnp.sum(jnp.where(this, all_parents, 0), axis=0, keepdims=True)
    hop = (column_of(parent_row, 64) == lane).astype(BF16)
    hops = [None, hop]
    for _ in range(2):
        hops.append(jnp.dot(hops[-1], hop, preferred_element_type=F32).astype(BF16))

    x_high = x_new.astype(BF16)
    x_low = (x_new - x_high.astype(F32)).astype(BF16)
    x_both = jnp.concatenate([x_high, x_low], axis=1)
    x_hist = x_hist_ref[0, 0].astype(F32)
    x_run = x_new * x_taps[3:4, :]
    for distance in range(1, 4):
        moved = jnp.dot(hops[distance], x_both, preferred_element_type=F32)
        moved = moved[:, 0:128] + moved[:, 128:256]
        for entry in range(3):
            use = (distance > depth) & (entry == 3 - distance + depth)
            moved = moved + jnp.where(use, x_hist[entry : entry + 1, :], 0.0)
        x_run = x_run + moved * x_taps[3 - distance : 4 - distance, :]
    x_conv = x_run * jax.nn.sigmoid(x_run)
    bc_run = bc_ref[:, 0:64].astype(F32) * bc_taps_ref[:, 3:4]
    for distance in range(1, 4):
        pick = ((distance > depth) & (lane == 3 - distance + depth)).astype(BF16)
        mover = jnp.concatenate([hops[distance], pick], axis=1)
        moved = lax.dot_general(bc_ref[...], mover, NT, preferred_element_type=F32)
        bc_run = bc_run + moved * bc_taps_ref[:, 3 - distance : 4 - distance]
    bc_conv = (bc_run * jax.nn.sigmoid(bc_run)).astype(BF16)

    raw = local_ref[0:2, :] + column_of(head_ref[0:1, 0:128], 128)[0:2, :]
    step = jnp.maximum(raw, 0.0) + jnp.log1p(jnp.exp(-jnp.abs(raw)))
    log_decay = -jnp.exp(column_of(head_ref[1:2, 0:128], 128)[0:2, :]) * step
    cum = lax.dot_general(
        jnp.concatenate([log_decay, jnp.zeros((6, 64), F32)], axis=0),
        anc.astype(F32),
        NT,
        precision=lax.Precision.HIGHEST,
        preferred_element_type=F32,
    )

    eye = (lane == row).astype(BF16)
    c_node = lax.dot_general(eye, bc_conv[256:512, :], NT, preferred_element_type=F32).astype(BF16)
    scores = jnp.dot(c_node, bc_conv[0:256, :], preferred_element_type=F32)
    state = state_ref[0, 0].reshape(2 * P_SIZE, N).astype(BF16)
    carried = lax.dot_general(c_node, state, NT, preferred_element_type=F32)
    x_bf = x_conv.astype(BF16)
    is_anc = anc > 0
    inner = []
    start = []
    for head in range(2):
        cum_row = cum[head : head + 1, :]
        cum_col = column_of(cum_row, 64)
        gap = jnp.where(is_anc, cum_col - cum_row, 0.0)
        weight = jnp.where(is_anc, jnp.exp(gap), 0.0) * scores * step[head : head + 1, :]
        inner.append(jnp.dot(weight.astype(BF16), x_bf, preferred_element_type=F32))
        start.append(jnp.exp(cum_col))
    first = lax.broadcasted_iota(jnp.int32, (64, 128), 1) < P_SIZE
    skip = column_of(head_ref[2:3, 0:128], 128)
    mixed = (
        jnp.where(first, inner[0], inner[1])
        + jnp.where(first, start[0], start[1]) * carried
        + jnp.where(first, skip[0:1, :], skip[1:2, :]) * x_conv
    )
    gated = mixed * (gate * jax.nn.sigmoid(gate))
    group_sq = jnp.sum(gated * gated, axis=1, keepdims=True)
    out_ref[:, 0:128] = (gated * gain).astype(BF16)
    out_ref[:, 128:256] = jnp.broadcast_to(group_sq, (64, 128)).astype(BF16)


def scale_heads_kernel(parts_ref, out_ref):
    total = parts_ref[0, :, 128:256].astype(F32)
    for part in range(1, parts_ref.shape[0]):
        total = total + parts_ref[part, :, 128:256].astype(F32)
    scale = lax.rsqrt(total / (H // G * P_SIZE) + EPSILON)
    for part in range(parts_ref.shape[0]):
        piece = parts_ref[part, :, 0:128].astype(F32) * scale
        out_ref[:, part * 128 : (part + 1) * 128] = piece.astype(BF16)


def local(
    hidden_in,
    norm_mixer,
    mixer_in,
    bc_proj,
    dt_proj,
    dt_bias,
    a_log,
    skip_d,
    conv_x,
    conv_bc,
    x_cache,
    bc_cache,
    ssm_cache,
    slot_ids,
    parents,
    ancestors,
    norm_gated,
    out_proj,
    norm_ffn,
    ffn_up,
    ffn_down,
):
    rows = lax.axis_size("row")
    cols = lax.axis_size("col")
    row_index = lax.axis_index("row")
    col_index = lax.axis_index("col")
    request = row_index // G
    group_index = row_index % G

    def pick(table, index, axis=0):
        return lax.dynamic_index_in_dim(table, index, axis, keepdims=False)

    out_weights = lax.all_gather(out_proj, "col", axis=0, tiled=False)

    hidden = spread(hidden_in, "col").reshape(512, 256)
    gain = norm_mixer[None, :]
    side = jnp.concatenate([bc_proj, dt_proj, jnp.zeros((256, G, 30), BF16)], axis=2)
    side = side.reshape(256, 256).T
    side_parts = call(
        project_side_kernel,
        jax.ShapeDtypeStruct((rows // G, G, 16, 256), BF16),
        hidden,
        gain,
        side,
    )
    side_parts = lax.all_to_all(side_parts.reshape(rows, 16, 256), "row", 0, 0, tiled=True)
    bc_own, local_rows = call(
        combine_side_kernel,
        (jax.ShapeDtypeStruct((16, 128), BF16), jax.ShapeDtypeStruct((8, 64), F32)),
        side_parts,
    )
    main_parts = call(
        project_main_kernel,
        jax.ShapeDtypeStruct((rows // G, G, 64, 256), BF16),
        hidden,
        gain,
        mixer_in.reshape(256, -1),
    )
    main_parts, bc_own = lax.optimization_barrier((main_parts, bc_own))
    main_parts = lax.all_to_all(main_parts.reshape(rows, 64, 256), "row", 0, 0, tiled=True)
    bc_new = lax.all_gather(bc_own, "col", axis=0, tiled=False)

    slot_index = pick(slot_ids, request)
    bc_hist = jnp.pad(pick(bc_cache[0], slot_index).T, ((0, 0), (0, 61)))
    bc_taps = jnp.pad(pick(conv_bc, group_index, 1).T.astype(F32), ((0, 0), (0, 124)))
    head = jnp.stack([pick(dt_bias, group_index), pick(a_log, group_index), pick(skip_d, group_index)])
    head = jnp.pad(head, ((0, 5), (0, 126)))
    place = jnp.stack([request, group_index]).astype(jnp.int32)

    def whole(array):
        shape = array.shape
        return pl.BlockSpec(shape, lambda step, place, slots: (0,) * len(shape))

    def slot_block(*shape):
        zeros = (0,) * (len(shape) - 2)
        return pl.BlockSpec(shape, lambda step, place, slots: (0, slots[place[0]]) + zeros)

    operands = [
        (main_parts, whole(main_parts)),
        (bc_new, whole(bc_new)),
        (local_rows, whole(local_rows)),
        (x_cache, slot_block(1, 1, 3, 128)),
        (bc_hist, whole(bc_hist)),
        (ssm_cache, slot_block(1, 1, 2, P_SIZE, N)),
        (conv_x, whole(conv_x)),
        (bc_taps, whole(bc_taps)),
        (head, whole(head)),
        (norm_gated, whole(norm_gated)),
        (parents, whole(parents)),
        (ancestors, pl.BlockSpec((1, 64, 64), lambda step, place, slots: (place[0], 0, 0))),
    ]
    mixed = pl.pallas_call(
        mixer_kernel,
        grid_spec=pltpu.PrefetchScalarGridSpec(
            num_scalar_prefetch=2,
            grid=(1,),
            in_specs=[spec for _, spec in operands],
            out_specs=pl.BlockSpec((64, 256), lambda step, place, slots: (0, 0)),
            scratch_shapes=[pltpu.VMEM((512, 128), BF16)],
        ),
        out_shape=jax.ShapeDtypeStruct((64, 256), BF16),
        compiler_params=pltpu.CompilerParams(vmem_limit_bytes=VMEM_LIMIT),
    )(place, slot_ids, *[operand for operand, _ in operands])

    mixed = lax.all_to_all(mixed.reshape(cols, 4, 256), "col", 0, 0, tiled=True)
    mixed = call(scale_heads_kernel, jax.ShapeDtypeStruct((4, cols * 128), BF16), mixed)
    heads = lax.all_gather(mixed, "row", axis=0, tiled=False)
    heads = heads.reshape(rows // G, G, 4, cols, 128)
    mixer_out = jnp.einsum("qgtck,cgkd->qtd", heads, out_weights, preferred_element_type=F32)
    residual = lax.dynamic_slice(
        hidden.reshape(8, 64, 256), (0, 4 * col_index, 0), (8, 4, 256)
    ).astype(F32)
    after = (residual + mixer_out).astype(BF16).reshape(32, 256)
    all_after = lax.all_gather(after, "col", axis=0, tiled=False)
    all_after = all_after.reshape(cols, 8, 4, 256).transpose(1, 0, 2, 3).reshape(512, 256)
    after_wide = all_after.astype(F32)
    ffn_part = jnp.sum(after_wide * after_wide, axis=1)
    up_term = jnp.dot(
        (after_wide * norm_ffn[None, :]).astype(BF16), ffn_up, preferred_element_type=F32
    )
    up_term = jnp.concatenate([up_term, ffn_part[:, None]], axis=1).astype(BF16)
    up_sum = sum_parts(up_term.reshape(rows, -1, up_term.shape[1]), "row")
    up_share = up_sum[:, :-1] * lax.rsqrt(up_sum[:, -1:] / D + EPSILON)
    act_share = jnp.square(jax.nn.relu(up_share)).astype(BF16)
    act_all = spread(act_share, "row").reshape(512, -1)
    ffn_term = jnp.dot(act_all, ffn_down, preferred_element_type=F32).astype(BF16)
    ffn_out = sum_parts(ffn_term.reshape(cols, -1, ffn_term.shape[1]), "col")
    own_after = lax.dynamic_slice(all_after, (32 * col_index, 0), (32, 256))
    return (own_after.astype(F32) + ffn_out).astype(BF16)


def solution(mesh):
    return jax.shard_map(
        local,
        mesh=mesh,
        in_specs=(
            P("col", "row"),
            P("row"),
            P("row", None, "col", None),
            P("row", None, "col"),
            P("row", None, "col"),
            P(None, "col"),
            P(None, "col"),
            P(None, "col"),
            P(None, None, "col"),
            P(),
            P("row", None, None, "col"),
            P("row", None, None, None),
            P("row", None, "col", None, None),
            P(),
            P(),
            P(),
            P(None, "col"),
            P(None, "col", "row"),
            P("row"),
            P("row", "col"),
            P("col", "row"),
        ),
        out_specs=P("col", "row"),
        check_vma=False,
    )
```

time: 310 us -> 290 us (0.935)
  waiting for transfers between devices: 81 us -> 55.2 us
  starting transfers between devices: 31.3 us -> 39.7 us
  blocking collectives: 148 us -> 152 us
  local copies, waits for them, and re-layouts: 16.8 us -> 12.9 us
    all_gather x1, waiting for transfers between devices: 39.6 us -> 0.02 us  [local(): out_weights = lax.all_gather(out_proj, 'col', axis=0, tiled=False)]
    all_gather x0 -> x1, blocking collectives: none -> 30.5 us  [local(): bc_new = lax.all_gather(bc_own, 'col', axis=0, tiled=False)]
    all_to_all x1 -> x0, blocking collectives: 27.2 us -> none  [local(): lax.all_to_all(parts.reshape(rows, 80, 256), 'row', 0, 0, tiled=True)]
    all_to_all x0 -> x3, starting transfers between devices: none -> 18.9 us  [the longest x1 7.63 us: local(): mixed = lax.all_to_all(mixed.reshape(cols, 4, 256), 'col', 0, 0, tiled=True)]
    all_to_all x0 -> x3, waiting for transfers between devices: none -> 18.4 us  [the longest x1 11.5 us: local(): mixed = lax.all_to_all(mixed.reshape(cols, 4, 256), 'col', 0, 0, tiled=True)]
    all_to_all x2 -> x1, starting transfers between devices: 22.2 us -> 15.2 us  [spread(): lax.all_to_all(jnp.broadcast_to(block[None], (size,) + block.shape), axis...]
    all_to_all x2 -> x1, waiting for transfers between devices: 23.2 us -> 18 us  [spread(): lax.all_to_all(jnp.broadcast_to(block[None], (size,) + block.shape), axis...]
    unnamed x24 -> x54, local copies, waits for them, and re-layouts: 1.08 us -> 6.29 us
  transfers between devices with their start and end apart: 4 -> 6, of which waited for: 3 -> 4; matrix products, arithmetic and copies ran while one was open for 5% -> 3% of each run, Pallas kernels for 0% -> 2%
where the time goes in v3:
time: 290 us; the launch traced here: 289 us
  blocking collectives  152 us (52%)
  waiting for transfers between devices  55.2 us (19%)
  starting transfers between devices  39.7 us (14%)
  between operations  15.5 us (5%)
  local copies, waits for them, and re-layouts  12.9 us (4%)
  matrix products  5.21 us (2%)
  Pallas kernels  4.59 us (2%)
  other arithmetic  4.2 us (1%)
    all_to_all x1, blocking collectives, sum_parts(): received = lax.all_to_all(parts, axis, 0, 0, tiled=True)  35.3 us
    all_to_all x1, blocking collectives, spread(): lax.all_to_all(jnp.broadcast_to(block[None], (size,) + block.shape), axis...  32.2 us
    all_gather x1, blocking collectives, local(): bc_new = lax.all_gather(bc_own, 'col', axis=0, tiled=False)  30.5 us
    all_gather x1, blocking collectives, local(): all_after = lax.all_gather(after, 'col', axis=0, tiled=False)  28.5 us
    all_gather x1, blocking collectives, local(): heads = lax.all_gather(mixed, 'row', axis=0, tiled=False)  25.1 us
    all_to_all x1, waiting for transfers between devices, sum_parts(): received = lax.all_to_all(parts, axis, 0, 0, tiled=True)  18.1 us
    all_to_all x1, waiting for transfers between devices, spread(): lax.all_to_all(jnp.broadcast_to(block[None], (size,) + block.shape), axis...  18 us
    all_to_all x1, starting transfers between devices, spread(): lax.all_to_all(jnp.broadcast_to(block[None], (size,) + block.shape), axis...  15.2 us
  transfers between devices with their start and end apart: 6, of which 4 were waited for; matrix products, arithmetic and copies ran while one was open for 3% of the time, Pallas kernels for 2%

profile of v3, /device:TPU:32, one launch (start us, length us, event | category | flops | bytes accessed | tf_op | source)
XLA Modules:
  0.0 289.0 jit_solution(7901681497400501150)
XLA Ops:
  6.5 0.7 all-gather.6.cloned.1.call-update
  7.3 1.4 broadcast_in_dim.8
  8.7 15.2 %all-to-all-start = ((bf16[16,32,256]{2,1,0:T(8,128)(2,1)}), bf16[16,32,256]{2,1,0:T(8,128)(2,1)S(1)}, u32[]{:S(2)}, u32[]{:S(2)}) async-start(bf16[16,32,256]{2,1,0:T(8,128)(2,1)} %broadcast_in_dim.8), calls=%async_computation | async-start | bytes 524288 | tf_op jit(solution)/shard_map/all_to_all | solution.py:23
  24.0 0.9 maximum_maximum_fusion
  24.9 18.0 %all-to-all-done = bf16[16,32,256]{2,1,0:T(8,128)(2,1)S(1)} async-done(((bf16[16,32,256]{2,1,0:T(8,128)(2,1)}), bf16[16,32,256]{2,1,0:T(8,128)(2,1)S(1)}, u32[]{:S(2)}, u32[]{:S(2)}) %all-to-all-start) | async-done | bytes 262176 | tf_op jit(solution)/shard_map/all_to_all | solution.py:23
  42.9 0.7 copy-done.9
  43.6 1.3 shard_map.200
  44.9 7.3 %all-to-all-start.1 = ((bf16[32,16,256]{2,1,0:T(8,128)(2,1)}), bf16[32,16,256]{2,1,0:T(8,128)(2,1)S(1)}, u32[]{:S(2)}, u32[]{:S(2)}) async-start(bf16[32,16,256]{2,1,0:T(8,128)(2,1)} %bitcast.7), calls=%async_computation.1 | async-start | bytes 524288 | tf_op jit(solution)/shard_map/all_to_all | solution.py:254
  52.2 0.4 reshape.56.main_ref
  52.8 1.5 shard_map.199
  54.2 6.9 %all-to-all-done.1.parts_ref = bf16[32,16,256]{2,1,0:T(8,128)(2,1)S(1)} async-done(((bf16[32,16,256]{2,1,0:T(8,128)(2,1)}), bf16[32,16,256]{2,1,0:T(8,128)(2,1)S(1)}, u32[]{:S(2)}, u32[]{:S(2)}) %all-to-all-start.1) | async-done | bytes 262176 | tf_op jit(solution)/shard_map/all_to_all | solution.py:254
  61.3 0.6 copy-done.7
  61.8 0.6 copy-done.11
  62.4 3.9 %all-to-all-start.2 = ((bf16[32,64,256]{2,1,0:T(8,128)(2,1)}), bf16[32,64,256]{2,1,0:T(8,128)(2,1)S(1)}, u32[]{:S(2)}, u32[]{:S(2)}) async-start(bf16[32,64,256]{2,1,0:T(8,128)(2,1)} %bitcast.8), calls=%async_computation.2 | async-start | bytes 2097152 | tf_op jit(solution)/shard_map/all_to_all | solution.py:268
  66.4 0.6 dynamic_slice.29
  68.2 0.8 copy.71
  69.6 0.2 copy.70
  70.3 0.6 pad_add_fusion.place_ref
  70.9 0.9 pad_convert_fusion.bc_taps_ref
  71.8 30.5 %all-gather = bf16[256,128]{1,0:T(8,128)(2,1)} all-gather(bf16[16,128]{1,0:T(8,128)(2,1)} %copy-done.11), channel_id=2, replica_groups=mesh['row'=32,'col'=16] {'col'}, dimensions={0}, use_global_device_ids=true | all-gather | bytes 69632 | tf_op jit(solution)/shard_map/all_gather | solution.py:269
  102.4 0.8 copy-done.3
  103.2 0.7 copy-done.8
  103.9 0.7 copy-done.12
  104.6 0.7 copy-done.14
  105.2 0.6 copy-done.15
  105.8 1.7 shard_map.202
  107.5 0.6 copy-done.4
  108.1 1.4 reshape.60
  109.5 7.6 %all-to-all-start.3 = ((bf16[16,4,256]{2,1,0:T(4,128)(2,1)}), bf16[16,4,256]{2,1,0:T(4,128)(2,1)S(1)}, u32[]{:S(2)}, u32[]{:S(2)}) async-start(bf16[16,4,256]{2,1,0:T(4,128)(2,1)} %reshape.60), calls=%async_computation.3 | async-start | bytes 65536 | tf_op jit(solution)/shard_map/all_to_all | solution.py:313
  117.1 11.5 %all-to-all-done.3.parts_ref = bf16[16,4,256]{2,1,0:T(4,128)(2,1)S(1)} async-done(((bf16[16,4,256]{2,1,0:T(4,128)(2,1)}), bf16[16,4,256]{2,1,0:T(4,128)(2,1)S(1)}, u32[]{:S(2)}, u32[]{:S(2)}) %all-to-all-start.3) | async-done | bytes 32800 | tf_op jit(solution)/shard_map/all_to_all | solution.py:313
  128.6 25.1 %all-gather.3 = bf16[32,4,2048]{2,1,0:T(4,128)(2,1)S(1)} all-gather(bf16[1,4,2048]{2,1,0:T(4,128)(2,1)S(1)} %bitcast.47), channel_id=3, replica_groups=mesh['row'=32,'col'=16] {'row'}, dimensions={0}, use_global_device_ids=true | all-gather | bytes 540672 | tf_op jit(solution)/shard_map/all_gather | solution.py:315
  153.7 0.3 reshape.77
  154.1 3.1 %fusion.1 = bf16[8,4,256]{2,0,1:T(8,128)(2,1)S(1)} fusion(bf16[16,4,128,256,1]{3,2,1,0,4:T(8,128)(2,1)} %bitcast.50, bf16[8,4,4,16,128]{4,3,2,1,0:T(8,128)(2,1)S(1)} %reshape.77, bf16[8,4,256]{2,1,0:T(4,128)(2,1)S(1)} %constant_dynamic-slice_fusion.5), kind=kOutput, calls=%fused_computation.6 | convolution fusion | flops 134242304 | bytes 4751360 | tf_op jit(solution)/shard_map/qgtck,cgkd->qtd/dot_general | solution.py:317
  157.2 28.5 %all_gather.27 = bf16[16,32,256]{2,1,0:T(8,128)(2,1)S(1)} all-gather(bf16[1,32,256]{2,1,0:T(8,128)(2,1)S(1)} %all_gather_reshape.3), channel_id=1, replica_groups=mesh['row'=32,'col'=16] {'col'}, dimensions={0}, use_global_device_ids=true | all-gather | bytes 278528 | tf_op jit(solution)/shard_map/all_gather | solution.py:322
  185.8 0.2 bitcast_convert_fusion
  186.0 0.3 copy.81
  186.3 0.2 reshape.66
  186.5 0.2 multiply_reduce_fusion
  186.9 0.7 convolution_convert_fusion
  187.7 0.2 pad_maximum_fusion
  187.9 35.3 %all_to_all.35 = bf16[32,16,2049]{2,1,0:T(8,128)(2,1)S(1)} all-to-all(bf16[32,16,2049]{2,1,0:T(8,128)(2,1)S(1)} %pad_maximum_fusion), channel_id=1, replica_groups=mesh['row'=32,'col'=16] {'row'}, dimensions={0} | all-to-all | bytes 4196352 | tf_op jit(solution)/shard_map/all_to_all | solution.py:29
  223.2 0.4 convert_reduce_fusion
  223.8 0.2 broadcast_in_dim.11
  224.0 32.2 %all_to_all.36 = bf16[32,16,2048]{2,1,0:T(8,128)(2,1)S(1)} all-to-all(bf16[32,16,2048]{2,1,0:T(8,128)(2,1)S(1)} %broadcast_in_dim.11), channel_id=1, replica_groups=mesh['row'=32,'col'=16] {'row'}, dimensions={0} | all-to-all | bytes 4194304 | tf_op jit(solution)/shard_map/all_to_all | solution.py:23
  256.2 1.4 convolution_convert_fusion.1
  257.6 5.6 %all-to-all-start.6 = ((bf16[16,32,256]{2,1,0:T(8,128)(2,1)}), bf16[16,32,256]{2,1,0:T(8,128)(2,1)S(1)}, u32[]{:S(2)}, u32[]{:S(2)}) async-start(bf16[16,32,256]{2,1,0:T(8,128)(2,1)} %bitcast.25), calls=%async_computation.6 | async-start | bytes 524288 | tf_op jit(solution)/shard_map/all_to_all | solution.py:29
  263.4 18.1 %all-to-all-done.6 = bf16[16,32,256]{2,1,0:T(8,128)(2,1)S(1)} async-done(((bf16[16,32,256]{2,1,0:T(8,128)(2,1)}), bf16[16,32,256]{2,1,0:T(8,128)(2,1)S(1)}, u32[]{:S(2)}, u32[]{:S(2)}) %all-to-all-start.6) | async-done | bytes 262176 | tf_op jit(solution)/shard_map/all_to_all | solution.py:29
  281.6 0.6 add_convert_fusion
  (68 shorter events, 1.6 us)
Async XLA Ops:
  6.5 180.4 %copy-start = (bf16[256,2048]{1,0:T(8,128)(2,1)S(1)}, bf16[256,2048]{1,0:T(8,128)(2,1)}, u32[]{:S(2)}) copy-start(bf16[256,2048]{1,0:T(8,128)(2,1)} %param.40) | copy-start | bytes 3145732
  6.5 46.1 %copy-start.10 = (f32[256]{0:T(256)S(1)}, f32[256]{0:T(256)}, u32[]{:S(2)}) copy-start(f32[256]{0:T(256)} %param.22) | copy-start | bytes 3076
  6.5 45.7 %copy-start.16 = (bf16[256,4,2,128]{3,2,1,0:T(2,128)(2,1)S(1)}, bf16[256,4,2,128]{3,2,1,0:T(2,128)(2,1)}, u32[]{:S(2)}) copy-start(bf16[256,4,2,128]{3,2,1,0:T(2,128)(2,1)} %param.23) | copy-start | bytes 1572868
  6.5 147.6 %all-gather.6.cloned.1.call-start = ((), (), s32[]{:S(2)}) async-start(), calls=%async_computation.7 | async-start | bytes 4456448 | tf_op jit(solution)/shard_map/all_gather | solution.py:241
  8.7 34.2 %all-to-all-start = ((bf16[16,32,256]{2,1,0:T(8,128)(2,1)}), bf16[16,32,256]{2,1,0:T(8,128)(2,1)S(1)}, u32[]{:S(2)}, u32[]{:S(2)}) async-start(bf16[16,32,256]{2,1,0:T(8,128)(2,1)} %broadcast_in_dim.8), calls=%async_computation | async-start | bytes 524288 | tf_op jit(solution)/shard_map/all_to_all | solution.py:23
  42.9 0.7 copy-start.9
  44.9 16.2 %all-to-all-start.1 = ((bf16[32,16,256]{2,1,0:T(8,128)(2,1)}), bf16[32,16,256]{2,1,0:T(8,128)(2,1)S(1)}, u32[]{:S(2)}, u32[]{:S(2)}) async-start(bf16[32,16,256]{2,1,0:T(8,128)(2,1)} %bitcast.7), calls=%async_computation.1 | async-start | bytes 524288 | tf_op jit(solution)/shard_map/all_to_all | solution.py:254
  52.6 13.8 %copy-start.13 = (s32[8]{0:T(128)S(1)}, s32[8]{0:T(128)}, u32[]{:S(2)}) copy-start(s32[8]{0:T(128)} %slot_ref.1) | copy-start | bytes 100
  52.6 15.5 %copy-start.17 = (bf16[4,4,512]{2,1,0:T(4,128)(2,1)S(1)}, bf16[4,4,512]{2,1,0:T(4,128)(2,1)}, u32[]{:S(2)}) copy-start(bf16[4,4,512]{2,1,0:T(4,128)(2,1)} %param.30) | copy-start | bytes 49156
  52.6 16.9 %copy-start.19 = (bf16[1,4,3,512]{3,1,2,0:T(4,128)(2,1)S(1)}, bf16[1,4,3,512]{3,1,2,0:T(4,128)(2,1)}, u32[]{:S(2)}) copy-start(bf16[1,4,3,512]{3,1,2,0:T(4,128)(2,1)} %param.32) | copy-start | bytes 36868
  52.7 17.2 %copy-start.21 = (f32[4,2]{0,1:T(2,128)S(1)}, f32[4,2]{0,1:T(2,128)}, u32[]{:S(2)}) copy-start(f32[4,2]{0,1:T(2,128)} %param.28) | copy-start | bytes 100
  52.7 17.2 %copy-start.22 = (f32[4,2]{0,1:T(2,128)S(1)}, f32[4,2]{0,1:T(2,128)}, u32[]{:S(2)}) copy-start(f32[4,2]{0,1:T(2,128)} %param.27) | copy-start | bytes 100
  52.7 17.4 %copy-start.20 = (f32[4,2]{0,1:T(2,128)S(1)}, f32[4,2]{0,1:T(2,128)}, u32[]{:S(2)}) copy-start(f32[4,2]{0,1:T(2,128)} %param.26) | copy-start | bytes 100
  52.7 17.6 %copy-start.18 = (bf16[1,4,3,128]{3,1,2,0:T(4,128)(2,1)S(1)}, bf16[1,4,3,128]{3,1,2,0:T(4,128)(2,1)}, u32[]{:S(2)}) copy-start(bf16[1,4,3,128]{3,1,2,0:T(4,128)(2,1)} %param.31) | copy-start | bytes 9220
  52.7 49.6 %copy-start.1 = (f32[1,4,2,64,256]{4,3,2,1,0:T(8,128)S(1)}, f32[1,4,2,64,256]{4,3,2,1,0:T(8,128)}, u32[]{:S(2)}) copy-start(f32[1,4,2,64,256]{4,3,2,1,0:T(8,128)} %state_ref.1) | copy-start | bytes 1572868
  52.7 49.6 %copy-start.2 = (s32[8,64,64]{2,1,0:T(8,128)S(1)}, s32[8,64,64]{2,1,0:T(8,128)}, u32[]{:S(2)}) copy-start(s32[8,64,64]{2,1,0:T(8,128)} %anc_ref.1) | copy-start | bytes 393220
  52.7 49.6 %copy-start.5 = (bf16[4,4,128]{2,1,0:T(4,128)(2,1)S(1)}, bf16[4,4,128]{2,1,0:T(4,128)(2,1)}, u32[]{:S(2)}) copy-start(bf16[4,4,128]{2,1,0:T(4,128)(2,1)} %x_taps_ref.1) | copy-start | bytes 12292
  52.7 49.6 %copy-start.6 = (s32[8,64]{1,0:T(8,128)S(1)}, s32[8,64]{1,0:T(8,128)}, u32[]{:S(2)}) copy-start(s32[8,64]{1,0:T(8,128)} %parents_ref.1) | copy-start | bytes 6148
  61.3 0.6 copy-start.7
  61.8 0.6 copy-start.11
  62.4 39.9 %all-to-all-start.2 = ((bf16[32,64,256]{2,1,0:T(8,128)(2,1)}), bf16[32,64,256]{2,1,0:T(8,128)(2,1)S(1)}, u32[]{:S(2)}, u32[]{:S(2)}) async-start(bf16[32,64,256]{2,1,0:T(8,128)(2,1)} %bitcast.8), calls=%async_computation.2 | async-start | bytes 2097152 | tf_op jit(solution)/shard_map/all_to_all | solution.py:268
  102.4 0.8 copy-start.3
  103.2 0.7 copy-start.8
  103.9 0.7 copy-start.12
  104.6 0.7 copy-start.14
  105.2 0.6 copy-start.15
  107.5 0.6 copy-start.4
  109.5 19.1 %all-to-all-start.3 = ((bf16[16,4,256]{2,1,0:T(4,128)(2,1)}), bf16[16,4,256]{2,1,0:T(4,128)(2,1)S(1)}, u32[]{:S(2)}, u32[]{:S(2)}) async-start(bf16[16,4,256]{2,1,0:T(4,128)(2,1)} %reshape.60), calls=%async_computation.3 | async-start | bytes 65536 | tf_op jit(solution)/shard_map/all_to_all | solution.py:313
  157.2 29.7 %copy-start.23 = (f32[256]{0:T(256)S(1)}, f32[256]{0:T(256)}, u32[]{:S(2)}) copy-start(f32[256]{0:T(256)} %param.39) | copy-start | bytes 3076
  224.0 32.2 %copy-start.24 = (bf16[2048,256]{1,0:T(8,128)(2,1)S(1)}, bf16[2048,256]{1,0:T(8,128)(2,1)}, u32[]{:S(2)}) copy-start(bf16[2048,256]{1,0:T(8,128)(2,1)} %param.41) | copy-start | bytes 3145732
  257.6 23.9 %all-to-all-start.6 = ((bf16[16,32,256]{2,1,0:T(8,128)(2,1)}), bf16[16,32,256]{2,1,0:T(8,128)(2,1)S(1)}, u32[]{:S(2)}, u32[]{:S(2)}) async-start(bf16[16,32,256]{2,1,0:T(8,128)(2,1)} %bitcast.25), calls=%async_computation.6 | async-start | bytes 524288 | tf_op jit(solution)/shard_map/all_to_all | solution.py:29
Sparse Core Ops, SparseCore 0:
  9.4 86.6 all-gather.5

commit v4 on v3

v4 whole, which is shorter than its diff:
```python
import functools

import jax
import jax.numpy as jnp
from jax import lax
from jax.experimental import pallas as pl
from jax.experimental.pallas import tpu as pltpu
from jax.sharding import PartitionSpec as P

D = 8192
H = 128
P_SIZE = 64
N = 256
G = 4

EPSILON = 1e-05
F32 = jnp.float32
BF16 = jnp.bfloat16
NT = (((1,), (1,)), ((), ()))
VMEM_LIMIT = 48 * 1024 * 1024


def exchange(parts, axis, groups=None):
    return lax.all_to_all(parts, axis, 0, 0, tiled=True, axis_index_groups=groups)


def call(kernel, out_shape, *operands):
    return pl.pallas_call(
        kernel,
        out_shape=out_shape,
        compiler_params=pltpu.CompilerParams(vmem_limit_bytes=VMEM_LIMIT),
    )(*operands)


def project_kernel(hidden_ref, gain_ref, main_ref, side_ref, out_ref):
    hidden = hidden_ref[...].astype(F32)
    normed = (hidden * gain_ref[...]).astype(BF16)
    squares = (hidden * hidden).astype(BF16)
    ones = jnp.ones((16, hidden.shape[1]), BF16)
    stat = lax.dot_general(ones, squares, NT, preferred_element_type=F32)
    for group in range(G):
        main = jnp.dot(
            normed, main_ref[:, group * 256 : (group + 1) * 256], preferred_element_type=F32
        ).astype(BF16)
        side = lax.dot_general(
            side_ref[group * 64 : (group + 1) * 64, :], normed, NT, preferred_element_type=F32
        )
        for request in range(8):
            nodes = slice(request * 64, (request + 1) * 64)
            out_ref[request, group, 0:64, :] = main[nodes, :]
            pieces = [side[0:16, nodes], side[16:32, nodes], side[32:48, nodes], stat[:, nodes]]
            out_ref[request, group, 64:80, :] = jnp.concatenate(pieces, axis=1).astype(BF16)


def column_of(row, size):
    eye = lax.broadcasted_iota(jnp.int32, (size, size), 0) == lax.broadcasted_iota(
        jnp.int32, (size, size), 1
    )
    wide = jnp.broadcast_to(row, (size, size))
    return jnp.sum(jnp.where(eye, wide, jnp.zeros_like(wide)), axis=1, keepdims=True)


def combine_kernel(parts_ref, bc_ref, local_ref):
    total = parts_ref[0].astype(F32)
    for part in range(1, parts_ref.shape[0]):
        total = total + parts_ref[part].astype(F32)
    scale = lax.rsqrt(total[64:65, 192:256] / D + EPSILON)
    bc = (total[64:80, 0:128] * jnp.concatenate([scale, scale], axis=1)).astype(BF16)
    for col in range(bc_ref.shape[0]):
        bc_ref[col] = bc
    main = total[0:64, :]
    main = jnp.concatenate(
        [main[:, 0:64], main[:, 128:192], main[:, 64:128], main[:, 192:256]], axis=1
    )
    local_ref[0:64, :] = main * column_of(scale, 64)
    step = total[64:72, 128:192] * scale
    local_ref[64:72, :] = jnp.concatenate([step] * 4, axis=1)


BASE, ANC, HOPS, SMALL, PACK = 512, 576, 640, 768, 784


def prepare_kernel(
    place_ref,
    slot_ref,
    x_hist_ref,
    bc_hist_ref,
    state_ref,
    x_taps_ref,
    bc_taps_ref,
    offset_ref,
    rate_ref,
    skip_ref,
    gain_ref,
    parents_ref,
    anc_ref,
    pack_ref,
    state_out_ref,
):
    request = place_ref[0]
    group = place_ref[1]

    def of_group(ref):
        table = ref[...]
        this = lax.broadcasted_iota(jnp.int32, table.shape, 0) == group
        return jnp.sum(jnp.where(this, table, 0.0), axis=0, keepdims=True)

    x_taps = jnp.zeros((4, 128), F32)
    bc_taps = jnp.zeros((4, 512), F32)
    for index in range(G):
        x_taps = jnp.where(group == index, x_taps_ref[:, index, :].astype(F32), x_taps)
        bc_taps = jnp.where(group == index, bc_taps_ref[:, index, :].astype(F32), bc_taps)

    lane = lax.broadcasted_iota(jnp.int32, (64, 64), 1)
    anc = anc_ref[0]
    anc_float = anc.astype(F32)
    depth_col = jnp.sum(anc, axis=1, keepdims=True) - 1
    depth_row = lax.dot_general(
        jnp.ones((8, 64), BF16), anc_float.astype(BF16), NT, preferred_element_type=F32
    )
    depth_row = depth_row[0:1, :].astype(jnp.int32) - 1
    all_parents = parents_ref[...]
    this = lax.broadcasted_iota(jnp.int32, all_parents.shape, 0) == request
    parent_row = jnp.sum(jnp.where(this, all_parents, 0), axis=0, keepdims=True)
    hop = (column_of(parent_row, 64) == lane).astype(F32)
    hops = [hop]
    for _ in range(2):
        moved = jnp.dot(
            hops[-1].astype(BF16), hop.astype(BF16), preferred_element_type=F32
        )
        hops.append(moved)
    pack_ref[HOPS : HOPS + 64, :] = jnp.concatenate(hops[0:2], axis=1)
    pack_ref[HOPS + 64 : HOPS + 128, :] = jnp.concatenate([hops[2], hops[2]], axis=1)
    pack_ref[ANC : ANC + 64, :] = jnp.concatenate([anc_float, anc_float], axis=1)

    x_hist = x_hist_ref[0, 0].astype(F32)
    x_base = jnp.zeros((64, 128), F32)
    rows = jnp.concatenate([bc_taps, bc_hist_ref[0, 0].astype(F32), jnp.zeros((9, 512), F32)], axis=0)
    square = (512, 512)
    eye = lax.broadcasted_iota(jnp.int32, square, 0) == lax.broadcasted_iota(jnp.int32, square, 1)
    turned = lax.dot_general(
        eye.astype(BF16), rows.astype(BF16), NT, preferred_element_type=F32
    )
    bc_base = jnp.zeros((512, 64), F32)
    for distance in range(1, 4):
        tap = 3 - distance
        for entry in range(3):
            use = (distance > depth_col) & (entry == tap + depth_col)
            x_base = x_base + jnp.where(
                use, x_hist[entry : entry + 1, :] * x_taps[tap : tap + 1, :], 0.0
            )
            use = (distance > depth_row) & (entry == tap + depth_row)
            share = turned[:, 4 + entry : 5 + entry] * turned[:, tap : tap + 1]
            bc_base = bc_base + jnp.where(use, share, 0.0)
    pack_ref[0:512, :] = jnp.concatenate([bc_base, turned, jnp.zeros((512, 48), F32)], axis=1)
    pack_ref[BASE : BASE + 64, :] = x_base

    first = lax.broadcasted_iota(jnp.int32, (1, 128), 1) < P_SIZE
    offset = column_of(of_group(offset_ref), 2)
    rate = column_of(-jnp.exp(of_group(rate_ref)), 2)
    skip = column_of(of_group(skip_ref), 2)
    pack_ref[SMALL : SMALL + 16, :] = jnp.concatenate(
        [
            x_taps,
            of_group(gain_ref),
            jnp.where(first, skip[0:1, :], skip[1:2, :]),
            jnp.zeros((2, 128), F32),
            jnp.broadcast_to(offset, (2, 128)),
            jnp.broadcast_to(rate, (2, 128)),
            jnp.zeros((4, 128), F32),
        ],
        axis=0,
    )
    state_out_ref[...] = state_ref[0, 0].reshape(2 * P_SIZE, N).astype(BF16)


def mixer_kernel(local_ref, bc_new_ref, pack_ref, state_ref, out_ref, bc_ref):
    for col in range(bc_new_ref.shape[0]):
        piece = bc_new_ref[col].astype(F32)
        bc_ref[col * 32 : col * 32 + 16, :] = piece[:, 0:64].astype(BF16)
        bc_ref[col * 32 + 16 : col * 32 + 32, :] = piece[:, 64:128].astype(BF16)
    hops = [
        pack_ref[HOPS : HOPS + 64, 0:64].astype(BF16),
        pack_ref[HOPS : HOPS + 64, 64:128].astype(BF16),
        pack_ref[HOPS + 64 : HOPS + 128, 0:64].astype(BF16),
    ]
    small = pack_ref[SMALL : SMALL + 16, :]

    x_new = local_ref[0:64, 0:128]
    gate = local_ref[0:64, 128:256]
    x_high = x_new.astype(BF16)
    x_low = (x_new - x_high.astype(F32)).astype(BF16)
    x_both = jnp.concatenate([x_high, x_low], axis=1)
    x_run = pack_ref[BASE : BASE + 64, :] + x_new * small[3:4, :]
    bc_run = pack_ref[0:512, 0:64] + bc_ref[...].astype(F32) * pack_ref[0:512, 67:68]
    for distance in range(1, 4):
        tap = 3 - distance
        moved = jnp.dot(hops[distance - 1], x_both, preferred_element_type=F32)
        x_run = x_run + (moved[:, 0:128] + moved[:, 128:256]) * small[tap : tap + 1, :]
        moved = lax.dot_general(bc_ref[...], hops[distance - 1], NT, preferred_element_type=F32)
        bc_run = bc_run + moved * pack_ref[0:512, 64 + tap : 65 + tap]
    x_conv = x_run * jax.nn.sigmoid(x_run)
    bc_conv = (bc_run * jax.nn.sigmoid(bc_run)).astype(BF16)

    raw = local_ref[64:66, 0:64] + small[8:10, 0:64]
    step = jnp.maximum(raw, 0.0) + jnp.log1p(jnp.exp(-jnp.abs(raw)))
    log_decay = small[10:12, 0:64] * step
    anc = pack_ref[ANC : ANC + 64, 0:64]
    cum = lax.dot_general(
        jnp.concatenate([log_decay, jnp.zeros((6, 64), F32)], axis=0),
        anc,
        NT,
        precision=lax.Precision.HIGHEST,
        preferred_element_type=F32,
    )

    square = (64, 64)
    eye = lax.broadcasted_iota(jnp.int32, square, 0) == lax.broadcasted_iota(jnp.int32, square, 1)
    c_node = lax.dot_general(
        eye.astype(BF16), bc_conv[256:512, :], NT, preferred_element_type=F32
    ).astype(BF16)
    scores = jnp.dot(c_node, bc_conv[0:256, :], preferred_element_type=F32)
    carried = lax.dot_general(c_node, state_ref[...], NT, preferred_element_type=F32)
    x_bf = x_conv.astype(BF16)
    is_anc = anc > 0.5
    inner = []
    start = []
    for head in range(2):
        cum_row = cum[head : head + 1, :]
        cum_col = column_of(cum_row, 64)
        gap = jnp.where(is_anc, cum_col - cum_row, 0.0)
        weight = jnp.where(is_anc, jnp.exp(gap), 0.0) * scores * step[head : head + 1, :]
        inner.append(jnp.dot(weight.astype(BF16), x_bf, preferred_element_type=F32))
        start.append(jnp.exp(cum_col))
    first = lax.broadcasted_iota(jnp.int32, (64, 128), 1) < P_SIZE
    mixed = (
        jnp.where(first, inner[0], inner[1])
        + jnp.where(first, start[0], start[1]) * carried
        + small[5:6, :] * x_conv
    )
    gated = mixed * (gate * jax.nn.sigmoid(gate))
    group_sq = jnp.sum(gated * gated, axis=1, keepdims=True)
    both = jnp.concatenate(
        [gated * small[4:5, :], jnp.broadcast_to(group_sq, (64, 128))], axis=1
    )
    for col in range(out_ref.shape[0]):
        out_ref[col] = both[col * 4 : col * 4 + 4, :].astype(BF16)


def scale_heads_kernel(parts_ref, out_ref):
    total = parts_ref[0, :, 128:256].astype(F32)
    for part in range(1, parts_ref.shape[0]):
        total = total + parts_ref[part, :, 128:256].astype(F32)
    scale = lax.rsqrt(total / (H // G * P_SIZE) + EPSILON)
    for part in range(parts_ref.shape[0]):
        piece = (parts_ref[part, :, 0:128].astype(F32) * scale).astype(BF16)
        for row in range(out_ref.shape[0]):
            out_ref[row, :, part * 128 : (part + 1) * 128] = piece


def out_kernel(heads_ref, weight_ref, residual_ref, out_ref, left_ref, sum_ref):
    group = pl.program_id(0)
    for request in range(8):
        left_ref[request * 4 : request * 4 + 4, :] = heads_ref[request * G + group].astype(F32)
    left = left_ref[...].astype(BF16)
    weight = weight_ref[...].reshape(-1, 256)
    term = jnp.dot(left, weight, preferred_element_type=F32)

    @pl.when(group == 0)
    def _():
        sum_ref[...] = residual_ref[...].astype(F32)

    sum_ref[...] += term

    @pl.when(group == G - 1)
    def _():
        after = sum_ref[...].astype(BF16)
        for col in range(out_ref.shape[0]):
            out_ref[col] = after


def up_kernel(flip, parity_ref, after_ref, gain_ref, weight_ref, out_ref):
    use = parity_ref[0] if not flip else 1 - parity_ref[0]
    after = after_ref[...].astype(F32)
    after = jnp.where(use == 0, after[:, 0:16, :], after[:, 16:32, :]).reshape(256, 256)
    normed = (after * gain_ref[...]).astype(BF16)
    stat = jnp.broadcast_to(jnp.sum(after * after, axis=1, keepdims=True), (256, 128))
    stat = stat.astype(BF16)
    for block in range(4):
        lanes = slice(block * 512, (block + 1) * 512)
        term = jnp.dot(normed, weight_ref[:, lanes], preferred_element_type=F32).astype(BF16)
        for part in range(16):
            out_ref[part, :, lanes] = term[part * 16 : (part + 1) * 16, :]
    for part in range(16):
        out_ref[part, :, 2048:2176] = stat[part * 16 : (part + 1) * 16, :]


def act_kernel(parts_ref, out_ref):
    stat = parts_ref[0, :, 2048:2176].astype(F32)
    for part in range(1, parts_ref.shape[0]):
        stat = stat + parts_ref[part, :, 2048:2176].astype(F32)
    scale = lax.rsqrt(stat / D + EPSILON)
    for block in range(16):
        lanes = slice(block * 128, (block + 1) * 128)
        up = parts_ref[0, :, lanes].astype(F32)
        for part in range(1, parts_ref.shape[0]):
            up = up + parts_ref[part, :, lanes].astype(F32)
        act = jnp.maximum(up * scale, 0.0)
        act = (act * act).astype(BF16)
        for part in range(out_ref.shape[0]):
            out_ref[part, :, lanes] = act


def down_half(act_ref, weight_ref, turn_ref):
    term = jnp.dot(act_ref[...].reshape(256, -1), weight_ref[...], preferred_element_type=F32)
    for col in range(16):
        for request in range(4):
            start = col * 16 + request * 4
            turn_ref[2 * request + col // 8, col % 8 * 4 : col % 8 * 4 + 4, :] = term[
                start : start + 4, :
            ]
    return turn_ref[...].astype(BF16)


def down_mine_kernel(act_ref, weight_ref, out_ref, turn_ref):
    out_ref[...] = down_half(act_ref, weight_ref, turn_ref)


def down_other_kernel(parity_ref, act_ref, weight_ref, mine_ref, out_ref, turn_ref):
    parity = parity_ref[0]
    out_ref[pl.ds(parity * 8, 8)] = mine_ref[...]
    out_ref[pl.ds(8 - parity * 8, 8)] = down_half(act_ref, weight_ref, turn_ref)


def local(
    hidden_in,
    norm_mixer,
    mixer_in,
    bc_proj,
    dt_proj,
    dt_bias,
    a_log,
    skip_d,
    conv_x,
    conv_bc,
    x_cache,
    bc_cache,
    ssm_cache,
    slot_ids,
    parents,
    ancestors,
    norm_gated,
    out_proj,
    norm_ffn,
    ffn_up,
    ffn_down,
):
    rows = lax.axis_size("row")
    cols = lax.axis_size("col")
    row_index = lax.axis_index("row")
    col_index = lax.axis_index("col")
    place = jnp.stack([row_index // G, row_index % G]).astype(jnp.int32)
    parity = (row_index % 2).astype(jnp.int32)[None]
    swap = [(row, row ^ 1) for row in range(rows)]
    halves = [[row for row in range(rows) if row % 2 == half] for half in range(2)]
    smem = pl.BlockSpec(memory_space=pltpu.SMEM)
    vmem = pl.BlockSpec(memory_space=pltpu.VMEM)
    params = pltpu.CompilerParams(vmem_limit_bytes=VMEM_LIMIT)

    out_weights = lax.all_gather(out_proj, "col", axis=0, tiled=False)

    hidden = exchange(jnp.broadcast_to(hidden_in[None], (cols,) + hidden_in.shape), "col")
    side = jnp.concatenate([bc_proj, dt_proj, jnp.zeros((256, G, 30), BF16)], axis=2)
    parts = call(
        project_kernel,
        jax.ShapeDtypeStruct((rows // G, G, 80, 256), BF16),
        hidden.reshape(512, 256),
        norm_mixer[None, :],
        mixer_in.reshape(256, -1),
        side.reshape(256, 256).T,
    )
    parts = exchange(parts.reshape(rows, 80, 256), "row")

    def whole(array):
        shape = array.shape
        return pl.BlockSpec(shape, lambda step, place, slots: (0,) * len(shape))

    def slot_block(*shape):
        zeros = (0,) * (len(shape) - 2)
        return pl.BlockSpec(shape, lambda step, place, slots: (0, slots[place[0]]) + zeros)

    operands = [
        (x_cache, slot_block(1, 1, 3, 128)),
        (bc_cache, slot_block(1, 1, 3, 512)),
        (ssm_cache, slot_block(1, 1, 2, P_SIZE, N)),
        (conv_x, whole(conv_x)),
        (conv_bc, whole(conv_bc)),
        (dt_bias, whole(dt_bias)),
        (a_log, whole(a_log)),
        (skip_d, whole(skip_d)),
        (norm_gated, whole(norm_gated)),
        (parents, whole(parents)),
        (ancestors, pl.BlockSpec((1, 64, 64), lambda step, place, slots: (place[0], 0, 0))),
    ]
    pack, state = pl.pallas_call(
        prepare_kernel,
        grid_spec=pltpu.PrefetchScalarGridSpec(
            num_scalar_prefetch=2,
            grid=(1,),
            in_specs=[spec for _, spec in operands],
            out_specs=[
                pl.BlockSpec((PACK, 128), lambda step, place, slots: (0, 0)),
                pl.BlockSpec((2 * P_SIZE, N), lambda step, place, slots: (0, 0)),
            ],
        ),
        out_shape=[
            jax.ShapeDtypeStruct((PACK, 128), F32),
            jax.ShapeDtypeStruct((2 * P_SIZE, N), BF16),
        ],
        compiler_params=params,
    )(place, slot_ids, *[operand for operand, _ in operands])

    bc_own, local_sums = call(
        combine_kernel,
        (jax.ShapeDtypeStruct((cols, 16, 128), BF16), jax.ShapeDtypeStruct((72, 256), F32)),
        parts,
    )
    bc_new = exchange(bc_own, "col")
    mixed = pl.pallas_call(
        mixer_kernel,
        out_shape=jax.ShapeDtypeStruct((cols, 4, 256), BF16),
        scratch_shapes=[pltpu.VMEM((512, 64), BF16)],
        compiler_params=params,
    )(local_sums, bc_new, pack, state)

    mixed = exchange(mixed, "col")
    heads = call(
        scale_heads_kernel, jax.ShapeDtypeStruct((rows, 4, cols * 128), BF16), mixed
    )
    heads = exchange(heads, "row")
    residual = lax.dynamic_slice(
        hidden.reshape(8, 64, 256), (0, 4 * col_index, 0), (8, 4, 256)
    ).reshape(32, 256)
    after = pl.pallas_call(
        out_kernel,
        grid=(G,),
        out_shape=jax.ShapeDtypeStruct((cols, 32, 256), BF16),
        in_specs=[
            pl.BlockSpec(heads.shape, lambda group: (0, 0, 0)),
            pl.BlockSpec((cols, 1, 128, 256), lambda group: (0, group, 0, 0)),
            pl.BlockSpec((32, 256), lambda group: (0, 0)),
        ],
        out_specs=pl.BlockSpec((cols, 32, 256), lambda group: (0, 0, 0)),
        scratch_shapes=[pltpu.VMEM((32, 2048), F32), pltpu.VMEM((32, 256), F32)],
        compiler_params=params,
    )(heads, out_weights, residual)
    after = exchange(after, "col")

    def up_half(flip):
        return pl.pallas_call(
            functools.partial(up_kernel, flip),
            out_shape=jax.ShapeDtypeStruct((16, 16, 2176), BF16),
            in_specs=[smem, vmem, vmem, vmem],
            out_specs=vmem,
            compiler_params=params,
        )(parity, after, norm_ffn[None, :], ffn_up)

    up_other = lax.ppermute(up_half(True), "row", swap)
    up_sum = (up_half(False).astype(F32) + up_other.astype(F32)).astype(BF16)
    up_parts = exchange(up_sum, "row", halves)
    act = call(act_kernel, jax.ShapeDtypeStruct((16, 16, 2048), BF16), up_parts)
    act_mine = exchange(act, "row", halves)
    act_other = lax.ppermute(act_mine, "row", swap)
    turn = [pltpu.VMEM((8, 32, 256), F32)]
    down_mine = pl.pallas_call(
        down_mine_kernel,
        out_shape=jax.ShapeDtypeStruct((8, 32, 256), BF16),
        scratch_shapes=turn,
        compiler_params=params,
    )(act_mine, ffn_down)
    down = pl.pallas_call(
        down_other_kernel,
        out_shape=jax.ShapeDtypeStruct((cols, 32, 256), BF16),
        in_specs=[smem, vmem, vmem, vmem],
        out_specs=vmem,
        scratch_shapes=turn,
        compiler_params=params,
    )(parity, act_other, ffn_down, down_mine)
    ffn_out = jnp.sum(exchange(down, "col").astype(F32), axis=0)
    own_after = lax.dynamic_slice(
        after, (8 * (col_index % 2), 4 * (col_index // 2), 0), (8, 4, 256)
    ).reshape(32, 256)
    return (own_after.astype(F32) + ffn_out).astype(BF16)


def solution(mesh):
    return jax.shard_map(
        local,
        mesh=mesh,
        in_specs=(
            P("col", "row"),
            P("row"),
            P("row", None, "col", None),
            P("row", None, "col"),
            P("row", None, "col"),
            P(None, "col"),
            P(None, "col"),
            P(None, "col"),
            P(None, None, "col"),
            P(),
            P("row", None, None, "col"),
            P("row", None, None, None),
            P("row", None, "col", None, None),
            P(),
            P(),
            P(),
            P(None, "col"),
            P(None, "col", "row"),
            P("row"),
            P("row", "col"),
            P("col", "row"),
        ),
        out_specs=P("col", "row"),
        check_vma=False,
    )
```

time: 290 us -> 237 us (0.82)
  blocking collectives: 152 us -> 84.7 us
  waiting for transfers between devices: 55.2 us -> 81.9 us
  local copies, waits for them, and re-layouts: 12.9 us -> 4.5 us
  Pallas kernels: 4.59 us -> 10.7 us
  matrix products: 5.21 us -> 0 us
  other arithmetic: 4.2 us -> 1.1 us
    all_gather x3 -> x0, blocking collectives: 84.2 us -> none  [the longest x1 30.5 us: local(): bc_new = lax.all_gather(bc_own, 'col', axis=0, tiled=False)]
    all_to_all x5, waiting for transfers between devices: 54.5 us -> 76.8 us  [exchange(): lax.all_to_all(parts, axis, 0, 0, tiled=True, axis_index_groups=groups)]
    all_to_all x2 -> x4, blocking collectives: 67.5 us -> 84.7 us  [exchange(): lax.all_to_all(parts, axis, 0, 0, tiled=True, axis_index_groups=groups)]
    pallas_call x1 -> x7, Pallas kernels: 1.69 us -> 7.71 us  [the longest x1 2.2 us: local(): pl.pallas_call(prepare_kernel, grid_spec=pltpu.PrefetchScalarGridSpec(num...]
    dot_general x3 -> x0, matrix products: 5.21 us -> none  [the longest x1 3.08 us: local(): jnp.einsum('qgtck,cgkd->qtd', heads, out_weights, preferred_element_type=...]
    ppermute x0 -> x2, waiting for transfers between devices: none -> 4.41 us  [the longest x1 2.27 us: local(): up_other = lax.ppermute(up_half(True), 'row', swap)]
    all_to_all x5, starting transfers between devices: 39.7 us -> 35.8 us  [exchange(): lax.all_to_all(parts, axis, 0, 0, tiled=True, axis_index_groups=groups)]
    ppermute x0 -> x2, starting transfers between devices: none -> 3.83 us  [the longest x1 1.92 us: local(): up_other = lax.ppermute(up_half(True), 'row', swap)]
  transfers between devices with their start and end apart: 6 -> 8, of which waited for: 4 -> 7; matrix products, arithmetic and copies ran while one was open for 3% -> 1% of each run, Pallas kernels for 2% -> 3%
where the time goes in v4:
time: 237 us; the launch traced here: 236 us
  blocking collectives  84.7 us (36%)
  waiting for transfers between devices  81.9 us (35%)
  starting transfers between devices  39.6 us (17%)
  between operations  13.7 us (6%)
  Pallas kernels  10.7 us (5%)
  local copies, waits for them, and re-layouts  4.5 us (2%)
    all_to_all x4, blocking collectives, exchange(): lax.all_to_all(parts, axis, 0, 0, tiled=True, axis_index_groups=groups)  84.7 us
    all_to_all x5, waiting for transfers between devices, exchange(): lax.all_to_all(parts, axis, 0, 0, tiled=True, axis_index_groups=groups)  76.8 us
    all_to_all x5, starting transfers between devices, exchange(): lax.all_to_all(parts, axis, 0, 0, tiled=True, axis_index_groups=groups)  35.8 us
  transfers between devices with their start and end apart: 8, of which 7 were waited for; matrix products, arithmetic and copies ran while one was open for 1% of the time, Pallas kernels for 3%

profile of v4, /device:TPU:32, one launch (start us, length us, event | category | flops | bytes accessed | tf_op | source)
XLA Modules:
  0.0 236.3 jit_solution(3576377507552002609)
XLA Ops:
  6.5 0.0 all-gather.3.cloned.1.call-start
  6.6 0.7 all-gather.3.cloned.1.call-update
  7.3 1.4 broadcast_in_dim.19
  8.7 15.2 %all-to-all-start = ((bf16[16,32,256]{2,1,0:T(8,128)(2,1)}), bf16[16,32,256]{2,1,0:T(8,128)(2,1)S(1)}, u32[]{:S(2)}, u32[]{:S(2)}) async-start(bf16[16,32,256]{2,1,0:T(8,128)(2,1)} %broadcast_in_dim.19), calls=%async_computation | async-start | bytes 524288 | tf_op jit(solution)/shard_map/all_to_all | solution.py:24
  23.9 0.4 reshape.23.main_ref
  24.3 0.1 pad.4.clone
  24.4 0.1 maximum_maximum_fusion
  24.5 18.4 %all-to-all-done = bf16[16,32,256]{2,1,0:T(8,128)(2,1)S(1)} async-done(((bf16[16,32,256]{2,1,0:T(8,128)(2,1)}), bf16[16,32,256]{2,1,0:T(8,128)(2,1)S(1)}, u32[]{:S(2)}, u32[]{:S(2)}) %all-to-all-start) | async-done | bytes 262176 | tf_op jit(solution)/shard_map/all_to_all | solution.py:24
  42.9 0.8 shard_map.199
  43.8 27.3 %all_to_all.45.parts_ref = bf16[32,80,256]{2,1,0:T(8,128)(2,1)S(1)} all-to-all(bf16[32,80,256]{2,1,0:T(8,128)(2,1)S(1)} %bitcast.12), channel_id=1, replica_groups=mesh['row'=32,'col'=16] {'row'}, dimensions={0} | all-to-all | bytes 2621440 | tf_op jit(solution)/shard_map/all_to_all | solution.py:24
  71.0 0.0 copy-start.19
  71.1 0.0 copy-start.4
  71.1 0.0 copy-start.5
  71.1 0.0 copy-start.8
  71.1 0.0 copy-start.9
  71.1 0.8 shard_map.200
  71.9 6.7 %all-to-all-start.2 = ((bf16[16,16,128]{2,1,0:T(8,128)(2,1)}), bf16[16,16,128]{2,1,0:T(8,128)(2,1)S(1)}, u32[]{:S(2)}, u32[]{:S(2)}) async-start(bf16[16,16,128]{2,1,0:T(8,128)(2,1)} %get-tuple-element.10), calls=%async_computation.2 | async-start | bytes 131072 | tf_op jit(solution)/shard_map/all_to_all | solution.py:24
  78.7 0.1 copy.29.offset_ref
  78.8 0.1 copy.30.rate_ref
  78.9 0.1 copy.31.skip_ref
  79.0 0.1 pad_add_fusion.place_ref
  79.1 2.2 shard_map.201
  81.3 9.7 %all-to-all-done.2.bc_new_ref = bf16[16,16,128]{2,1,0:T(8,128)(2,1)S(1)} async-done(((bf16[16,16,128]{2,1,0:T(8,128)(2,1)}), bf16[16,16,128]{2,1,0:T(8,128)(2,1)S(1)}, u32[]{:S(2)}, u32[]{:S(2)}) %all-to-all-start.2) | async-done | bytes 65568 | tf_op jit(solution)/shard_map/all_to_all | solution.py:24
  91.0 0.8 shard_map.202
  91.9 15.9 %all_to_all.46.parts_ref = bf16[16,4,256]{2,1,0:T(4,128)(2,1)S(1)} all-to-all(bf16[16,4,256]{2,1,0:T(4,128)(2,1)S(1)} %shard_map.202), channel_id=1, replica_groups=mesh['row'=32,'col'=16] {'col'}, dimensions={0} | all-to-all | bytes 65536 | tf_op jit(solution)/shard_map/all_to_all | solution.py:24
  107.7 1.1 shard_map.203
  108.8 3.9 %all-to-all-start.4 = ((bf16[32,4,2048]{2,1,0:T(4,128)(2,1)}), bf16[32,4,2048]{2,1,0:T(4,128)(2,1)S(1)}, u32[]{:S(2)}, u32[]{:S(2)}) async-start(bf16[32,4,2048]{2,1,0:T(4,128)(2,1)} %shard_map.203), calls=%async_computation.4 | async-start | bytes 1048576 | tf_op jit(solution)/shard_map/all_to_all | solution.py:24
  112.7 11.7 %all-to-all-done.4.heads_ref = bf16[32,4,2048]{2,1,0:T(4,128)(2,1)S(1)} async-done(((bf16[32,4,2048]{2,1,0:T(4,128)(2,1)}), bf16[32,4,2048]{2,1,0:T(4,128)(2,1)S(1)}, u32[]{:S(2)}, u32[]{:S(2)}) %all-to-all-start.4) | async-done | bytes 524320 | tf_op jit(solution)/shard_map/all_to_all | solution.py:24
  124.5 2.2 copy-done.1
  126.6 2.2 shard_map.204
  128.8 4.5 %all-to-all-start.5 = ((bf16[16,32,256]{2,1,0:T(8,128)(2,1)}), bf16[16,32,256]{2,1,0:T(8,128)(2,1)S(1)}, u32[]{:S(2)}, u32[]{:S(2)}) async-start(bf16[16,32,256]{2,1,0:T(8,128)(2,1)} %shard_map.204), calls=%async_computation.5 | async-start | bytes 524288 | tf_op jit(solution)/shard_map/all_to_all | solution.py:24
  133.3 18.7 %all-to-all-done.5.after_ref = bf16[16,32,256]{2,1,0:T(8,128)(2,1)S(1)} async-done(((bf16[16,32,256]{2,1,0:T(8,128)(2,1)}), bf16[16,32,256]{2,1,0:T(8,128)(2,1)S(1)}, u32[]{:S(2)}, u32[]{:S(2)}) %all-to-all-start.5) | async-done | bytes 262176 | tf_op jit(solution)/shard_map/all_to_all | solution.py:24
  152.0 0.4 shard_map.206
  152.5 1.9 collective-permute-start
  154.4 0.4 shard_map.205
  154.9 2.3 collective-permute-done
  157.1 0.3 add_convert_fusion
  157.4 21.9 %all_to_all.47.parts_ref = bf16[16,16,2176]{2,1,0:T(8,128)(2,1)S(1)} all-to-all(bf16[16,16,2176]{2,1,0:T(8,128)(2,1)S(1)} %add_convert_fusion), channel_id=1, replica_groups={{0,32,64,96,128,160,192,224,256,288,320,352,384,416,448,480},{16,48,80,..., dimensions={0} | all-to-all | bytes 2228224 | tf_op jit(solution)/shard_map/all_to_all | solution.py:24
  179.3 0.3 shard_map.207
  179.6 0.0 copy-start.2
  179.6 19.8 %all_to_all.48.act_ref = bf16[16,16,2048]{2,1,0:T(8,128)(2,1)S(1)} all-to-all(bf16[16,16,2048]{2,1,0:T(8,128)(2,1)S(1)} %shard_map.207), channel_id=1, replica_groups={{0,32,64,96,128,160,192,224,256,288,320,352,384,416,448,480},{16,48,80,..., dimensions={0} | all-to-all | bytes 2097152 | tf_op jit(solution)/shard_map/all_to_all | solution.py:24
  199.3 1.9 collective-permute-start.1
  201.2 0.5 shard_map.208.mine_ref
  201.7 2.1 collective-permute-done.1.act_ref
  203.9 1.2 shard_map.209
  205.0 5.4 %all-to-all-start.8 = ((bf16[16,32,256]{2,1,0:T(8,128)(2,1)}), bf16[16,32,256]{2,1,0:T(8,128)(2,1)S(1)}, u32[]{:S(2)}, u32[]{:S(2)}) async-start(bf16[16,32,256]{2,1,0:T(8,128)(2,1)} %shard_map.209), calls=%async_computation.8 | async-start | bytes 524288 | tf_op jit(solution)/shard_map/all_to_all | solution.py:24
  210.5 18.3 %all-to-all-done.8 = bf16[16,32,256]{2,1,0:T(8,128)(2,1)S(1)} async-done(((bf16[16,32,256]{2,1,0:T(8,128)(2,1)}), bf16[16,32,256]{2,1,0:T(8,128)(2,1)S(1)}, u32[]{:S(2)}, u32[]{:S(2)}) %all-to-all-start.8) | async-done | bytes 262176 | tf_op jit(solution)/shard_map/all_to_all | solution.py:24
  228.8 0.6 add_convert_fusion.1
  (42 shorter events, 0.2 us)
Async XLA Ops:
  6.5 17.4 %copy-start.12 = (bf16[256,4,2,128]{3,2,1,0:T(2,128)(2,1)S(1)}, bf16[256,4,2,128]{3,2,1,0:T(2,128)(2,1)}, u32[]{:S(2)}) copy-start(bf16[256,4,2,128]{3,2,1,0:T(2,128)(2,1)} %param.23) | copy-start | bytes 1572868
  6.5 17.8 %copy-start.13 = (bf16[256,4,32]{0,2,1:T(8,128)(2,1)S(1)}, bf16[256,4,32]{0,2,1:T(8,128)(2,1)}, u32[]{:S(2)}) copy-start(bf16[256,4,32]{0,2,1:T(8,128)(2,1)} %param.24) | copy-start | bytes 196612
  6.5 17.8 %copy-start.15 = (bf16[256,4,2]{0,2,1:T(2,128)(2,1)S(1)}, bf16[256,4,2]{0,2,1:T(2,128)(2,1)}, u32[]{:S(2)}) copy-start(bf16[256,4,2]{0,2,1:T(2,128)(2,1)} %param.25) | copy-start | bytes 12292
  6.5 36.4 %copy-start.10 = (f32[256]{0:T(256)S(1)}, f32[256]{0:T(256)}, u32[]{:S(2)}) copy-start(f32[256]{0:T(256)} %param.22) | copy-start | bytes 3076
  6.5 117.9 %all-gather.3.cloned.1.call-start = ((), (), s32[]{:S(2)}) async-start(), calls=%async_computation.9 | async-start | bytes 4456448 | tf_op jit(solution)/shard_map/all_gather | solution.py:370
  8.7 34.2 %all-to-all-start = ((bf16[16,32,256]{2,1,0:T(8,128)(2,1)}), bf16[16,32,256]{2,1,0:T(8,128)(2,1)S(1)}, u32[]{:S(2)}, u32[]{:S(2)}) async-start(bf16[16,32,256]{2,1,0:T(8,128)(2,1)} %broadcast_in_dim.19), calls=%async_computation | async-start | bytes 524288 | tf_op jit(solution)/shard_map/all_to_all | solution.py:24
  71.0 7.6 %copy-start.14 = (bf16[1,4,3,512]{3,1,2,0:T(4,128)(2,1)S(1)}, bf16[1,4,3,512]{3,1,2,0:T(4,128)(2,1)}, u32[]{:S(2)}) copy-start(bf16[1,4,3,512]{3,1,2,0:T(4,128)(2,1)} %param.32) | copy-start | bytes 36868
  71.0 7.7 %copy-start.16 = (bf16[1,4,3,128]{3,1,2,0:T(4,128)(2,1)S(1)}, bf16[1,4,3,128]{3,1,2,0:T(4,128)(2,1)}, u32[]{:S(2)}) copy-start(bf16[1,4,3,128]{3,1,2,0:T(4,128)(2,1)} %param.31) | copy-start | bytes 9220
  71.0 7.7 %copy-start.17 = (f32[4,2]{0,1:T(2,128)S(1)}, f32[4,2]{0,1:T(2,128)}, u32[]{:S(2)}) copy-start(f32[4,2]{0,1:T(2,128)} %param.26) | copy-start | bytes 100
  71.0 7.8 %copy-start.18 = (f32[4,2]{0,1:T(2,128)S(1)}, f32[4,2]{0,1:T(2,128)}, u32[]{:S(2)}) copy-start(f32[4,2]{0,1:T(2,128)} %param.27) | copy-start | bytes 100
  71.0 7.9 %copy-start.19 = (f32[4,2]{0,1:T(2,128)S(1)}, f32[4,2]{0,1:T(2,128)}, u32[]{:S(2)}) copy-start(f32[4,2]{0,1:T(2,128)} %param.28) | copy-start | bytes 100
  71.1 8.0 %copy-start.3 = (f32[1,4,2,64,256]{4,3,2,1,0:T(8,128)S(1)}, f32[1,4,2,64,256]{4,3,2,1,0:T(8,128)}, u32[]{:S(2)}) copy-start(f32[1,4,2,64,256]{4,3,2,1,0:T(8,128)} %state_ref.1) | copy-start | bytes 1572868
  71.1 8.0 %copy-start.4 = (s32[8,64,64]{2,1,0:T(8,128)S(1)}, s32[8,64,64]{2,1,0:T(8,128)}, u32[]{:S(2)}) copy-start(s32[8,64,64]{2,1,0:T(8,128)} %anc_ref.1) | copy-start | bytes 393220
  71.1 8.0 %copy-start.5 = (bf16[4,4,512]{2,1,0:T(4,128)(2,1)S(1)}, bf16[4,4,512]{2,1,0:T(4,128)(2,1)}, u32[]{:S(2)}) copy-start(bf16[4,4,512]{2,1,0:T(4,128)(2,1)} %bc_taps_ref.1) | copy-start | bytes 49156
  71.1 8.0 %copy-start.7 = (bf16[4,4,128]{2,1,0:T(4,128)(2,1)S(1)}, bf16[4,4,128]{2,1,0:T(4,128)(2,1)}, u32[]{:S(2)}) copy-start(bf16[4,4,128]{2,1,0:T(4,128)(2,1)} %x_taps_ref.1) | copy-start | bytes 12292
  71.1 8.0 %copy-start.8 = (s32[8,64]{1,0:T(8,128)S(1)}, s32[8,64]{1,0:T(8,128)}, u32[]{:S(2)}) copy-start(s32[8,64]{1,0:T(8,128)} %parents_ref.1) | copy-start | bytes 6148
  71.1 8.0 %copy-start.9 = (f32[4,128]{1,0:T(4,128)S(1)}, f32[4,128]{1,0:T(4,128)}, u32[]{:S(2)}) copy-start(f32[4,128]{1,0:T(4,128)} %gain_ref.1) | copy-start | bytes 6148
  71.1 8.0 %copy-start.11 = (s32[8]{0:T(128)S(1)}, s32[8]{0:T(128)}, u32[]{:S(2)}) copy-start(s32[8]{0:T(128)} %slot_ref.1) | copy-start | bytes 100
  71.9 19.1 %all-to-all-start.2 = ((bf16[16,16,128]{2,1,0:T(8,128)(2,1)}), bf16[16,16,128]{2,1,0:T(8,128)(2,1)S(1)}, u32[]{:S(2)}, u32[]{:S(2)}) async-start(bf16[16,16,128]{2,1,0:T(8,128)(2,1)} %get-tuple-element.10), calls=%async_computation.2 | async-start | bytes 131072 | tf_op jit(solution)/shard_map/all_to_all | solution.py:24
  108.8 15.7 %all-to-all-start.4 = ((bf16[32,4,2048]{2,1,0:T(4,128)(2,1)}), bf16[32,4,2048]{2,1,0:T(4,128)(2,1)S(1)}, u32[]{:S(2)}, u32[]{:S(2)}) async-start(bf16[32,4,2048]{2,1,0:T(4,128)(2,1)} %shard_map.203), calls=%async_computation.4 | async-start | bytes 1048576 | tf_op jit(solution)/shard_map/all_to_all | solution.py:24
  124.5 2.2 copy-start.1
  126.6 25.4 %copy-start = (bf16[256,2048]{1,0:T(8,128)(2,1)S(1)}, bf16[256,2048]{1,0:T(8,128)(2,1)}, u32[]{:S(2)}) copy-start(bf16[256,2048]{1,0:T(8,128)(2,1)} %weight_ref.5) | copy-start | bytes 3145732
  126.6 25.4 %copy-start.6 = (f32[256]{0:T(256)S(1)}, f32[256]{0:T(256)}, u32[]{:S(2)}) copy-start(f32[256]{0:T(256)} %param.39) | copy-start | bytes 3076
  128.8 23.2 %all-to-all-start.5 = ((bf16[16,32,256]{2,1,0:T(8,128)(2,1)}), bf16[16,32,256]{2,1,0:T(8,128)(2,1)S(1)}, u32[]{:S(2)}, u32[]{:S(2)}) async-start(bf16[16,32,256]{2,1,0:T(8,128)(2,1)} %shard_map.204), calls=%async_computation.5 | async-start | bytes 524288 | tf_op jit(solution)/shard_map/all_to_all | solution.py:24
  152.5 4.6 %collective-permute-start = (bf16[16,16,2176]{2,1,0:T(8,128)(2,1)S(1)}, bf16[16,16,2176]{2,1,0:T(8,128)(2,1)S(1)}, u32[]{:S(2)}, u32[]{:S(2)}) collective-permute-start(bf16[16,16,2176]{2,1,0:T(8,128)(2,1)S(1)} %shard_map.206), channel_id=1, source_target_pairs={{0,16},{16,0},{32,48},{48,32},{64,80},{80,64},{96,112},{112,96},{1... | collective-permute-start | bytes 3342344 | tf_op jit(solution)/shard_map/ppermute | solution.py:468
  179.6 21.7 %copy-start.2 = (bf16[2048,256]{1,0:T(8,128)(2,1)S(1)}, bf16[2048,256]{1,0:T(8,128)(2,1)}, u32[]{:S(2)}) copy-start(bf16[2048,256]{1,0:T(8,128)(2,1)} %weight_ref.7) | copy-start | bytes 3145732
  199.3 4.5 %collective-permute-start.1 = (bf16[16,16,2048]{2,1,0:T(8,128)(2,1)S(1)}, bf16[16,16,2048]{2,1,0:T(8,128)(2,1)S(1)}, u32[]{:S(2)}, u32[]{:S(2)}) collective-permute-start(bf16[16,16,2048]{2,1,0:T(8,128)(2,1)S(1)} %all_to_all.48.act_ref), channel_id=1, source_target_pairs={{0,16},{16,0},{32,48},{48,32},{64,80},{80,64},{96,112},{112,96},{1... | collective-permute-start | bytes 3145736 | tf_op jit(solution)/shard_map/ppermute | solution.py:473
  205.0 23.8 %all-to-all-start.8 = ((bf16[16,32,256]{2,1,0:T(8,128)(2,1)}), bf16[16,32,256]{2,1,0:T(8,128)(2,1)S(1)}, u32[]{:S(2)}, u32[]{:S(2)}) async-start(bf16[16,32,256]{2,1,0:T(8,128)(2,1)} %shard_map.209), calls=%async_computation.8 | async-start | bytes 524288 | tf_op jit(solution)/shard_map/all_to_all | solution.py:24
Sparse Core Ops, SparseCore 0:
  9.5 88.5 all-gather.2

commit v5 on v4

--- a/solution.py
+++ b/solution.py
@@ -32,24 +32,30 @@
     )(*operands)
 
 
-def project_kernel(hidden_ref, gain_ref, main_ref, side_ref, out_ref):
+def copies_kernel(block_ref, out_ref):
+    for part in range(out_ref.shape[0]):
+        out_ref[part] = block_ref[...]
+
+
+def project_kernel(flip, parity_ref, hidden_ref, gain_ref, main_ref, side_ref, out_ref):
+    use = parity_ref[0] if not flip else 1 - parity_ref[0]
     hidden = hidden_ref[...].astype(F32)
     normed = (hidden * gain_ref[...]).astype(BF16)
     squares = (hidden * hidden).astype(BF16)
     ones = jnp.ones((16, hidden.shape[1]), BF16)
     stat = lax.dot_general(ones, squares, NT, preferred_element_type=F32)
-    for group in range(G):
-        main = jnp.dot(
-            normed, main_ref[:, group * 256 : (group + 1) * 256], preferred_element_type=F32
-        ).astype(BF16)
-        side = lax.dot_general(
-            side_ref[group * 64 : (group + 1) * 64, :], normed, NT, preferred_element_type=F32
-        )
+    for half in range(G // 2):
+        group = 2 * half + use
+        main = main_ref[:, pl.ds(pl.multiple_of(group * 256, 256), 256)]
+        main = jnp.dot(normed, main, preferred_element_type=F32).astype(BF16)
+        side = side_ref[pl.ds(pl.multiple_of(group * 64, 64), 64), :]
+        side = lax.dot_general(side, normed, NT, preferred_element_type=F32)
         for request in range(8):
+            part = request * (G // 2) + half
             nodes = slice(request * 64, (request + 1) * 64)
-            out_ref[request, group, 0:64, :] = main[nodes, :]
+            out_ref[part, 0:64, :] = main[nodes, :]
             pieces = [side[0:16, nodes], side[16:32, nodes], side[32:48, nodes], stat[:, nodes]]
-            out_ref[request, group, 64:80, :] = jnp.concatenate(pieces, axis=1).astype(BF16)
+            out_ref[part, 64:80, :] = jnp.concatenate(pieces, axis=1).astype(BF16)
 
 
 def column_of(row, size):
@@ -369,17 +375,33 @@
 
     out_weights = lax.all_gather(out_proj, "col", axis=0, tiled=False)
 
-    hidden = exchange(jnp.broadcast_to(hidden_in[None], (cols,) + hidden_in.shape), "col")
+    copies = call(copies_kernel, jax.ShapeDtypeStruct((cols, 32, 256), BF16), hidden_in)
+    hidden = exchange(copies, "col")
     side = jnp.concatenate([bc_proj, dt_proj, jnp.zeros((256, G, 30), BF16)], axis=2)
-    parts = call(
-        project_kernel,
-        jax.ShapeDtypeStruct((rows // G, G, 80, 256), BF16),
-        hidden.reshape(512, 256),
-        norm_mixer[None, :],
-        mixer_in.reshape(256, -1),
-        side.reshape(256, 256).T,
-    )
-    parts = exchange(parts.reshape(rows, 80, 256), "row")
+    side = side.reshape(256, 256).T
+    main = mixer_in.reshape(256, -1)
+
+    def pair_sum(half):
+        other = lax.ppermute(half(True), "row", swap)
+        return (half(False).astype(F32) + other.astype(F32)).astype(BF16)
+
+    def project_half(flip):
+        return pl.pallas_call(
+            functools.partial(project_kernel, flip),
+            out_shape=jax.ShapeDtypeStruct((16, 80, 256), BF16),
+            in_specs=[smem, vmem, vmem, vmem, vmem],
+            out_specs=vmem,
+            compiler_params=params,
+        )(parity, hidden.reshape(512, 256), norm_mixer[None, :], main, side)
+
+    parts = exchange(pair_sum(project_half), "row", halves)
+
+    bc_own, local_sums = call(
+        combine_kernel,
+        (jax.ShapeDtypeStruct((cols, 16, 128), BF16), jax.ShapeDtypeStruct((72, 256), F32)),
+        parts,
+    )
+    bc_own, place = lax.optimization_barrier((bc_own, place))
 
     def whole(array):
         shape = array.shape
@@ -420,11 +442,6 @@
         compiler_params=params,
     )(place, slot_ids, *[operand for operand, _ in operands])
 
-    bc_own, local_sums = call(
-        combine_kernel,
-        (jax.ShapeDtypeStruct((cols, 16, 128), BF16), jax.ShapeDtypeStruct((72, 256), F32)),
-        parts,
-    )
     bc_new = exchange(bc_own, "col")
     mixed = pl.pallas_call(
         mixer_kernel,
@@ -452,7 +469,7 @@
         ],
         out_specs=pl.BlockSpec((cols, 32, 256), lambda group: (0, 0, 0)),
         scratch_shapes=[pltpu.VMEM((32, 2048), F32), pltpu.VMEM((32, 256), F32)],
-        compiler_params=params,
+        compiler_params=pltpu.CompilerParams(vmem_limit_bytes=60 * 1024 * 1024),
     )(heads, out_weights, residual)
     after = exchange(after, "col")
 
@@ -465,9 +482,7 @@
             compiler_params=params,
         )(parity, after, norm_ffn[None, :], ffn_up)
 
-    up_other = lax.ppermute(up_half(True), "row", swap)
-    up_sum = (up_half(False).astype(F32) + up_other.astype(F32)).astype(BF16)
-    up_parts = exchange(up_sum, "row", halves)
+    up_parts = exchange(pair_sum(up_half), "row", halves)
     act = call(act_kernel, jax.ShapeDtypeStruct((16, 16, 2048), BF16), up_parts)
     act_mine = exchange(act, "row", halves)
     act_other = lax.ppermute(act_mine, "row", swap)

time: 237 us -> 235 us (level)
  waiting for transfers between devices: 81.9 us -> 77.3 us
  starting transfers between devices: 39.6 us -> 44.2 us
  blocking collectives: 84.7 us -> 80.3 us
  Pallas kernels: 10.7 us -> 13.8 us
    all_to_all x5, waiting for transfers between devices: 76.8 us -> 70.7 us  [exchange(): lax.all_to_all(parts, axis, 0, 0, tiled=True, axis_index_groups=groups)]
    all_to_all x4, blocking collectives: 84.7 us -> 80.3 us  [exchange(): lax.all_to_all(parts, axis, 0, 0, tiled=True, axis_index_groups=groups)]
    all_to_all x5, starting transfers between devices: 35.8 us -> 38.5 us  [exchange(): lax.all_to_all(parts, axis, 0, 0, tiled=True, axis_index_groups=groups)]
  transfers between devices with their start and end apart: 8 -> 9, of which waited for: 7 -> 8; matrix products, arithmetic and copies ran while one was open for 1% -> 1% of each run, Pallas kernels for 3% -> 3%
where the time goes in v5:
time: 235 us
  blocking collectives  80.3 us (34%)
  waiting for transfers between devices  77.3 us (33%)
  starting transfers between devices  44.2 us (19%)
  Pallas kernels  13.8 us (6%)
  between operations  13.7 us (6%)
  local copies, waits for them, and re-layouts  3 us (1%)
    all_to_all x4, blocking collectives, exchange(): lax.all_to_all(parts, axis, 0, 0, tiled=True, axis_index_groups=groups)  80.3 us
    all_to_all x5, waiting for transfers between devices, exchange(): lax.all_to_all(parts, axis, 0, 0, tiled=True, axis_index_groups=groups)  70.7 us
    all_to_all x5, starting transfers between devices, exchange(): lax.all_to_all(parts, axis, 0, 0, tiled=True, axis_index_groups=groups)  38.5 us
  transfers between devices with their start and end apart: 9, of which 8 were waited for; matrix products, arithmetic and copies ran while one was open for 1% of the time, Pallas kernels for 3%

profile of v5, /device:TPU:32, one launch (start us, length us, event | category | flops | bytes accessed | tf_op | source)
XLA Modules:
  0.0 234.5 jit_solution(12621657681641853819)
XLA Ops:
  6.5 0.7 all-gather.3.cloned.1.call-update
  7.3 0.7 copy-done.4
  8.0 0.7 shard_map.199
  8.7 15.2 %all-to-all-start = ((bf16[16,32,256]{2,1,0:T(8,128)(2,1)}), bf16[16,32,256]{2,1,0:T(8,128)(2,1)S(1)}, u32[]{:S(2)}, u32[]{:S(2)}) async-start(bf16[16,32,256]{2,1,0:T(8,128)(2,1)} %shard_map.199), calls=%async_computation | async-start | bytes 524288 | tf_op jit(solution)/shard_map/all_to_all | solution.py:24
  23.9 0.4 reshape.20.main_ref
  24.3 0.1 pad.4.clone
  24.4 0.1 maximum_maximum_fusion
  24.5 18.4 %all-to-all-done = bf16[16,32,256]{2,1,0:T(8,128)(2,1)S(1)} async-done(((bf16[16,32,256]{2,1,0:T(8,128)(2,1)}), bf16[16,32,256]{2,1,0:T(8,128)(2,1)S(1)}, u32[]{:S(2)}, u32[]{:S(2)}) %all-to-all-start) | async-done | bytes 262176 | tf_op jit(solution)/shard_map/all_to_all | solution.py:24
  42.9 0.6 shard_map.201
  43.5 1.9 collective-permute-start
  45.4 0.6 shard_map.200
  46.0 1.5 collective-permute-done
  47.5 1.0 add_convert_fusion.1
  48.5 0.0 copy-start.2
  48.6 7.2 %all-to-all-start.1 = ((bf16[16,80,256]{2,1,0:T(8,128)(2,1)}), bf16[16,80,256]{2,1,0:T(8,128)(2,1)S(1)}, u32[]{:S(2)}, u32[]{:S(2)}) async-start(bf16[16,80,256]{2,1,0:T(8,128)(2,1)} %add_convert_fusion.1), calls=%async_computation.1 | async-start | bytes 1310720 | tf_op jit(solution)/shard_map/all_to_all | solution.py:24
  55.8 0.1 pad_add_fusion.place_ref
  55.9 13.1 %all-to-all-done.1.parts_ref = bf16[16,80,256]{2,1,0:T(8,128)(2,1)S(1)} async-done(((bf16[16,80,256]{2,1,0:T(8,128)(2,1)}), bf16[16,80,256]{2,1,0:T(8,128)(2,1)S(1)}, u32[]{:S(2)}, u32[]{:S(2)}) %all-to-all-start.1) | async-done | bytes 655392 | tf_op jit(solution)/shard_map/all_to_all | solution.py:24
  69.1 0.7 shard_map.202
  69.8 6.7 %all-to-all-start.2 = ((bf16[16,16,128]{2,1,0:T(8,128)(2,1)}), bf16[16,16,128]{2,1,0:T(8,128)(2,1)S(1)}, u32[]{:S(2)}, u32[]{:S(2)}) async-start(bf16[16,16,128]{2,1,0:T(8,128)(2,1)} %get-tuple-element.13), calls=%async_computation.2 | async-start | bytes 131072 | tf_op jit(solution)/shard_map/all_to_all | solution.py:24
  76.6 0.1 copy.29.offset_ref
  76.7 0.1 copy.30.rate_ref
  76.8 0.1 copy.31.skip_ref
  76.9 2.2 shard_map.203
  79.1 9.7 %all-to-all-done.2.bc_new_ref = bf16[16,16,128]{2,1,0:T(8,128)(2,1)S(1)} async-done(((bf16[16,16,128]{2,1,0:T(8,128)(2,1)}), bf16[16,16,128]{2,1,0:T(8,128)(2,1)S(1)}, u32[]{:S(2)}, u32[]{:S(2)}) %all-to-all-start.2) | async-done | bytes 65568 | tf_op jit(solution)/shard_map/all_to_all | solution.py:24
  88.8 0.8 shard_map.204
  89.7 15.4 %all_to_all.45.parts_ref = bf16[16,4,256]{2,1,0:T(4,128)(2,1)S(1)} all-to-all(bf16[16,4,256]{2,1,0:T(4,128)(2,1)S(1)} %shard_map.204), channel_id=1, replica_groups=mesh['row'=32,'col'=16] {'col'}, dimensions={0} | all-to-all | bytes 65536 | tf_op jit(solution)/shard_map/all_to_all | solution.py:24
  105.1 1.1 shard_map.205
  106.2 3.9 %all-to-all-start.4 = ((bf16[32,4,2048]{2,1,0:T(4,128)(2,1)}), bf16[32,4,2048]{2,1,0:T(4,128)(2,1)S(1)}, u32[]{:S(2)}, u32[]{:S(2)}) async-start(bf16[32,4,2048]{2,1,0:T(4,128)(2,1)} %shard_map.205), calls=%async_computation.4 | async-start | bytes 1048576 | tf_op jit(solution)/shard_map/all_to_all | solution.py:24
  110.1 0.6 reshape.23.residual_ref
  110.7 11.1 %all-to-all-done.4.heads_ref = bf16[32,4,2048]{2,1,0:T(4,128)(2,1)S(1)} async-done(((bf16[32,4,2048]{2,1,0:T(4,128)(2,1)}), bf16[32,4,2048]{2,1,0:T(4,128)(2,1)S(1)}, u32[]{:S(2)}, u32[]{:S(2)}) %all-to-all-start.4) | async-done | bytes 524320 | tf_op jit(solution)/shard_map/all_to_all | solution.py:24
  121.8 0.8 copy-done.12
  122.6 4.4 %shard_map.206 = bf16[16,32,256]{2,1,0:T(8,128)(2,1)} custom-call(bf16[32,4,2048]{2,1,0:T(4,128)(2,1)} %copy-done.12, bf16[16,4,128,256]{3,2,1,0:T(8,128)(2,1)} %bitcast.20, bf16[32,256]{1,0:T(8,128)(2,1)} %reshape.23.residual_ref), custom_call_target="tpu_custom_call" | custom-call | tf_op jit(solution)/shard_map/pallas_call | solution.py:461
  127.0 23.3 %all_to_all.46.after_ref = bf16[16,32,256]{2,1,0:T(8,128)(2,1)S(1)} all-to-all(bf16[16,32,256]{2,1,0:T(8,128)(2,1)} %shard_map.206), channel_id=1, replica_groups=mesh['row'=32,'col'=16] {'col'}, dimensions={0} | all-to-all | bytes 524288 | tf_op jit(solution)/shard_map/all_to_all | solution.py:24
  150.3 0.4 shard_map.208
  150.7 1.9 collective-permute-start.1
  152.7 0.4 shard_map.207
  153.1 2.3 collective-permute-done.1
  155.4 0.3 add_convert_fusion
  155.6 21.9 %all_to_all.47.parts_ref = bf16[16,16,2176]{2,1,0:T(8,128)(2,1)S(1)} all-to-all(bf16[16,16,2176]{2,1,0:T(8,128)(2,1)S(1)} %add_convert_fusion), channel_id=1, replica_groups={{0,32,64,96,128,160,192,224,256,288,320,352,384,416,448,480},{16,48,80,..., dimensions={0} | all-to-all | bytes 2228224 | tf_op jit(solution)/shard_map/all_to_all | solution.py:24
  177.5 0.3 shard_map.209
  177.8 19.8 %all_to_all.48.act_ref = bf16[16,16,2048]{2,1,0:T(8,128)(2,1)S(1)} all-to-all(bf16[16,16,2048]{2,1,0:T(8,128)(2,1)S(1)} %shard_map.209), channel_id=1, replica_groups={{0,32,64,96,128,160,192,224,256,288,320,352,384,416,448,480},{16,48,80,..., dimensions={0} | all-to-all | bytes 2097152 | tf_op jit(solution)/shard_map/all_to_all | solution.py:24
  197.5 1.9 collective-permute-start.2
  199.5 0.5 shard_map.210.mine_ref
  199.9 2.1 collective-permute-done.2.act_ref
  202.1 1.2 shard_map.211
  203.2 5.4 %all-to-all-start.8 = ((bf16[16,32,256]{2,1,0:T(8,128)(2,1)}), bf16[16,32,256]{2,1,0:T(8,128)(2,1)S(1)}, u32[]{:S(2)}, u32[]{:S(2)}) async-start(bf16[16,32,256]{2,1,0:T(8,128)(2,1)} %shard_map.211), calls=%async_computation.8 | async-start | bytes 524288 | tf_op jit(solution)/shard_map/all_to_all | solution.py:24
  208.7 18.3 %all-to-all-done.8 = bf16[16,32,256]{2,1,0:T(8,128)(2,1)S(1)} async-done(((bf16[16,32,256]{2,1,0:T(8,128)(2,1)}), bf16[16,32,256]{2,1,0:T(8,128)(2,1)S(1)}, u32[]{:S(2)}, u32[]{:S(2)}) %all-to-all-start.8) | async-done | bytes 262176 | tf_op jit(solution)/shard_map/all_to_all | solution.py:24
  227.1 0.6 add_convert_fusion.2
  (48 shorter events, 0.2 us)
Async XLA Ops:
  6.5 17.9 %copy-start.14 = (bf16[256,4,32]{0,2,1:T(8,128)(2,1)S(1)}, bf16[256,4,32]{0,2,1:T(8,128)(2,1)}, u32[]{:S(2)}) copy-start(bf16[256,4,32]{0,2,1:T(8,128)(2,1)} %param.24) | copy-start | bytes 196612
  6.5 17.9 %copy-start.16 = (bf16[256,4,2]{0,2,1:T(2,128)(2,1)S(1)}, bf16[256,4,2]{0,2,1:T(2,128)(2,1)}, u32[]{:S(2)}) copy-start(bf16[256,4,2]{0,2,1:T(2,128)(2,1)} %param.25) | copy-start | bytes 12292
  6.5 36.4 %copy-start.9 = (f32[256]{0:T(256)S(1)}, f32[256]{0:T(256)}, u32[]{:S(2)}) copy-start(f32[256]{0:T(256)} %param.22) | copy-start | bytes 3076
  6.5 115.3 %all-gather.3.cloned.1.call-start = ((), (), s32[]{:S(2)}) async-start(), calls=%async_computation.9 | async-start | bytes 4456448 | tf_op jit(solution)/shard_map/all_gather | solution.py:376
  7.3 0.7 copy-start.4
  8.0 16.0 %copy-start.13 = (bf16[256,4,2,128]{3,2,1,0:T(2,128)(2,1)S(1)}, bf16[256,4,2,128]{3,2,1,0:T(2,128)(2,1)}, u32[]{:S(2)}) copy-start(bf16[256,4,2,128]{3,2,1,0:T(2,128)(2,1)} %param.23) | copy-start | bytes 1572868
  8.7 34.2 %all-to-all-start = ((bf16[16,32,256]{2,1,0:T(8,128)(2,1)}), bf16[16,32,256]{2,1,0:T(8,128)(2,1)S(1)}, u32[]{:S(2)}, u32[]{:S(2)}) async-start(bf16[16,32,256]{2,1,0:T(8,128)(2,1)} %shard_map.199), calls=%async_computation | async-start | bytes 524288 | tf_op jit(solution)/shard_map/all_to_all | solution.py:24
  43.5 4.0 %collective-permute-start = (bf16[16,80,256]{2,1,0:T(8,128)(2,1)S(1)}, bf16[16,80,256]{2,1,0:T(8,128)(2,1)S(1)}, u32[]{:S(2)}, u32[]{:S(2)}) collective-permute-start(bf16[16,80,256]{2,1,0:T(8,128)(2,1)S(1)} %shard_map.201), channel_id=1, source_target_pairs={{0,16},{16,0},{32,48},{48,32},{64,80},{80,64},{96,112},{112,96},{1... | collective-permute-start | bytes 1966088 | tf_op jit(solution)/shard_map/ppermute | solution.py:385
  48.5 28.0 %copy-start.15 = (bf16[1,4,3,512]{3,1,2,0:T(4,128)(2,1)S(1)}, bf16[1,4,3,512]{3,1,2,0:T(4,128)(2,1)}, u32[]{:S(2)}) copy-start(bf16[1,4,3,512]{3,1,2,0:T(4,128)(2,1)} %param.32) | copy-start | bytes 36868
  48.5 28.1 %copy-start.17 = (bf16[1,4,3,128]{3,1,2,0:T(4,128)(2,1)S(1)}, bf16[1,4,3,128]{3,1,2,0:T(4,128)(2,1)}, u32[]{:S(2)}) copy-start(bf16[1,4,3,128]{3,1,2,0:T(4,128)(2,1)} %param.31) | copy-start | bytes 9220
  48.5 28.1 %copy-start.18 = (f32[4,2]{0,1:T(2,128)S(1)}, f32[4,2]{0,1:T(2,128)}, u32[]{:S(2)}) copy-start(f32[4,2]{0,1:T(2,128)} %param.26) | copy-start | bytes 100
  48.5 28.2 %copy-start.19 = (f32[4,2]{0,1:T(2,128)S(1)}, f32[4,2]{0,1:T(2,128)}, u32[]{:S(2)}) copy-start(f32[4,2]{0,1:T(2,128)} %param.27) | copy-start | bytes 100
  48.5 28.3 %copy-start.20 = (f32[4,2]{0,1:T(2,128)S(1)}, f32[4,2]{0,1:T(2,128)}, u32[]{:S(2)}) copy-start(f32[4,2]{0,1:T(2,128)} %param.28) | copy-start | bytes 100
  48.5 28.4 %copy-start.2 = (f32[1,4,2,64,256]{4,3,2,1,0:T(8,128)S(1)}, f32[1,4,2,64,256]{4,3,2,1,0:T(8,128)}, u32[]{:S(2)}) copy-start(f32[1,4,2,64,256]{4,3,2,1,0:T(8,128)} %state_ref.1) | copy-start | bytes 1572868
  48.5 28.3 %copy-start.3 = (s32[8,64,64]{2,1,0:T(8,128)S(1)}, s32[8,64,64]{2,1,0:T(8,128)}, u32[]{:S(2)}) copy-start(s32[8,64,64]{2,1,0:T(8,128)} %anc_ref.1) | copy-start | bytes 393220
  48.6 28.3 %copy-start.5 = (bf16[4,4,512]{2,1,0:T(4,128)(2,1)S(1)}, bf16[4,4,512]{2,1,0:T(4,128)(2,1)}, u32[]{:S(2)}) copy-start(bf16[4,4,512]{2,1,0:T(4,128)(2,1)} %bc_taps_ref.1) | copy-start | bytes 49156
  48.6 28.3 %copy-start.7 = (bf16[4,4,128]{2,1,0:T(4,128)(2,1)S(1)}, bf16[4,4,128]{2,1,0:T(4,128)(2,1)}, u32[]{:S(2)}) copy-start(bf16[4,4,128]{2,1,0:T(4,128)(2,1)} %x_taps_ref.1) | copy-start | bytes 12292
  48.6 28.3 %copy-start.8 = (s32[8,64]{1,0:T(8,128)S(1)}, s32[8,64]{1,0:T(8,128)}, u32[]{:S(2)}) copy-start(s32[8,64]{1,0:T(8,128)} %parents_ref.1) | copy-start | bytes 6148
  48.6 28.3 %copy-start.10 = (f32[4,128]{1,0:T(4,128)S(1)}, f32[4,128]{1,0:T(4,128)}, u32[]{:S(2)}) copy-start(f32[4,128]{1,0:T(4,128)} %gain_ref.1) | copy-start | bytes 6148
  48.6 28.3 %copy-start.11 = (s32[8]{0:T(128)S(1)}, s32[8]{0:T(128)}, u32[]{:S(2)}) copy-start(s32[8]{0:T(128)} %slot_ref.1) | copy-start | bytes 100
  48.6 20.5 %all-to-all-start.1 = ((bf16[16,80,256]{2,1,0:T(8,128)(2,1)}), bf16[16,80,256]{2,1,0:T(8,128)(2,1)S(1)}, u32[]{:S(2)}, u32[]{:S(2)}) async-start(bf16[16,80,256]{2,1,0:T(8,128)(2,1)} %add_convert_fusion.1), calls=%async_computation.1 | async-start | bytes 1310720 | tf_op jit(solution)/shard_map/all_to_all | solution.py:24
  69.8 19.0 %all-to-all-start.2 = ((bf16[16,16,128]{2,1,0:T(8,128)(2,1)}), bf16[16,16,128]{2,1,0:T(8,128)(2,1)S(1)}, u32[]{:S(2)}, u32[]{:S(2)}) async-start(bf16[16,16,128]{2,1,0:T(8,128)(2,1)} %get-tuple-element.13), calls=%async_computation.2 | async-start | bytes 131072 | tf_op jit(solution)/shard_map/all_to_all | solution.py:24
  106.2 15.7 %all-to-all-start.4 = ((bf16[32,4,2048]{2,1,0:T(4,128)(2,1)}), bf16[32,4,2048]{2,1,0:T(4,128)(2,1)S(1)}, u32[]{:S(2)}, u32[]{:S(2)}) async-start(bf16[32,4,2048]{2,1,0:T(4,128)(2,1)} %shard_map.205), calls=%async_computation.4 | async-start | bytes 1048576 | tf_op jit(solution)/shard_map/all_to_all | solution.py:24
  121.8 0.8 copy-start.12
  122.6 27.7 %copy-start = (bf16[256,2048]{1,0:T(8,128)(2,1)S(1)}, bf16[256,2048]{1,0:T(8,128)(2,1)}, u32[]{:S(2)}) copy-start(bf16[256,2048]{1,0:T(8,128)(2,1)} %weight_ref.5) | copy-start | bytes 3145732
  122.6 27.7 %copy-start.6 = (f32[256]{0:T(256)S(1)}, f32[256]{0:T(256)}, u32[]{:S(2)}) copy-start(f32[256]{0:T(256)} %param.39) | copy-start | bytes 3076
  150.7 4.6 %collective-permute-start.1 = (bf16[16,16,2176]{2,1,0:T(8,128)(2,1)S(1)}, bf16[16,16,2176]{2,1,0:T(8,128)(2,1)S(1)}, u32[]{:S(2)}, u32[]{:S(2)}) collective-permute-start(bf16[16,16,2176]{2,1,0:T(8,128)(2,1)S(1)} %shard_map.208), channel_id=1, source_target_pairs={{0,16},{16,0},{32,48},{48,32},{64,80},{80,64},{96,112},{112,96},{1... | collective-permute-start | bytes 3342344 | tf_op jit(solution)/shard_map/ppermute | solution.py:385
  177.8 21.7 %copy-start.1 = (bf16[2048,256]{1,0:T(8,128)(2,1)S(1)}, bf16[2048,256]{1,0:T(8,128)(2,1)}, u32[]{:S(2)}) copy-start(bf16[2048,256]{1,0:T(8,128)(2,1)} %weight_ref.7) | copy-start | bytes 3145732
  197.5 4.5 %collective-permute-start.2 = (bf16[16,16,2048]{2,1,0:T(8,128)(2,1)S(1)}, bf16[16,16,2048]{2,1,0:T(8,128)(2,1)S(1)}, u32[]{:S(2)}, u32[]{:S(2)}) collective-permute-start(bf16[16,16,2048]{2,1,0:T(8,128)(2,1)S(1)} %all_to_all.48.act_ref), channel_id=1, source_target_pairs={{0,16},{16,0},{32,48},{48,32},{64,80},{80,64},{96,112},{112,96},{1... | collective-permute-start | bytes 3145736 | tf_op jit(solution)/shard_map/ppermute | solution.py:488
  203.2 23.8 %all-to-all-start.8 = ((bf16[16,32,256]{2,1,0:T(8,128)(2,1)}), bf16[16,32,256]{2,1,0:T(8,128)(2,1)S(1)}, u32[]{:S(2)}, u32[]{:S(2)}) async-start(bf16[16,32,256]{2,1,0:T(8,128)(2,1)} %shard_map.211), calls=%async_computation.8 | async-start | bytes 524288 | tf_op jit(solution)/shard_map/all_to_all | solution.py:24
Sparse Core Ops, SparseCore 0:
  9.4 88.1 all-gather.2

commit v6 on v5

--- a/solution.py
+++ b/solution.py
@@ -258,43 +258,47 @@
     for part in range(1, parts_ref.shape[0]):
         total = total + parts_ref[part, :, 128:256].astype(F32)
     scale = lax.rsqrt(total / (H // G * P_SIZE) + EPSILON)
-    for part in range(parts_ref.shape[0]):
-        piece = (parts_ref[part, :, 0:128].astype(F32) * scale).astype(BF16)
-        for row in range(out_ref.shape[0]):
-            out_ref[row, :, part * 128 : (part + 1) * 128] = piece
-
-
-def out_kernel(heads_ref, weight_ref, residual_ref, out_ref, left_ref, sum_ref):
-    group = pl.program_id(0)
-    for request in range(8):
-        left_ref[request * 4 : request * 4 + 4, :] = heads_ref[request * G + group].astype(F32)
-    left = left_ref[...].astype(BF16)
-    weight = weight_ref[...].reshape(-1, 256)
-    term = jnp.dot(left, weight, preferred_element_type=F32)
-
-    @pl.when(group == 0)
-    def _():
-        sum_ref[...] = residual_ref[...].astype(F32)
-
-    sum_ref[...] += term
-
-    @pl.when(group == G - 1)
-    def _():
-        after = sum_ref[...].astype(BF16)
-        for col in range(out_ref.shape[0]):
-            out_ref[col] = after
-
-
-def up_kernel(flip, parity_ref, after_ref, gain_ref, weight_ref, out_ref):
-    use = parity_ref[0] if not flip else 1 - parity_ref[0]
-    after = after_ref[...].astype(F32)
-    after = jnp.where(use == 0, after[:, 0:16, :], after[:, 16:32, :]).reshape(256, 256)
-    normed = (after * gain_ref[...]).astype(BF16)
+    pieces = [parts_ref[part, :, 0:128].astype(F32) * scale for part in range(parts_ref.shape[0])]
+    heads = jnp.concatenate(pieces, axis=0).astype(BF16)
+    for row in range(out_ref.shape[0]):
+        out_ref[row] = heads
+
+
+def out_kernel(parity_ref, heads_ref, weight_ref, residual_ref, mine_ref, other_ref, left_ref):
+    total = residual_ref[...].astype(F32)
+    for group in range(G):
+        for request in range(8):
+            heads = heads_ref[request * G + group].astype(F32)
+            for col in range(16):
+                left_ref[request * 4 : request * 4 + 4, col * 128 : (col + 1) * 128] = heads[
+                    col * 4 : col * 4 + 4, :
+                ]
+        left = left_ref[...].astype(BF16)
+        weight = weight_ref[:, group].reshape(-1, 256)
+        total = total + jnp.dot(left, weight, preferred_element_type=F32)
+    after = total.astype(BF16)
+    first = parity_ref[0] == 0
+    mine_ref[...] = jnp.where(first, after[0:16, :], after[16:32, :])
+    other_ref[...] = jnp.where(first, after[16:32, :], after[0:16, :])
+
+
+def pair_copies_kernel(mine_ref, other_ref, out_ref):
+    for col in range(out_ref.shape[0]):
+        out_ref[col, :, 0:256] = mine_ref[...]
+        out_ref[col, :, 256:512] = other_ref[...]
+
+
+def up_kernel(after_ref, gain_ref, other_gain_ref, weight_ref, other_weight_ref, out_ref):
+    after = after_ref[...].reshape(256, 512).astype(F32)
     stat = jnp.broadcast_to(jnp.sum(after * after, axis=1, keepdims=True), (256, 128))
     stat = stat.astype(BF16)
+    mine = (after[:, 0:256] * gain_ref[...]).astype(BF16)
+    other = (after[:, 256:512] * other_gain_ref[...]).astype(BF16)
     for block in range(4):
         lanes = slice(block * 512, (block + 1) * 512)
-        term = jnp.dot(normed, weight_ref[:, lanes], preferred_element_type=F32).astype(BF16)
+        term = jnp.dot(mine, weight_ref[:, lanes], preferred_element_type=F32)
+        term = term + jnp.dot(other, other_weight_ref[:, lanes], preferred_element_type=F32)
+        term = term.astype(BF16)
         for part in range(16):
             out_ref[part, :, lanes] = term[part * 16 : (part + 1) * 16, :]
     for part in range(16):
@@ -317,7 +321,7 @@
             out_ref[part, :, lanes] = act
 
 
-def down_half(act_ref, weight_ref, turn_ref):
+def down_kernel(act_ref, weight_ref, out_ref, turn_ref):
     term = jnp.dot(act_ref[...].reshape(256, -1), weight_ref[...], preferred_element_type=F32)
     for col in range(16):
         for request in range(4):
@@ -325,17 +329,13 @@
             turn_ref[2 * request + col // 8, col % 8 * 4 : col % 8 * 4 + 4, :] = term[
                 start : start + 4, :
             ]
-    return turn_ref[...].astype(BF16)
-
-
-def down_mine_kernel(act_ref, weight_ref, out_ref, turn_ref):
-    out_ref[...] = down_half(act_ref, weight_ref, turn_ref)
-
-
-def down_other_kernel(parity_ref, act_ref, weight_ref, mine_ref, out_ref, turn_ref):
+    out_ref[...] = turn_ref[...].astype(BF16)
+
+
+def join_kernel(parity_ref, mine_ref, other_ref, out_ref):
     parity = parity_ref[0]
     out_ref[pl.ds(parity * 8, 8)] = mine_ref[...]
-    out_ref[pl.ds(8 - parity * 8, 8)] = down_half(act_ref, weight_ref, turn_ref)
+    out_ref[pl.ds(8 - parity * 8, 8)] = other_ref[...]
 
 
 def local(
@@ -394,7 +394,14 @@
             compiler_params=params,
         )(parity, hidden.reshape(512, 256), norm_mixer[None, :], main, side)
 
-    parts = exchange(pair_sum(project_half), "row", halves)
+    parts = pair_sum(project_half)
+    parts, up_mine, down_mine, gain_mine = lax.optimization_barrier(
+        (parts, ffn_up, ffn_down, norm_ffn[None, :])
+    )
+    up_other, down_other, gain_other = [
+        lax.ppermute(weight, "row", swap) for weight in (up_mine, down_mine, gain_mine)
+    ]
+    parts = exchange(parts, "row", halves)
 
     bc_own, local_sums = call(
         combine_kernel,
@@ -451,60 +458,67 @@
     )(local_sums, bc_new, pack, state)
 
     mixed = exchange(mixed, "col")
-    heads = call(
-        scale_heads_kernel, jax.ShapeDtypeStruct((rows, 4, cols * 128), BF16), mixed
-    )
+    heads = call(scale_heads_kernel, jax.ShapeDtypeStruct((rows, cols * 4, 128), BF16), mixed)
+    heads, out_weights = lax.optimization_barrier((heads, out_weights))
     heads = exchange(heads, "row")
     residual = lax.dynamic_slice(
         hidden.reshape(8, 64, 256), (0, 4 * col_index, 0), (8, 4, 256)
     ).reshape(32, 256)
-    after = pl.pallas_call(
+    half_after = jax.ShapeDtypeStruct((16, 256), BF16)
+    after_mine, after_other = pl.pallas_call(
         out_kernel,
-        grid=(G,),
+        out_shape=(half_after, half_after),
+        in_specs=[smem, vmem, vmem, vmem],
+        out_specs=(vmem, vmem),
+        scratch_shapes=[pltpu.VMEM((32, 2048), F32)],
+        compiler_params=params,
+    )(parity, heads, out_weights, residual)
+
+    after_other = lax.ppermute(after_other, "row", swap)
+    after = exchange(
+        call(
+            pair_copies_kernel,
+            jax.ShapeDtypeStruct((cols, 16, 512), BF16),
+            after_mine,
+            after_other,
+        ),
+        "col",
+    )
+    up_parts = call(
+        up_kernel,
+        jax.ShapeDtypeStruct((16, 16, 2176), BF16),
+        after,
+        gain_mine,
+        gain_other,
+        up_mine,
+        up_other,
+    )
+    up_parts = exchange(up_parts, "row", halves)
+    act = call(act_kernel, jax.ShapeDtypeStruct((16, 16, 2048), BF16), up_parts)
+    act = exchange(act, "row", halves)
+
+    def down_half(weight):
+        return pl.pallas_call(
+            down_kernel,
+            out_shape=jax.ShapeDtypeStruct((8, 32, 256), BF16),
+            scratch_shapes=[pltpu.VMEM((8, 32, 256), F32)],
+            compiler_params=params,
+        )(act, weight)
+
+    from_other = lax.ppermute(down_half(down_other), "row", swap)
+    down = pl.pallas_call(
+        join_kernel,
         out_shape=jax.ShapeDtypeStruct((cols, 32, 256), BF16),
-        in_specs=[
-            pl.BlockSpec(heads.shape, lambda group: (0, 0, 0)),
-            pl.BlockSpec((cols, 1, 128, 256), lambda group: (0, group, 0, 0)),
-            pl.BlockSpec((32, 256), lambda group: (0, 0)),
-        ],
-        out_specs=pl.BlockSpec((cols, 32, 256), lambda group: (0, 0, 0)),
-        scratch_shapes=[pltpu.VMEM((32, 2048), F32), pltpu.VMEM((32, 256), F32)],
-        compiler_params=pltpu.CompilerParams(vmem_limit_bytes=60 * 1024 * 1024),
-    )(heads, out_weights, residual)
-    after = exchange(after, "col")
-
-    def up_half(flip):
-        return pl.pallas_call(
-            functools.partial(up_kernel, flip),
-            out_shape=jax.ShapeDtypeStruct((16, 16, 2176), BF16),
-            in_specs=[smem, vmem, vmem, vmem],
-            out_specs=vmem,
-            compiler_params=params,
-        )(parity, after, norm_ffn[None, :], ffn_up)
-
-    up_parts = exchange(pair_sum(up_half), "row", halves)
-    act = call(act_kernel, jax.ShapeDtypeStruct((16, 16, 2048), BF16), up_parts)
-    act_mine = exchange(act, "row", halves)
-    act_other = lax.ppermute(act_mine, "row", swap)
-    turn = [pltpu.VMEM((8, 32, 256), F32)]
-    down_mine = pl.pallas_call(
-        down_mine_kernel,
-        out_shape=jax.ShapeDtypeStruct((8, 32, 256), BF16),
-        scratch_shapes=turn,
+        in_specs=[smem, vmem, vmem],
+        out_specs=vmem,
         compiler_params=params,
-    )(act_mine, ffn_down)
-    down = pl.pallas_call(
-        down_other_kernel,
-        out_shape=jax.ShapeDtypeStruct((cols, 32, 256), BF16),
-        in_specs=[smem, vmem, vmem, vmem],
-        out_specs=vmem,
-        scratch_shapes=turn,
-        compiler_params=params,
-    )(parity, act_other, ffn_down, down_mine)
+    )(parity, down_half(down_mine), from_other)
     ffn_out = jnp.sum(exchange(down, "col").astype(F32), axis=0)
-    own_after = lax.dynamic_slice(
-        after, (8 * (col_index % 2), 4 * (col_index // 2), 0), (8, 4, 256)
-    ).reshape(32, 256)
+    own = lax.dynamic_slice(
+        after, (8 * (col_index % 2), 4 * (col_index // 2 % 4), 0), (8, 4, 512)
+    ).reshape(32, 512)
+    own_other = lax.ppermute(own[:, 256:], "row", swap)
+    own_after = jnp.where(col_index // 8 == row_index % 2, own[:, :256], own_other)
     return (own_after.astype(F32) + ffn_out).astype(BF16)
 
 

time: 235 us -> 236 us (level)
  blocking collectives: 80.3 us -> 15.4 us
  waiting for transfers between devices: 77.3 us -> 119 us
  starting transfers between devices: 44.2 us -> 67.1 us
    all_to_all x4 -> x1, blocking collectives: 80.3 us -> 15.4 us  [exchange(): lax.all_to_all(parts, axis, 0, 0, tiled=True, axis_index_groups=groups)]
    all_to_all x5 -> x8, waiting for transfers between devices: 70.7 us -> 114 us  [exchange(): lax.all_to_all(parts, axis, 0, 0, tiled=True, axis_index_groups=groups)]
    all_to_all x5 -> x8, starting transfers between devices: 38.5 us -> 53.5 us  [exchange(): lax.all_to_all(parts, axis, 0, 0, tiled=True, axis_index_groups=groups)]
    ppermute x1 -> x6, starting transfers between devices: 1.91 us -> 11.7 us  [the longest x3 5.91 us: local(): lax.ppermute(weight, 'row', swap)]
    pallas_call x5 -> x4, Pallas kernels: 6.89 us -> 2.47 us  [the longest x2 0.92 us: down_half(): pl.pallas_call(down_kernel, out_shape=jax.ShapeDtypeStruct((8, 32, 256),...]
    pallas_call x4 -> x6, Pallas kernels: 2.81 us -> 6.1 us  [call(): pl.pallas_call(kernel, out_shape=out_shape, compiler_params=pltpu.Compile...]
  transfers between devices with their start and end apart: 9 -> 16, of which waited for: 8 -> 12; matrix products, arithmetic and copies ran while one was open for 1% -> 1% of each run, Pallas kernels for 3% -> 4%
where the time goes in v6:
time: 236 us; the launch traced here: 235 us
  waiting for transfers between devices  119 us (50%)
  starting transfers between devices  67.1 us (28%)
  blocking collectives  15.4 us (7%)
  between operations  13.8 us (6%)
  Pallas kernels  12.7 us (5%)
  local copies, waits for them, and re-layouts  4.83 us (2%)
    all_to_all x8, waiting for transfers between devices, exchange(): lax.all_to_all(parts, axis, 0, 0, tiled=True, axis_index_groups=groups)  114 us
    all_to_all x8, starting transfers between devices, exchange(): lax.all_to_all(parts, axis, 0, 0, tiled=True, axis_index_groups=groups)  53.5 us
    all_to_all x1, blocking collectives, exchange(): lax.all_to_all(parts, axis, 0, 0, tiled=True, axis_index_groups=groups)  15.4 us
    pallas_call x6, Pallas kernels, call(): pl.pallas_call(kernel, out_shape=out_shape, compiler_params=pltpu.Compile...  6.1 us
    ppermute x3, starting transfers between devices, local(): lax.ppermute(weight, 'row', swap)  5.91 us
  transfers between devices with their start and end apart: 16, of which 12 were waited for; matrix products, arithmetic and copies ran while one was open for 1% of the time, Pallas kernels for 4%

profile of v6, /device:TPU:32, one launch (start us, length us, event | category | flops | bytes accessed | tf_op | source)
XLA Modules:
  0.0 235.0 jit_solution(1427339593163691020)
XLA Ops:
  6.5 0.7 all-gather.3.cloned.1.call-update
  7.3 0.7 copy-done.5
  8.0 0.7 shard_map.199
  8.7 15.2 %all-to-all-start = ((bf16[16,32,256]{2,1,0:T(8,128)(2,1)}), bf16[16,32,256]{2,1,0:T(8,128)(2,1)S(1)}, u32[]{:S(2)}, u32[]{:S(2)}) async-start(bf16[16,32,256]{2,1,0:T(8,128)(2,1)} %shard_map.199), calls=%async_computation | async-start | bytes 524288 | tf_op jit(solution)/shard_map/all_to_all | solution.py:24
  23.9 1.4 reshape.20.main_ref
  25.5 17.4 %all-to-all-done = bf16[16,32,256]{2,1,0:T(8,128)(2,1)S(1)} async-done(((bf16[16,32,256]{2,1,0:T(8,128)(2,1)}), bf16[16,32,256]{2,1,0:T(8,128)(2,1)S(1)}, u32[]{:S(2)}, u32[]{:S(2)}) %all-to-all-start) | async-done | bytes 262176 | tf_op jit(solution)/shard_map/all_to_all | solution.py:24
  42.9 0.6 shard_map.201
  43.5 1.9 collective-permute-start
  45.4 0.6 shard_map.200
  46.0 1.5 collective-permute-done
  47.5 1.0 add_convert_fusion
  48.6 7.2 %all-to-all-start.1 = ((bf16[16,80,256]{2,1,0:T(8,128)(2,1)}), bf16[16,80,256]{2,1,0:T(8,128)(2,1)S(1)}, u32[]{:S(2)}, u32[]{:S(2)}) async-start(bf16[16,80,256]{2,1,0:T(8,128)(2,1)} %add_convert_fusion), calls=%async_computation.1 | async-start | bytes 1310720 | tf_op jit(solution)/shard_map/all_to_all | solution.py:24
  55.9 13.1 %all-to-all-done.1.parts_ref = bf16[16,80,256]{2,1,0:T(8,128)(2,1)S(1)} async-done(((bf16[16,80,256]{2,1,0:T(8,128)(2,1)}), bf16[16,80,256]{2,1,0:T(8,128)(2,1)S(1)}, u32[]{:S(2)}, u32[]{:S(2)}) %all-to-all-start.1) | async-done | bytes 655392 | tf_op jit(solution)/shard_map/all_to_all | solution.py:24
  69.1 0.7 shard_map.202
  69.8 6.7 %all-to-all-start.2 = ((bf16[16,16,128]{2,1,0:T(8,128)(2,1)}), bf16[16,16,128]{2,1,0:T(8,128)(2,1)S(1)}, u32[]{:S(2)}, u32[]{:S(2)}) async-start(bf16[16,16,128]{2,1,0:T(8,128)(2,1)} %get-tuple-element.22), calls=%async_computation.2 | async-start | bytes 131072 | tf_op jit(solution)/shard_map/all_to_all | solution.py:24
  76.9 2.2 shard_map.203
  79.1 9.6 %all-to-all-done.2.bc_new_ref = bf16[16,16,128]{2,1,0:T(8,128)(2,1)S(1)} async-done(((bf16[16,16,128]{2,1,0:T(8,128)(2,1)}), bf16[16,16,128]{2,1,0:T(8,128)(2,1)S(1)}, u32[]{:S(2)}, u32[]{:S(2)}) %all-to-all-start.2) | async-done | bytes 65568 | tf_op jit(solution)/shard_map/all_to_all | solution.py:24
  88.8 0.8 shard_map.204
  89.6 15.4 %all_to_all.45.parts_ref = bf16[16,4,256]{2,1,0:T(4,128)(2,1)S(1)} all-to-all(bf16[16,4,256]{2,1,0:T(4,128)(2,1)S(1)} %shard_map.204), channel_id=1, replica_groups=mesh['row'=32,'col'=16] {'col'}, dimensions={0} | all-to-all | bytes 65536 | tf_op jit(solution)/shard_map/all_to_all | solution.py:24
  105.0 0.9 shard_map.205
  105.9 3.9 %all-to-all-start.4 = ((bf16[32,64,128]{2,1,0:T(8,128)(2,1)}), bf16[32,64,128]{2,1,0:T(8,128)(2,1)S(1)}, u32[]{:S(2)}, u32[]{:S(2)}) async-start(bf16[32,64,128]{2,1,0:T(8,128)(2,1)} %shard_map.205), calls=%async_computation.4 | async-start | bytes 1048576 | tf_op jit(solution)/shard_map/all_to_all | solution.py:24
  109.8 2.1 collective-permute-start.4
  112.0 9.6 %all-to-all-done.4.heads_ref = bf16[32,64,128]{2,1,0:T(8,128)(2,1)S(1)} async-done(((bf16[32,64,128]{2,1,0:T(8,128)(2,1)}), bf16[32,64,128]{2,1,0:T(8,128)(2,1)S(1)}, u32[]{:S(2)}, u32[]{:S(2)}) %all-to-all-start.4) | async-done | bytes 524320 | tf_op jit(solution)/shard_map/all_to_all | solution.py:24
  121.6 2.2 copy-done
  123.8 0.8 shard_map.206
  124.6 2.0 collective-permute-start.1
  126.6 1.1 collective-permute-done.1.other_ref
  127.7 0.7 shard_map.207
  128.4 4.6 %all-to-all-start.5 = ((bf16[16,16,512]{2,1,0:T(8,128)(2,1)}), bf16[16,16,512]{2,1,0:T(8,128)(2,1)S(1)}, u32[]{:S(2)}, u32[]{:S(2)}) async-start(bf16[16,16,512]{2,1,0:T(8,128)(2,1)} %shard_map.207), calls=%async_computation.5 | async-start | bytes 524288 | tf_op jit(solution)/shard_map/all_to_all | solution.py:24
  133.0 1.9 collective-permute-start.3
  134.9 1.1 collective-permute-done.3.other_gain_ref
  136.0 15.8 %all-to-all-done.5.after_ref = bf16[16,16,512]{2,1,0:T(8,128)(2,1)S(1)} async-done(((bf16[16,16,512]{2,1,0:T(8,128)(2,1)}), bf16[16,16,512]{2,1,0:T(8,128)(2,1)S(1)}, u32[]{:S(2)}, u32[]{:S(2)}) %all-to-all-start.5) | async-done | bytes 262176 | tf_op jit(solution)/shard_map/all_to_all | solution.py:24
  151.8 1.7 shard_map.208
  153.6 3.8 %all-to-all-start.6 = ((bf16[16,16,2176]{2,1,0:T(8,128)(2,1)}), bf16[16,16,2176]{2,1,0:T(8,128)(2,1)S(1)}, u32[]{:S(2)}, u32[]{:S(2)}) async-start(bf16[16,16,2176]{2,1,0:T(8,128)(2,1)} %shard_map.208), calls=%async_computation.6 | async-start | bytes 2228224 | tf_op jit(solution)/shard_map/all_to_all | solution.py:24
  157.4 1.9 collective-permute-start.5
  159.3 15.8 %all-to-all-done.6.parts_ref = bf16[16,16,2176]{2,1,0:T(8,128)(2,1)S(1)} async-done(((bf16[16,16,2176]{2,1,0:T(8,128)(2,1)}), bf16[16,16,2176]{2,1,0:T(8,128)(2,1)S(1)}, u32[]{:S(2)}, u32[]{:S(2)}) %all-to-all-start.6) | async-done | bytes 1114144 | tf_op jit(solution)/shard_map/all_to_all | solution.py:24
  175.2 1.3 shard_map.209
  176.5 3.7 %all-to-all-start.7 = ((bf16[16,16,2048]{2,1,0:T(8,128)(2,1)}), bf16[16,16,2048]{2,1,0:T(8,128)(2,1)S(1)}, u32[]{:S(2)}, u32[]{:S(2)}) async-start(bf16[16,16,2048]{2,1,0:T(8,128)(2,1)} %shard_map.209), calls=%async_computation.7 | async-start | bytes 2097152 | tf_op jit(solution)/shard_map/all_to_all | solution.py:24
  180.1 16.1 %all-to-all-done.7.act_ref = bf16[16,16,2048]{2,1,0:T(8,128)(2,1)S(1)} async-done(((bf16[16,16,2048]{2,1,0:T(8,128)(2,1)}), bf16[16,16,2048]{2,1,0:T(8,128)(2,1)S(1)}, u32[]{:S(2)}, u32[]{:S(2)}) %all-to-all-start.7) | async-done | bytes 1048608 | tf_op jit(solution)/shard_map/all_to_all | solution.py:24
  196.2 0.5 shard_map.211
  196.7 1.9 collective-permute-start.6
  198.6 0.5 shard_map.210.mine_ref
  199.1 0.8 collective-permute-done.6.other_ref
  199.9 0.7 shard_map.212
  200.7 8.4 %all-to-all-start.8 = ((bf16[16,32,256]{2,1,0:T(8,128)(2,1)}), bf16[16,32,256]{2,1,0:T(8,128)(2,1)S(1)}, u32[]{:S(2)}, u32[]{:S(2)}) async-start(bf16[16,32,256]{2,1,0:T(8,128)(2,1)} %shard_map.212), calls=%async_computation.8 | async-start | bytes 524288 | tf_op jit(solution)/shard_map/all_to_all | solution.py:24
  209.1 1.9 collective-permute-start.2
  211.1 16.4 %all-to-all-done.8 = bf16[16,32,256]{2,1,0:T(8,128)(2,1)S(1)} async-done(((bf16[16,32,256]{2,1,0:T(8,128)(2,1)}), bf16[16,32,256]{2,1,0:T(8,128)(2,1)S(1)}, u32[]{:S(2)}, u32[]{:S(2)}) %all-to-all-start.8) | async-done | bytes 262176 | tf_op jit(solution)/shard_map/all_to_all | solution.py:24
  227.5 0.6 add_convert_fusion.1
  (58 shorter events, 0.7 us)
Async XLA Ops:
  6.5 18.9 %copy-start.13 = (bf16[256,4,32]{0,2,1:T(8,128)(2,1)S(1)}, bf16[256,4,32]{0,2,1:T(8,128)(2,1)}, u32[]{:S(2)}) copy-start(bf16[256,4,32]{0,2,1:T(8,128)(2,1)} %param.24) | copy-start | bytes 196612
  6.5 18.9 %copy-start.15 = (bf16[256,4,2]{0,2,1:T(2,128)(2,1)S(1)}, bf16[256,4,2]{0,2,1:T(2,128)(2,1)}, u32[]{:S(2)}) copy-start(bf16[256,4,2]{0,2,1:T(2,128)(2,1)} %param.25) | copy-start | bytes 12292
  6.5 36.4 %copy-start.9 = (f32[256]{0:T(256)S(1)}, f32[256]{0:T(256)}, u32[]{:S(2)}) copy-start(f32[256]{0:T(256)} %param.22) | copy-start | bytes 3076
  6.5 99.4 %all-gather.3.cloned.1.call-start = ((), (), s32[]{:S(2)}) async-start(), calls=%async_computation.9 | async-start | bytes 4456448 | tf_op jit(solution)/shard_map/all_gather | solution.py:376
  7.3 0.7 copy-start.5
  8.7 34.2 %all-to-all-start = ((bf16[16,32,256]{2,1,0:T(8,128)(2,1)}), bf16[16,32,256]{2,1,0:T(8,128)(2,1)S(1)}, u32[]{:S(2)}, u32[]{:S(2)}) async-start(bf16[16,32,256]{2,1,0:T(8,128)(2,1)} %shard_map.199), calls=%async_computation | async-start | bytes 524288 | tf_op jit(solution)/shard_map/all_to_all | solution.py:24
  43.5 4.0 %collective-permute-start = (bf16[16,80,256]{2,1,0:T(8,128)(2,1)S(1)}, bf16[16,80,256]{2,1,0:T(8,128)(2,1)S(1)}, u32[]{:S(2)}, u32[]{:S(2)}) collective-permute-start(bf16[16,80,256]{2,1,0:T(8,128)(2,1)S(1)} %shard_map.201), channel_id=1, source_target_pairs={{0,16},{16,0},{32,48},{48,32},{64,80},{80,64},{96,112},{112,96},{1... | collective-permute-start | bytes 1966088 | tf_op jit(solution)/shard_map/ppermute | solution.py:385
  48.5 28.0 %copy-start.14 = (bf16[1,4,3,512]{3,1,2,0:T(4,128)(2,1)S(1)}, bf16[1,4,3,512]{3,1,2,0:T(4,128)(2,1)}, u32[]{:S(2)}) copy-start(bf16[1,4,3,512]{3,1,2,0:T(4,128)(2,1)} %param.32) | copy-start | bytes 36868
  48.5 28.0 %copy-start.16 = (bf16[1,4,3,128]{3,1,2,0:T(4,128)(2,1)S(1)}, bf16[1,4,3,128]{3,1,2,0:T(4,128)(2,1)}, u32[]{:S(2)}) copy-start(bf16[1,4,3,128]{3,1,2,0:T(4,128)(2,1)} %param.31) | copy-start | bytes 9220
  48.5 28.1 %copy-start.17 = (f32[4,2]{0,1:T(2,128)S(1)}, f32[4,2]{0,1:T(2,128)}, u32[]{:S(2)}) copy-start(f32[4,2]{0,1:T(2,128)} %param.26) | copy-start | bytes 100
  48.5 28.2 %copy-start.18 = (f32[4,2]{0,1:T(2,128)S(1)}, f32[4,2]{0,1:T(2,128)}, u32[]{:S(2)}) copy-start(f32[4,2]{0,1:T(2,128)} %param.27) | copy-start | bytes 100
  48.5 28.3 %copy-start.19 = (f32[4,2]{0,1:T(2,128)S(1)}, f32[4,2]{0,1:T(2,128)}, u32[]{:S(2)}) copy-start(f32[4,2]{0,1:T(2,128)} %param.28) | copy-start | bytes 100
  48.5 28.3 %copy-start.3 = (f32[1,4,2,64,256]{4,3,2,1,0:T(8,128)S(1)}, f32[1,4,2,64,256]{4,3,2,1,0:T(8,128)}, u32[]{:S(2)}) copy-start(f32[1,4,2,64,256]{4,3,2,1,0:T(8,128)} %state_ref.1) | copy-start | bytes 1572868
  48.5 28.3 %copy-start.4 = (s32[8,64,64]{2,1,0:T(8,128)S(1)}, s32[8,64,64]{2,1,0:T(8,128)}, u32[]{:S(2)}) copy-start(s32[8,64,64]{2,1,0:T(8,128)} %anc_ref.1) | copy-start | bytes 393220
  48.5 28.3 %copy-start.6 = (bf16[4,4,512]{2,1,0:T(4,128)(2,1)S(1)}, bf16[4,4,512]{2,1,0:T(4,128)(2,1)}, u32[]{:S(2)}) copy-start(bf16[4,4,512]{2,1,0:T(4,128)(2,1)} %bc_taps_ref.1) | copy-start | bytes 49156
  48.5 28.3 %copy-start.7 = (bf16[4,4,128]{2,1,0:T(4,128)(2,1)S(1)}, bf16[4,4,128]{2,1,0:T(4,128)(2,1)}, u32[]{:S(2)}) copy-start(bf16[4,4,128]{2,1,0:T(4,128)(2,1)} %x_taps_ref.1) | copy-start | bytes 12292
  48.6 28.3 %copy-start.8 = (s32[8,64]{1,0:T(8,128)S(1)}, s32[8,64]{1,0:T(8,128)}, u32[]{:S(2)}) copy-start(s32[8,64]{1,0:T(8,128)} %parents_ref.1) | copy-start | bytes 6148
  48.6 28.3 %copy-start.10 = (f32[4,128]{1,0:T(4,128)S(1)}, f32[4,128]{1,0:T(4,128)}, u32[]{:S(2)}) copy-start(f32[4,128]{1,0:T(4,128)} %gain_ref.1) | copy-start | bytes 6148
  48.6 28.3 %copy-start.12 = (s32[8]{0:T(128)S(1)}, s32[8]{0:T(128)}, u32[]{:S(2)}) copy-start(s32[8]{0:T(128)} %slot_ref.1) | copy-start | bytes 100
  48.6 20.5 %all-to-all-start.1 = ((bf16[16,80,256]{2,1,0:T(8,128)(2,1)}), bf16[16,80,256]{2,1,0:T(8,128)(2,1)S(1)}, u32[]{:S(2)}, u32[]{:S(2)}) async-start(bf16[16,80,256]{2,1,0:T(8,128)(2,1)} %add_convert_fusion), calls=%async_computation.1 | async-start | bytes 1310720 | tf_op jit(solution)/shard_map/all_to_all | solution.py:24
  69.8 19.0 %all-to-all-start.2 = ((bf16[16,16,128]{2,1,0:T(8,128)(2,1)}), bf16[16,16,128]{2,1,0:T(8,128)(2,1)S(1)}, u32[]{:S(2)}, u32[]{:S(2)}) async-start(bf16[16,16,128]{2,1,0:T(8,128)(2,1)} %get-tuple-element.22), calls=%async_computation.2 | async-start | bytes 131072 | tf_op jit(solution)/shard_map/all_to_all | solution.py:24
  79.1 30.7 %copy-start.1 = (bf16[256,2048]{1,0:T(8,128)(2,1)S(1)}, bf16[256,2048]{1,0:T(8,128)(2,1)}, u32[]{:S(2)}) copy-start(bf16[256,2048]{1,0:T(8,128)(2,1)} %weight_ref) | copy-start | bytes 3145732
  105.9 15.7 %all-to-all-start.4 = ((bf16[32,64,128]{2,1,0:T(8,128)(2,1)}), bf16[32,64,128]{2,1,0:T(8,128)(2,1)S(1)}, u32[]{:S(2)}, u32[]{:S(2)}) async-start(bf16[32,64,128]{2,1,0:T(8,128)(2,1)} %shard_map.205), calls=%async_computation.4 | async-start | bytes 1048576 | tf_op jit(solution)/shard_map/all_to_all | solution.py:24
  109.8 26.2 %collective-permute-start.4 = (bf16[256,2048]{1,0:T(8,128)(2,1)S(1)}, bf16[256,2048]{1,0:T(8,128)(2,1)S(1)}, u32[]{:S(2)}, u32[]{:S(2)}) collective-permute-start(bf16[256,2048]{1,0:T(8,128)(2,1)S(1)} %copy-done.1), channel_id=1, source_target_pairs={{0,16},{16,0},{32,48},{48,32},{64,80},{80,64},{96,112},{112,96},{1... | collective-permute-start | bytes 3145736 | tf_op jit(solution)/shard_map/ppermute | solution.py:402
  121.6 2.2 copy-start
  123.8 9.2 %copy-start.11 = (f32[256]{0:T(256)S(1)}, f32[256]{0:T(256)}, u32[]{:S(2)}) copy-start(f32[256]{0:T(256)} %param.39) | copy-start | bytes 3076
  124.6 3.1 %collective-permute-start.1 = (bf16[16,256]{1,0:T(8,128)(2,1)S(1)}, bf16[16,256]{1,0:T(8,128)(2,1)S(1)}, u32[]{:S(2)}, u32[]{:S(2)}) collective-permute-start(bf16[16,256]{1,0:T(8,128)(2,1)S(1)} %get-tuple-element.29), channel_id=1, source_target_pairs={{0,16},{16,0},{32,48},{48,32},{64,80},{80,64},{96,112},{112,96},{1... | collective-permute-start | bytes 24584 | tf_op jit(solution)/shard_map/ppermute | solution.py:477
  128.4 23.4 %all-to-all-start.5 = ((bf16[16,16,512]{2,1,0:T(8,128)(2,1)}), bf16[16,16,512]{2,1,0:T(8,128)(2,1)S(1)}, u32[]{:S(2)}, u32[]{:S(2)}) async-start(bf16[16,16,512]{2,1,0:T(8,128)(2,1)} %shard_map.207), calls=%async_computation.5 | async-start | bytes 524288 | tf_op jit(solution)/shard_map/all_to_all | solution.py:24
  133.0 3.0 %collective-permute-start.3 = (f32[1,256]{1,0:T(1,128)S(1)}, f32[1,256]{1,0:T(1,128)S(1)}, u32[]{:S(2)}, u32[]{:S(2)}) collective-permute-start(f32[1,256]{1,0:T(1,128)S(1)} %bitcast.19), channel_id=1, source_target_pairs={{0,16},{16,0},{32,48},{48,32},{64,80},{80,64},{96,112},{112,96},{1... | collective-permute-start | bytes 3080 | tf_op jit(solution)/shard_map/ppermute | solution.py:402
  153.6 3.8 %copy-start.2 = (bf16[2048,256]{1,0:T(8,128)(2,1)S(1)}, bf16[2048,256]{1,0:T(8,128)(2,1)}, u32[]{:S(2)}) copy-start(bf16[2048,256]{1,0:T(8,128)(2,1)} %weight_ref.1) | copy-start | bytes 3145732
  153.6 21.6 %all-to-all-start.6 = ((bf16[16,16,2176]{2,1,0:T(8,128)(2,1)}), bf16[16,16,2176]{2,1,0:T(8,128)(2,1)S(1)}, u32[]{:S(2)}, u32[]{:S(2)}) async-start(bf16[16,16,2176]{2,1,0:T(8,128)(2,1)} %shard_map.208), calls=%async_computation.6 | async-start | bytes 2228224 | tf_op jit(solution)/shard_map/all_to_all | solution.py:24
  157.4 22.7 %collective-permute-start.5 = (bf16[2048,256]{1,0:T(8,128)(2,1)S(1)}, bf16[2048,256]{1,0:T(8,128)(2,1)S(1)}, u32[]{:S(2)}, u32[]{:S(2)}) collective-permute-start(bf16[2048,256]{1,0:T(8,128)(2,1)S(1)} %copy-done.2), channel_id=1, source_target_pairs={{0,16},{16,0},{32,48},{48,32},{64,80},{80,64},{96,112},{112,96},{1... | collective-permute-start | bytes 3145736 | tf_op jit(solution)/shard_map/ppermute | solution.py:402
  176.5 19.8 %all-to-all-start.7 = ((bf16[16,16,2048]{2,1,0:T(8,128)(2,1)}), bf16[16,16,2048]{2,1,0:T(8,128)(2,1)S(1)}, u32[]{:S(2)}, u32[]{:S(2)}) async-start(bf16[16,16,2048]{2,1,0:T(8,128)(2,1)} %shard_map.209), calls=%async_computation.7 | async-start | bytes 2097152 | tf_op jit(solution)/shard_map/all_to_all | solution.py:24
  196.7 3.2 %collective-permute-start.6 = (bf16[8,32,256]{2,1,0:T(8,128)(2,1)S(1)}, bf16[8,32,256]{2,1,0:T(8,128)(2,1)S(1)}, u32[]{:S(2)}, u32[]{:S(2)}) collective-permute-start(bf16[8,32,256]{2,1,0:T(8,128)(2,1)S(1)} %shard_map.211), channel_id=1, source_target_pairs={{0,16},{16,0},{32,48},{48,32},{64,80},{80,64},{96,112},{112,96},{1... | collective-permute-start | bytes 393224 | tf_op jit(solution)/shard_map/ppermute | solution.py:508
  200.7 26.8 %all-to-all-start.8 = ((bf16[16,32,256]{2,1,0:T(8,128)(2,1)}), bf16[16,32,256]{2,1,0:T(8,128)(2,1)S(1)}, u32[]{:S(2)}, u32[]{:S(2)}) async-start(bf16[16,32,256]{2,1,0:T(8,128)(2,1)} %shard_map.212), calls=%async_computation.8 | async-start | bytes 524288 | tf_op jit(solution)/shard_map/all_to_all | solution.py:24
  209.1 18.4 %collective-permute-start.2 = (bf16[32,256]{1,0:T(8,128)(2,1)S(1)}, bf16[32,256]{1,0:T(8,128)(2,1)S(1)}, u32[]{:S(2)}, u32[]{:S(2)}) collective-permute-start(bf16[32,256]{1,0:T(8,128)(2,1)S(1)} %slice.9), channel_id=1, source_target_pairs={{0,16},{16,0},{32,48},{48,32},{64,80},{80,64},{96,112},{112,96},{1... | collective-permute-start | bytes 49160 | tf_op jit(solution)/shard_map/ppermute | solution.py:520
Sparse Core Ops, SparseCore 0:
  9.4 88.6 all-gather.2

commit v7 on v6

--- a/solution.py
+++ b/solution.py
@@ -264,6 +264,10 @@
         out_ref[row] = heads
 
 
+def by_group_kernel(weight_ref, out_ref):
+    out_ref[0] = weight_ref[...].reshape(-1, 256)
+
+
 def out_kernel(parity_ref, heads_ref, weight_ref, residual_ref, mine_ref, other_ref, left_ref):
     total = residual_ref[...].astype(F32)
     for group in range(G):
@@ -274,8 +278,7 @@
                     col * 4 : col * 4 + 4, :
                 ]
         left = left_ref[...].astype(BF16)
-        weight = weight_ref[:, group].reshape(-1, 256)
-        total = total + jnp.dot(left, weight, preferred_element_type=F32)
+        total = total + jnp.dot(left, weight_ref[group], preferred_element_type=F32)
     after = total.astype(BF16)
     first = parity_ref[0] == 0
     mine_ref[...] = jnp.where(first, after[0:16, :], after[16:32, :])
@@ -395,12 +398,6 @@
         )(parity, hidden.reshape(512, 256), norm_mixer[None, :], main, side)
 
     parts = pair_sum(project_half)
-    parts, up_mine, down_mine, gain_mine = lax.optimization_barrier(
-        (parts, ffn_up, ffn_down, norm_ffn[None, :])
-    )
-    up_other, down_other, gain_other = [
-        lax.ppermute(weight, "row", swap) for weight in (up_mine, down_mine, gain_mine)
-    ]
     parts = exchange(parts, "row", halves)
 
     bc_own, local_sums = call(
@@ -450,6 +447,12 @@
     )(place, slot_ids, *[operand for operand, _ in operands])
 
     bc_new = exchange(bc_own, "col")
+    bc_new, up_mine, down_mine, gain_mine = lax.optimization_barrier(
+        (bc_new, ffn_up, ffn_down, norm_ffn[None, :])
+    )
+    up_other, down_other, gain_other = [
+        lax.ppermute(weight, "row", swap) for weight in (up_mine, down_mine, gain_mine)
+    ]
     mixed = pl.pallas_call(
         mixer_kernel,
         out_shape=jax.ShapeDtypeStruct((cols, 4, 256), BF16),
@@ -460,6 +463,14 @@
     mixed = exchange(mixed, "col")
     heads = call(scale_heads_kernel, jax.ShapeDtypeStruct((rows, cols * 4, 128), BF16), mixed)
     heads, out_weights = lax.optimization_barrier((heads, out_weights))
+    out_weights = pl.pallas_call(
+        by_group_kernel,
+        grid=(G,),
+        out_shape=jax.ShapeDtypeStruct((G, cols * 128, 256), BF16),
+        in_specs=[pl.BlockSpec((cols, 1, 128, 256), lambda group: (0, group, 0, 0))],
+        out_specs=pl.BlockSpec((1, cols * 128, 256), lambda group: (group, 0, 0)),
+        compiler_params=params,
+    )(out_weights)
     heads = exchange(heads, "row")
     residual = lax.dynamic_slice(
         hidden.reshape(8, 64, 256), (0, 4 * col_index, 0), (8, 4, 256)
@@ -493,6 +504,7 @@
         up_mine,
         up_other,
     )
+    up_parts, down_other = lax.optimization_barrier((up_parts, down_other))
     up_parts = exchange(up_parts, "row", halves)
     act = call(act_kernel, jax.ShapeDtypeStruct((16, 16, 2048), BF16), up_parts)
     act = exchange(act, "row", halves)

time: 236 us -> 234 us (level)
  blocking collectives: 15.4 us -> 55.6 us
  waiting for transfers between devices: 119 us -> 79.9 us
  starting transfers between devices: 67.1 us -> 59.6 us
    all_to_all x1 -> x3, blocking collectives: 15.4 us -> 55.6 us  [exchange(): lax.all_to_all(parts, axis, 0, 0, tiled=True, axis_index_groups=groups)]
    all_to_all x8 -> x6, waiting for transfers between devices: 114 us -> 74.6 us  [exchange(): lax.all_to_all(parts, axis, 0, 0, tiled=True, axis_index_groups=groups)]
    all_to_all x8 -> x6, starting transfers between devices: 53.5 us -> 45.6 us  [exchange(): lax.all_to_all(parts, axis, 0, 0, tiled=True, axis_index_groups=groups)]
    pallas_call x0 -> x1, Pallas kernels: none -> 3.02 us  [local(): pl.pallas_call(by_group_kernel, grid=(G,), out_shape=jax.ShapeDtypeStruct...]
    unnamed x45 -> x47, local copies, waits for them, and re-layouts: 3.28 us -> 5.25 us
  transfers between devices with their start and end apart: 16 -> 14, of which waited for: 12 -> 10; matrix products, arithmetic and copies ran while one was open for 1% -> 1% of each run, Pallas kernels for 4% -> 5%
where the time goes in v7:
time: 234 us; the launch traced here: 232 us
  waiting for transfers between devices  79.9 us (34%)
  starting transfers between devices  59.6 us (25%)
  blocking collectives  55.6 us (24%)
  Pallas kernels  14.9 us (6%)
  between operations  13.8 us (6%)
  local copies, waits for them, and re-layouts  6.8 us (3%)
    all_to_all x6, waiting for transfers between devices, exchange(): lax.all_to_all(parts, axis, 0, 0, tiled=True, axis_index_groups=groups)  74.6 us
    all_to_all x3, blocking collectives, exchange(): lax.all_to_all(parts, axis, 0, 0, tiled=True, axis_index_groups=groups)  55.6 us
    all_to_all x6, starting transfers between devices, exchange(): lax.all_to_all(parts, axis, 0, 0, tiled=True, axis_index_groups=groups)  45.6 us
    ppermute x3, starting transfers between devices, local(): lax.ppermute(weight, 'row', swap)  6.25 us
    unnamed x47, local copies, waits for them, and re-layouts  5.25 us
  transfers between devices with their start and end apart: 14, of which 10 were waited for; matrix products, arithmetic and copies ran while one was open for 1% of the time, Pallas kernels for 5%

profile of v7, /device:TPU:32, one launch (start us, length us, event | category | flops | bytes accessed | tf_op | source)
XLA Modules:
  0.0 232.5 jit_solution(15852319525457139891)
XLA Ops:
  6.5 0.7 all-gather.3.cloned.1.call-update
  7.3 0.7 copy-done.6
  8.0 0.7 shard_map.199
  8.7 15.2 %all-to-all-start = ((bf16[16,32,256]{2,1,0:T(8,128)(2,1)}), bf16[16,32,256]{2,1,0:T(8,128)(2,1)S(1)}, u32[]{:S(2)}, u32[]{:S(2)}) async-start(bf16[16,32,256]{2,1,0:T(8,128)(2,1)} %shard_map.199), calls=%async_computation | async-start | bytes 524288 | tf_op jit(solution)/shard_map/all_to_all | solution.py:24
  23.9 1.4 reshape.20.main_ref
  25.5 17.4 %all-to-all-done = bf16[16,32,256]{2,1,0:T(8,128)(2,1)S(1)} async-done(((bf16[16,32,256]{2,1,0:T(8,128)(2,1)}), bf16[16,32,256]{2,1,0:T(8,128)(2,1)S(1)}, u32[]{:S(2)}, u32[]{:S(2)}) %all-to-all-start) | async-done | bytes 262176 | tf_op jit(solution)/shard_map/all_to_all | solution.py:24
  42.9 0.6 shard_map.201
  43.5 1.9 collective-permute-start
  45.4 0.6 shard_map.200
  46.0 1.5 collective-permute-done
  47.5 1.0 add_convert_fusion
  48.6 7.2 %all-to-all-start.1 = ((bf16[16,80,256]{2,1,0:T(8,128)(2,1)}), bf16[16,80,256]{2,1,0:T(8,128)(2,1)S(1)}, u32[]{:S(2)}, u32[]{:S(2)}) async-start(bf16[16,80,256]{2,1,0:T(8,128)(2,1)} %add_convert_fusion), calls=%async_computation.1 | async-start | bytes 1310720 | tf_op jit(solution)/shard_map/all_to_all | solution.py:24
  55.9 13.1 %all-to-all-done.1.parts_ref = bf16[16,80,256]{2,1,0:T(8,128)(2,1)S(1)} async-done(((bf16[16,80,256]{2,1,0:T(8,128)(2,1)}), bf16[16,80,256]{2,1,0:T(8,128)(2,1)S(1)}, u32[]{:S(2)}, u32[]{:S(2)}) %all-to-all-start.1) | async-done | bytes 655392 | tf_op jit(solution)/shard_map/all_to_all | solution.py:24
  69.0 0.7 shard_map.202
  69.7 6.7 %all-to-all-start.2 = ((bf16[16,16,128]{2,1,0:T(8,128)(2,1)}), bf16[16,16,128]{2,1,0:T(8,128)(2,1)S(1)}, u32[]{:S(2)}, u32[]{:S(2)}) async-start(bf16[16,16,128]{2,1,0:T(8,128)(2,1)} %get-tuple-element.23), calls=%async_computation.2 | async-start | bytes 131072 | tf_op jit(solution)/shard_map/all_to_all | solution.py:24
  76.9 2.2 shard_map.203
  79.1 9.5 %all-to-all-done.2.bc_new_ref = bf16[16,16,128]{2,1,0:T(8,128)(2,1)S(1)} async-done(((bf16[16,16,128]{2,1,0:T(8,128)(2,1)}), bf16[16,16,128]{2,1,0:T(8,128)(2,1)S(1)}, u32[]{:S(2)}, u32[]{:S(2)}) %all-to-all-start.2) | async-done | bytes 65568 | tf_op jit(solution)/shard_map/all_to_all | solution.py:24
  88.6 0.8 shard_map.204
  89.5 15.6 %all_to_all.45.parts_ref = bf16[16,4,256]{2,1,0:T(4,128)(2,1)S(1)} all-to-all(bf16[16,4,256]{2,1,0:T(4,128)(2,1)S(1)} %shard_map.204), channel_id=1, replica_groups=mesh['row'=32,'col'=16] {'col'}, dimensions={0} | all-to-all | bytes 65536 | tf_op jit(solution)/shard_map/all_to_all | solution.py:24
  105.0 0.9 shard_map.205
  105.9 3.9 %all-to-all-start.4 = ((bf16[32,64,128]{2,1,0:T(8,128)(2,1)}), bf16[32,64,128]{2,1,0:T(8,128)(2,1)S(1)}, u32[]{:S(2)}, u32[]{:S(2)}) async-start(bf16[32,64,128]{2,1,0:T(8,128)(2,1)} %shard_map.205), calls=%async_computation.4 | async-start | bytes 1048576 | tf_op jit(solution)/shard_map/all_to_all | solution.py:24
  109.8 2.1 collective-permute-start.4
  111.9 2.3 collective-permute-start.5
  114.2 3.0 %shard_map.206.weight_ref = bf16[4,2048,256]{2,1,0:T(8,128)(2,1)S(1)} custom-call(bf16[16,4,128,256]{3,2,1,0:T(8,128)(2,1)} %bitcast.20), custom_call_target="tpu_custom_call" | custom-call | tf_op jit(solution)/shard_map/pallas_call | solution.py:466
  117.2 2.0 copy-done
  119.2 2.3 %all-to-all-done.4.heads_ref = bf16[32,64,128]{2,1,0:T(8,128)(2,1)S(1)} async-done(((bf16[32,64,128]{2,1,0:T(8,128)(2,1)}), bf16[32,64,128]{2,1,0:T(8,128)(2,1)S(1)}, u32[]{:S(2)}, u32[]{:S(2)}) %all-to-all-start.4) | async-done | bytes 524320 | tf_op jit(solution)/shard_map/all_to_all | solution.py:24
  121.5 2.2 copy-done.1
  123.7 0.8 shard_map.207
  124.5 2.0 collective-permute-start.1
  126.5 1.1 collective-permute-done.1.other_ref
  127.6 0.7 shard_map.208
  128.3 4.6 %all-to-all-start.5 = ((bf16[16,16,512]{2,1,0:T(8,128)(2,1)}), bf16[16,16,512]{2,1,0:T(8,128)(2,1)S(1)}, u32[]{:S(2)}, u32[]{:S(2)}) async-start(bf16[16,16,512]{2,1,0:T(8,128)(2,1)} %shard_map.208), calls=%async_computation.5 | async-start | bytes 524288 | tf_op jit(solution)/shard_map/all_to_all | solution.py:24
  132.9 1.9 collective-permute-start.3
  134.8 1.1 collective-permute-done.3.other_gain_ref
  136.0 15.8 %all-to-all-done.5.after_ref = bf16[16,16,512]{2,1,0:T(8,128)(2,1)S(1)} async-done(((bf16[16,16,512]{2,1,0:T(8,128)(2,1)}), bf16[16,16,512]{2,1,0:T(8,128)(2,1)S(1)}, u32[]{:S(2)}, u32[]{:S(2)}) %all-to-all-start.5) | async-done | bytes 262176 | tf_op jit(solution)/shard_map/all_to_all | solution.py:24
  151.8 0.7 shard_map.209
  152.5 21.7 %all_to_all.46.parts_ref = bf16[16,16,2176]{2,1,0:T(8,128)(2,1)S(1)} all-to-all(bf16[16,16,2176]{2,1,0:T(8,128)(2,1)S(1)} %shard_map.209), channel_id=1, replica_groups={{0,32,64,96,128,160,192,224,256,288,320,352,384,416,448,480},{16,48,80,..., dimensions={0} | all-to-all | bytes 2228224 | tf_op jit(solution)/shard_map/all_to_all | solution.py:24
  174.3 0.3 shard_map.210
  174.5 18.3 %all_to_all.47.act_ref = bf16[16,16,2048]{2,1,0:T(8,128)(2,1)S(1)} all-to-all(bf16[16,16,2048]{2,1,0:T(8,128)(2,1)S(1)} %shard_map.210), channel_id=1, replica_groups={{0,32,64,96,128,160,192,224,256,288,320,352,384,416,448,480},{16,48,80,..., dimensions={0} | all-to-all | bytes 2097152 | tf_op jit(solution)/shard_map/all_to_all | solution.py:24
  192.9 1.8 shard_map.212
  194.6 1.9 collective-permute-start.6
  196.6 0.5 shard_map.211.mine_ref
  197.1 0.8 collective-permute-done.6.other_ref
  197.9 0.7 shard_map.213
  198.6 8.0 %all-to-all-start.8 = ((bf16[16,32,256]{2,1,0:T(8,128)(2,1)}), bf16[16,32,256]{2,1,0:T(8,128)(2,1)S(1)}, u32[]{:S(2)}, u32[]{:S(2)}) async-start(bf16[16,32,256]{2,1,0:T(8,128)(2,1)} %shard_map.213), calls=%async_computation.8 | async-start | bytes 524288 | tf_op jit(solution)/shard_map/all_to_all | solution.py:24
  206.7 1.9 collective-permute-start.2
  208.6 16.4 %all-to-all-done.8 = bf16[16,32,256]{2,1,0:T(8,128)(2,1)S(1)} async-done(((bf16[16,32,256]{2,1,0:T(8,128)(2,1)}), bf16[16,32,256]{2,1,0:T(8,128)(2,1)S(1)}, u32[]{:S(2)}, u32[]{:S(2)}) %all-to-all-start.8) | async-done | bytes 262176 | tf_op jit(solution)/shard_map/all_to_all | solution.py:24
  225.0 0.6 add_convert_fusion.1
  (59 shorter events, 0.7 us)
Async XLA Ops:
  6.5 18.9 %copy-start.16 = (bf16[256,4,2]{0,2,1:T(2,128)(2,1)S(1)}, bf16[256,4,2]{0,2,1:T(2,128)(2,1)}, u32[]{:S(2)}) copy-start(bf16[256,4,2]{0,2,1:T(2,128)(2,1)} %param.25) | copy-start | bytes 12292
  6.5 18.9 %copy-start.14 = (bf16[256,4,32]{0,2,1:T(8,128)(2,1)S(1)}, bf16[256,4,32]{0,2,1:T(8,128)(2,1)}, u32[]{:S(2)}) copy-start(bf16[256,4,32]{0,2,1:T(8,128)(2,1)} %param.24) | copy-start | bytes 196612
  6.5 36.4 %copy-start.10 = (f32[256]{0:T(256)S(1)}, f32[256]{0:T(256)}, u32[]{:S(2)}) copy-start(f32[256]{0:T(256)} %param.22) | copy-start | bytes 3076
  6.5 99.3 %all-gather.3.cloned.1.call-start = ((), (), s32[]{:S(2)}) async-start(), calls=%async_computation.9 | async-start | bytes 4456448 | tf_op jit(solution)/shard_map/all_gather | solution.py:379
  7.3 0.7 copy-start.6
  8.7 34.2 %all-to-all-start = ((bf16[16,32,256]{2,1,0:T(8,128)(2,1)}), bf16[16,32,256]{2,1,0:T(8,128)(2,1)S(1)}, u32[]{:S(2)}, u32[]{:S(2)}) async-start(bf16[16,32,256]{2,1,0:T(8,128)(2,1)} %shard_map.199), calls=%async_computation | async-start | bytes 524288 | tf_op jit(solution)/shard_map/all_to_all | solution.py:24
  43.5 4.0 %collective-permute-start = (bf16[16,80,256]{2,1,0:T(8,128)(2,1)S(1)}, bf16[16,80,256]{2,1,0:T(8,128)(2,1)S(1)}, u32[]{:S(2)}, u32[]{:S(2)}) collective-permute-start(bf16[16,80,256]{2,1,0:T(8,128)(2,1)S(1)} %shard_map.201), channel_id=1, source_target_pairs={{0,16},{16,0},{32,48},{48,32},{64,80},{80,64},{96,112},{112,96},{1... | collective-permute-start | bytes 1966088 | tf_op jit(solution)/shard_map/ppermute | solution.py:388
  48.5 28.0 %copy-start.17 = (bf16[1,4,3,128]{3,1,2,0:T(4,128)(2,1)S(1)}, bf16[1,4,3,128]{3,1,2,0:T(4,128)(2,1)}, u32[]{:S(2)}) copy-start(bf16[1,4,3,128]{3,1,2,0:T(4,128)(2,1)} %param.31) | copy-start | bytes 9220
  48.5 28.0 %copy-start.15 = (bf16[1,4,3,512]{3,1,2,0:T(4,128)(2,1)S(1)}, bf16[1,4,3,512]{3,1,2,0:T(4,128)(2,1)}, u32[]{:S(2)}) copy-start(bf16[1,4,3,512]{3,1,2,0:T(4,128)(2,1)} %param.32) | copy-start | bytes 36868
  48.5 28.1 %copy-start.18 = (f32[4,2]{0,1:T(2,128)S(1)}, f32[4,2]{0,1:T(2,128)}, u32[]{:S(2)}) copy-start(f32[4,2]{0,1:T(2,128)} %param.26) | copy-start | bytes 100
  48.5 28.2 %copy-start.19 = (f32[4,2]{0,1:T(2,128)S(1)}, f32[4,2]{0,1:T(2,128)}, u32[]{:S(2)}) copy-start(f32[4,2]{0,1:T(2,128)} %param.27) | copy-start | bytes 100
  48.5 28.3 %copy-start.20 = (f32[4,2]{0,1:T(2,128)S(1)}, f32[4,2]{0,1:T(2,128)}, u32[]{:S(2)}) copy-start(f32[4,2]{0,1:T(2,128)} %param.28) | copy-start | bytes 100
  48.5 28.3 %copy-start.4 = (f32[1,4,2,64,256]{4,3,2,1,0:T(8,128)S(1)}, f32[1,4,2,64,256]{4,3,2,1,0:T(8,128)}, u32[]{:S(2)}) copy-start(f32[1,4,2,64,256]{4,3,2,1,0:T(8,128)} %state_ref.1) | copy-start | bytes 1572868
  48.5 28.3 %copy-start.5 = (s32[8,64,64]{2,1,0:T(8,128)S(1)}, s32[8,64,64]{2,1,0:T(8,128)}, u32[]{:S(2)}) copy-start(s32[8,64,64]{2,1,0:T(8,128)} %anc_ref.1) | copy-start | bytes 393220
  48.5 28.3 %copy-start.7 = (bf16[4,4,512]{2,1,0:T(4,128)(2,1)S(1)}, bf16[4,4,512]{2,1,0:T(4,128)(2,1)}, u32[]{:S(2)}) copy-start(bf16[4,4,512]{2,1,0:T(4,128)(2,1)} %bc_taps_ref.1) | copy-start | bytes 49156
  48.5 28.3 %copy-start.8 = (bf16[4,4,128]{2,1,0:T(4,128)(2,1)S(1)}, bf16[4,4,128]{2,1,0:T(4,128)(2,1)}, u32[]{:S(2)}) copy-start(bf16[4,4,128]{2,1,0:T(4,128)(2,1)} %x_taps_ref.1) | copy-start | bytes 12292
  48.5 28.3 %copy-start.9 = (s32[8,64]{1,0:T(8,128)S(1)}, s32[8,64]{1,0:T(8,128)}, u32[]{:S(2)}) copy-start(s32[8,64]{1,0:T(8,128)} %parents_ref.1) | copy-start | bytes 6148
  48.5 28.3 %copy-start.11 = (f32[4,128]{1,0:T(4,128)S(1)}, f32[4,128]{1,0:T(4,128)}, u32[]{:S(2)}) copy-start(f32[4,128]{1,0:T(4,128)} %gain_ref.1) | copy-start | bytes 6148
  48.6 28.3 %copy-start.13 = (s32[8]{0:T(128)S(1)}, s32[8]{0:T(128)}, u32[]{:S(2)}) copy-start(s32[8]{0:T(128)} %slot_ref.1) | copy-start | bytes 100
  48.6 20.4 %all-to-all-start.1 = ((bf16[16,80,256]{2,1,0:T(8,128)(2,1)}), bf16[16,80,256]{2,1,0:T(8,128)(2,1)S(1)}, u32[]{:S(2)}, u32[]{:S(2)}) async-start(bf16[16,80,256]{2,1,0:T(8,128)(2,1)} %add_convert_fusion), calls=%async_computation.1 | async-start | bytes 1310720 | tf_op jit(solution)/shard_map/all_to_all | solution.py:24
  69.7 18.9 %all-to-all-start.2 = ((bf16[16,16,128]{2,1,0:T(8,128)(2,1)}), bf16[16,16,128]{2,1,0:T(8,128)(2,1)S(1)}, u32[]{:S(2)}, u32[]{:S(2)}) async-start(bf16[16,16,128]{2,1,0:T(8,128)(2,1)} %get-tuple-element.23), calls=%async_computation.2 | async-start | bytes 131072 | tf_op jit(solution)/shard_map/all_to_all | solution.py:24
  79.1 30.7 %copy-start.2 = (bf16[256,2048]{1,0:T(8,128)(2,1)S(1)}, bf16[256,2048]{1,0:T(8,128)(2,1)}, u32[]{:S(2)}) copy-start(bf16[256,2048]{1,0:T(8,128)(2,1)} %weight_ref) | copy-start | bytes 3145732
  105.9 15.7 %all-to-all-start.4 = ((bf16[32,64,128]{2,1,0:T(8,128)(2,1)}), bf16[32,64,128]{2,1,0:T(8,128)(2,1)S(1)}, u32[]{:S(2)}, u32[]{:S(2)}) async-start(bf16[32,64,128]{2,1,0:T(8,128)(2,1)} %shard_map.205), calls=%async_computation.4 | async-start | bytes 1048576 | tf_op jit(solution)/shard_map/all_to_all | solution.py:24
  109.8 26.2 %collective-permute-start.4 = (bf16[256,2048]{1,0:T(8,128)(2,1)S(1)}, bf16[256,2048]{1,0:T(8,128)(2,1)S(1)}, u32[]{:S(2)}, u32[]{:S(2)}) collective-permute-start(bf16[256,2048]{1,0:T(8,128)(2,1)S(1)} %copy-done.2), channel_id=1, source_target_pairs={{0,16},{16,0},{32,48},{48,32},{64,80},{80,64},{96,112},{112,96},{1... | collective-permute-start | bytes 3145736 | tf_op jit(solution)/shard_map/ppermute | solution.py:454
  111.9 40.6 %collective-permute-start.5 = (bf16[2048,256]{1,0:T(8,128)(2,1)}, bf16[2048,256]{1,0:T(8,128)(2,1)}, u32[]{:S(2)}, u32[]{:S(2)}) collective-permute-start(bf16[2048,256]{1,0:T(8,128)(2,1)} %weight_ref.1), channel_id=1, source_target_pairs={{0,16},{16,0},{32,48},{48,32},{64,80},{80,64},{96,112},{112,96},{1... | collective-permute-start | bytes 3145736 | tf_op jit(solution)/shard_map/ppermute | solution.py:454
  117.2 2.0 copy-start
  121.5 2.2 copy-start.1
  123.7 9.2 %copy-start.12 = (f32[256]{0:T(256)S(1)}, f32[256]{0:T(256)}, u32[]{:S(2)}) copy-start(f32[256]{0:T(256)} %param.39) | copy-start | bytes 3076
  124.5 3.1 %collective-permute-start.1 = (bf16[16,256]{1,0:T(8,128)(2,1)S(1)}, bf16[16,256]{1,0:T(8,128)(2,1)S(1)}, u32[]{:S(2)}, u32[]{:S(2)}) collective-permute-start(bf16[16,256]{1,0:T(8,128)(2,1)S(1)} %get-tuple-element.31), channel_id=1, source_target_pairs={{0,16},{16,0},{32,48},{48,32},{64,80},{80,64},{96,112},{112,96},{1... | collective-permute-start | bytes 24584 | tf_op jit(solution)/shard_map/ppermute | solution.py:488
  128.3 23.5 %all-to-all-start.5 = ((bf16[16,16,512]{2,1,0:T(8,128)(2,1)}), bf16[16,16,512]{2,1,0:T(8,128)(2,1)S(1)}, u32[]{:S(2)}, u32[]{:S(2)}) async-start(bf16[16,16,512]{2,1,0:T(8,128)(2,1)} %shard_map.208), calls=%async_computation.5 | async-start | bytes 524288 | tf_op jit(solution)/shard_map/all_to_all | solution.py:24
  132.9 3.0 %collective-permute-start.3 = (f32[1,256]{1,0:T(1,128)S(1)}, f32[1,256]{1,0:T(1,128)S(1)}, u32[]{:S(2)}, u32[]{:S(2)}) collective-permute-start(f32[1,256]{1,0:T(1,128)S(1)} %bitcast.18), channel_id=1, source_target_pairs={{0,16},{16,0},{32,48},{48,32},{64,80},{80,64},{96,112},{112,96},{1... | collective-permute-start | bytes 3080 | tf_op jit(solution)/shard_map/ppermute | solution.py:454
  192.9 3.7 %copy-start.3 = (bf16[2048,256]{1,0:T(8,128)(2,1)S(1)}, bf16[2048,256]{1,0:T(8,128)(2,1)}, u32[]{:S(2)}) copy-start(bf16[2048,256]{1,0:T(8,128)(2,1)} %weight_ref.1) | copy-start | bytes 3145732
  194.6 3.2 %collective-permute-start.6 = (bf16[8,32,256]{2,1,0:T(8,128)(2,1)S(1)}, bf16[8,32,256]{2,1,0:T(8,128)(2,1)S(1)}, u32[]{:S(2)}, u32[]{:S(2)}) collective-permute-start(bf16[8,32,256]{2,1,0:T(8,128)(2,1)S(1)} %shard_map.212), channel_id=1, source_target_pairs={{0,16},{16,0},{32,48},{48,32},{64,80},{80,64},{96,112},{112,96},{1... | collective-permute-start | bytes 393224 | tf_op jit(solution)/shard_map/ppermute | solution.py:520
  198.6 26.4 %all-to-all-start.8 = ((bf16[16,32,256]{2,1,0:T(8,128)(2,1)}), bf16[16,32,256]{2,1,0:T(8,128)(2,1)S(1)}, u32[]{:S(2)}, u32[]{:S(2)}) async-start(bf16[16,32,256]{2,1,0:T(8,128)(2,1)} %shard_map.213), calls=%async_computation.8 | async-start | bytes 524288 | tf_op jit(solution)/shard_map/all_to_all | solution.py:24
  206.7 18.4 %collective-permute-start.2 = (bf16[32,256]{1,0:T(8,128)(2,1)S(1)}, bf16[32,256]{1,0:T(8,128)(2,1)S(1)}, u32[]{:S(2)}, u32[]{:S(2)}) collective-permute-start(bf16[32,256]{1,0:T(8,128)(2,1)S(1)} %slice.9), channel_id=1, source_target_pairs={{0,16},{16,0},{32,48},{48,32},{64,80},{80,64},{96,112},{112,96},{1... | collective-permute-start | bytes 49160 | tf_op jit(solution)/shard_map/ppermute | solution.py:532
Sparse Core Ops, SparseCore 0:
  9.4 88.3 all-gather.2

commit v8 on v7

--- a/solution.py
+++ b/solution.py
@@ -264,10 +264,6 @@
         out_ref[row] = heads
 
 
-def by_group_kernel(weight_ref, out_ref):
-    out_ref[0] = weight_ref[...].reshape(-1, 256)
-
-
 def out_kernel(parity_ref, heads_ref, weight_ref, residual_ref, mine_ref, other_ref, left_ref):
     total = residual_ref[...].astype(F32)
     for group in range(G):
@@ -278,7 +274,8 @@
                     col * 4 : col * 4 + 4, :
                 ]
         left = left_ref[...].astype(BF16)
-        total = total + jnp.dot(left, weight_ref[group], preferred_element_type=F32)
+        weight = weight_ref[:, group].reshape(-1, 256)
+        total = total + jnp.dot(left, weight, preferred_element_type=F32)
     after = total.astype(BF16)
     first = parity_ref[0] == 0
     mine_ref[...] = jnp.where(first, after[0:16, :], after[16:32, :])
@@ -324,15 +321,36 @@
             out_ref[part, :, lanes] = act
 
 
-def down_kernel(act_ref, weight_ref, out_ref, turn_ref):
-    term = jnp.dot(act_ref[...].reshape(256, -1), weight_ref[...], preferred_element_type=F32)
+def turn(term, turn_ref):
     for col in range(16):
         for request in range(4):
             start = col * 16 + request * 4
             turn_ref[2 * request + col // 8, col % 8 * 4 : col % 8 * 4 + 4, :] = term[
                 start : start + 4, :
             ]
-    out_ref[...] = turn_ref[...].astype(BF16)
+    return turn_ref[...].astype(BF16)
+
+
+def down_mine_kernel(act_ref, weight_ref, out_ref, turn_ref):
+    act = act_ref[...].reshape(256, -1)
+    out_ref[...] = turn(jnp.dot(act, weight_ref[...], preferred_element_type=F32), turn_ref)
+
+
+def down_other_kernel(act_ref, far_ref, out_ref, turn_ref, weight_ref, done_ref):
+    copies = [
+        pltpu.make_async_copy(
+            far_ref.at[pl.ds(part * 512, 512)], weight_ref.at[part], done_ref.at[part]
+        )
+        for part in range(4)
+    ]
+    for copy in copies:
+        copy.start()
+    term = jnp.zeros((256, 256), F32)
+    for part in range(4):
+        act = act_ref[:, :, part * 512 : (part + 1) * 512].reshape(256, 512)
+        copies[part].wait()
+        term = term + jnp.dot(act, weight_ref[part], preferred_element_type=F32)
+    out_ref[...] = turn(term, turn_ref)
 
 
 def join_kernel(parity_ref, mine_ref, other_ref, out_ref):
@@ -374,6 +392,7 @@
     halves = [[row for row in range(rows) if row % 2 == half] for half in range(2)]
     smem = pl.BlockSpec(memory_space=pltpu.SMEM)
     vmem = pl.BlockSpec(memory_space=pltpu.VMEM)
+    hbm = pl.BlockSpec(memory_space=pltpu.HBM)
     params = pltpu.CompilerParams(vmem_limit_bytes=VMEM_LIMIT)
 
     out_weights = lax.all_gather(out_proj, "col", axis=0, tiled=False)
@@ -462,15 +481,6 @@
 
     mixed = exchange(mixed, "col")
     heads = call(scale_heads_kernel, jax.ShapeDtypeStruct((rows, cols * 4, 128), BF16), mixed)
-    heads, out_weights = lax.optimization_barrier((heads, out_weights))
-    out_weights = pl.pallas_call(
-        by_group_kernel,
-        grid=(G,),
-        out_shape=jax.ShapeDtypeStruct((G, cols * 128, 256), BF16),
-        in_specs=[pl.BlockSpec((cols, 1, 128, 256), lambda group: (0, group, 0, 0))],
-        out_specs=pl.BlockSpec((1, cols * 128, 256), lambda group: (group, 0, 0)),
-        compiler_params=params,
-    )(out_weights)
     heads = exchange(heads, "row")
     residual = lax.dynamic_slice(
         hidden.reshape(8, 64, 256), (0, 4 * col_index, 0), (8, 4, 256)
@@ -509,22 +519,36 @@
     act = call(act_kernel, jax.ShapeDtypeStruct((16, 16, 2048), BF16), up_parts)
     act = exchange(act, "row", halves)
 
-    def down_half(weight):
-        return pl.pallas_call(
-            down_kernel,
-            out_shape=jax.ShapeDtypeStruct((8, 32, 256), BF16),
-            scratch_shapes=[pltpu.VMEM((8, 32, 256), F32)],
-            compiler_params=params,
-        )(act, weight)
-
-    from_other = lax.ppermute(down_half(down_other), "row", swap)
+    down_shape = jax.ShapeDtypeStruct((8, 32, 256), BF16)
+    turn_shape = pltpu.VMEM((8, 32, 256), F32)
+    for_other = pl.pallas_call(
+        down_other_kernel,
+        out_shape=down_shape,
+        in_specs=[vmem, hbm],
+        out_specs=vmem,
+        scratch_shapes=[
+            turn_shape,
+            pltpu.VMEM((4, 512, 256), BF16),
+            pltpu.SemaphoreType.DMA((4,)),
+        ],
+        compiler_params=params,
+    )(act, down_other)
+    from_other = lax.ppermute(for_other, "row", swap)
+    for_mine = pl.pallas_call(
+        down_mine_kernel,
+        out_shape=down_shape,
+        in_specs=[vmem, vmem],
+        out_specs=vmem,
+        scratch_shapes=[turn_shape],
+        compiler_params=params,
+    )(act, down_mine)
     down = pl.pallas_call(
         join_kernel,
         out_shape=jax.ShapeDtypeStruct((cols, 32, 256), BF16),
         in_specs=[smem, vmem, vmem],
         out_specs=vmem,
         compiler_params=params,
-    )(parity, down_half(down_mine), from_other)
+    )(parity, for_mine, from_other)
     ffn_out = jnp.sum(exchange(down, "col").astype(F32), axis=0)
     own = lax.dynamic_slice(
         after, (8 * (col_index % 2), 4 * (col_index // 2 % 4), 0), (8, 4, 512)

time: 234 us -> 233 us (level)
  waiting for transfers between devices: 79.9 us -> 85 us
  Pallas kernels: 14.9 us -> 12.2 us
    all_to_all x6, waiting for transfers between devices: 74.6 us -> 79.7 us  [exchange(): lax.all_to_all(parts, axis, 0, 0, tiled=True, axis_index_groups=groups)]
    pallas_call x3 -> x2, Pallas kernels: 5.26 us -> 2.55 us  [the longest x1 2.09 us: local(): pl.pallas_call(down_other_kernel, out_shape=down_shape, in_specs=[vmem, h...]
    unnamed x47 -> x45, local copies, waits for them, and re-layouts: 5.25 us -> 3.28 us
  transfers between devices with their start and end apart: 14 -> 14, of which waited for: 10 -> 10; matrix products, arithmetic and copies ran while one was open for 1% -> 1% of each run, Pallas kernels for 5% -> 4%
where the time goes in v8:
time: 233 us; the launch traced here: 231 us
  waiting for transfers between devices  85 us (36%)
  starting transfers between devices  59 us (25%)
  blocking collectives  54.8 us (24%)
  between operations  13.8 us (6%)
  Pallas kernels  12.2 us (5%)
  local copies, waits for them, and re-layouts  4.83 us (2%)
    all_to_all x6, waiting for transfers between devices, exchange(): lax.all_to_all(parts, axis, 0, 0, tiled=True, axis_index_groups=groups)  79.7 us
    all_to_all x3, blocking collectives, exchange(): lax.all_to_all(parts, axis, 0, 0, tiled=True, axis_index_groups=groups)  54.8 us
    all_to_all x6, starting transfers between devices, exchange(): lax.all_to_all(parts, axis, 0, 0, tiled=True, axis_index_groups=groups)  45 us
    ppermute x3, starting transfers between devices, local(): lax.ppermute(weight, 'row', swap)  6.25 us
  transfers between devices with their start and end apart: 14, of which 10 were waited for; matrix products, arithmetic and copies ran while one was open for 1% of the time, Pallas kernels for 4%

profile of v8, /device:TPU:32, one launch (start us, length us, event | category | flops | bytes accessed | tf_op | source)
XLA Modules:
  0.0 231.5 jit_solution(9856648977589319520)
XLA Ops:
  6.5 0.7 all-gather.3.cloned.1.call-update
  7.3 0.7 copy-done.5
  8.0 0.7 shard_map.199
  8.7 15.2 %all-to-all-start = ((bf16[16,32,256]{2,1,0:T(8,128)(2,1)}), bf16[16,32,256]{2,1,0:T(8,128)(2,1)S(1)}, u32[]{:S(2)}, u32[]{:S(2)}) async-start(bf16[16,32,256]{2,1,0:T(8,128)(2,1)} %shard_map.199), calls=%async_computation | async-start | bytes 524288 | tf_op jit(solution)/shard_map/all_to_all | solution.py:24
  23.9 1.4 reshape.20.main_ref
  25.5 17.4 %all-to-all-done = bf16[16,32,256]{2,1,0:T(8,128)(2,1)S(1)} async-done(((bf16[16,32,256]{2,1,0:T(8,128)(2,1)}), bf16[16,32,256]{2,1,0:T(8,128)(2,1)S(1)}, u32[]{:S(2)}, u32[]{:S(2)}) %all-to-all-start) | async-done | bytes 262176 | tf_op jit(solution)/shard_map/all_to_all | solution.py:24
  42.9 0.6 shard_map.201
  43.5 1.9 collective-permute-start
  45.4 0.6 shard_map.200
  46.0 1.5 collective-permute-done
  47.5 1.0 add_convert_fusion
  48.6 7.2 %all-to-all-start.1 = ((bf16[16,80,256]{2,1,0:T(8,128)(2,1)}), bf16[16,80,256]{2,1,0:T(8,128)(2,1)S(1)}, u32[]{:S(2)}, u32[]{:S(2)}) async-start(bf16[16,80,256]{2,1,0:T(8,128)(2,1)} %add_convert_fusion), calls=%async_computation.1 | async-start | bytes 1310720 | tf_op jit(solution)/shard_map/all_to_all | solution.py:24
  55.9 13.1 %all-to-all-done.1.parts_ref = bf16[16,80,256]{2,1,0:T(8,128)(2,1)S(1)} async-done(((bf16[16,80,256]{2,1,0:T(8,128)(2,1)}), bf16[16,80,256]{2,1,0:T(8,128)(2,1)S(1)}, u32[]{:S(2)}, u32[]{:S(2)}) %all-to-all-start.1) | async-done | bytes 655392 | tf_op jit(solution)/shard_map/all_to_all | solution.py:24
  69.0 0.7 shard_map.202
  69.8 6.7 %all-to-all-start.2 = ((bf16[16,16,128]{2,1,0:T(8,128)(2,1)}), bf16[16,16,128]{2,1,0:T(8,128)(2,1)S(1)}, u32[]{:S(2)}, u32[]{:S(2)}) async-start(bf16[16,16,128]{2,1,0:T(8,128)(2,1)} %get-tuple-element.21), calls=%async_computation.2 | async-start | bytes 131072 | tf_op jit(solution)/shard_map/all_to_all | solution.py:24
  76.6 0.1 copy.29.offset_ref
  76.6 0.1 copy.30.rate_ref
  76.9 2.2 shard_map.203
  79.1 9.6 %all-to-all-done.2.bc_new_ref = bf16[16,16,128]{2,1,0:T(8,128)(2,1)S(1)} async-done(((bf16[16,16,128]{2,1,0:T(8,128)(2,1)}), bf16[16,16,128]{2,1,0:T(8,128)(2,1)S(1)}, u32[]{:S(2)}, u32[]{:S(2)}) %all-to-all-start.2) | async-done | bytes 65568 | tf_op jit(solution)/shard_map/all_to_all | solution.py:24
  88.8 0.8 shard_map.204
  89.6 15.4 %all_to_all.45.parts_ref = bf16[16,4,256]{2,1,0:T(4,128)(2,1)S(1)} all-to-all(bf16[16,4,256]{2,1,0:T(4,128)(2,1)S(1)} %shard_map.204), channel_id=1, replica_groups=mesh['row'=32,'col'=16] {'col'}, dimensions={0} | all-to-all | bytes 65536 | tf_op jit(solution)/shard_map/all_to_all | solution.py:24
  105.0 0.9 shard_map.205
  105.9 3.9 %all-to-all-start.4 = ((bf16[32,64,128]{2,1,0:T(8,128)(2,1)}), bf16[32,64,128]{2,1,0:T(8,128)(2,1)S(1)}, u32[]{:S(2)}, u32[]{:S(2)}) async-start(bf16[32,64,128]{2,1,0:T(8,128)(2,1)} %shard_map.205), calls=%async_computation.4 | async-start | bytes 1048576 | tf_op jit(solution)/shard_map/all_to_all | solution.py:24
  109.8 2.1 collective-permute-start.4
  111.9 2.3 collective-permute-start.5
  114.2 7.4 %all-to-all-done.4.heads_ref = bf16[32,64,128]{2,1,0:T(8,128)(2,1)S(1)} async-done(((bf16[32,64,128]{2,1,0:T(8,128)(2,1)}), bf16[32,64,128]{2,1,0:T(8,128)(2,1)S(1)}, u32[]{:S(2)}, u32[]{:S(2)}) %all-to-all-start.4) | async-done | bytes 524320 | tf_op jit(solution)/shard_map/all_to_all | solution.py:24
  121.6 2.2 copy-done
  123.8 0.8 shard_map.206
  124.6 2.0 collective-permute-start.1
  126.5 1.1 collective-permute-done.1.other_ref
  127.6 0.7 shard_map.207
  128.3 4.6 %all-to-all-start.5 = ((bf16[16,16,512]{2,1,0:T(8,128)(2,1)}), bf16[16,16,512]{2,1,0:T(8,128)(2,1)S(1)}, u32[]{:S(2)}, u32[]{:S(2)}) async-start(bf16[16,16,512]{2,1,0:T(8,128)(2,1)} %shard_map.207), calls=%async_computation.5 | async-start | bytes 524288 | tf_op jit(solution)/shard_map/all_to_all | solution.py:24
  132.9 1.9 collective-permute-start.3
  134.9 1.1 collective-permute-done.3.other_gain_ref
  136.0 15.8 %all-to-all-done.5.after_ref = bf16[16,16,512]{2,1,0:T(8,128)(2,1)S(1)} async-done(((bf16[16,16,512]{2,1,0:T(8,128)(2,1)}), bf16[16,16,512]{2,1,0:T(8,128)(2,1)S(1)}, u32[]{:S(2)}, u32[]{:S(2)}) %all-to-all-start.5) | async-done | bytes 262176 | tf_op jit(solution)/shard_map/all_to_all | solution.py:24
  151.8 0.7 shard_map.208
  152.5 20.6 %all_to_all.46.parts_ref = bf16[16,16,2176]{2,1,0:T(8,128)(2,1)S(1)} all-to-all(bf16[16,16,2176]{2,1,0:T(8,128)(2,1)S(1)} %shard_map.208), channel_id=1, replica_groups={{0,32,64,96,128,160,192,224,256,288,320,352,384,416,448,480},{16,48,80,..., dimensions={0} | all-to-all | bytes 2228224 | tf_op jit(solution)/shard_map/all_to_all | solution.py:24
  173.1 0.3 shard_map.209
  173.4 18.8 %all_to_all.47.act_ref = bf16[16,16,2048]{2,1,0:T(8,128)(2,1)S(1)} all-to-all(bf16[16,16,2048]{2,1,0:T(8,128)(2,1)S(1)} %shard_map.209), channel_id=1, replica_groups={{0,32,64,96,128,160,192,224,256,288,320,352,384,416,448,480},{16,48,80,..., dimensions={0} | all-to-all | bytes 2097152 | tf_op jit(solution)/shard_map/all_to_all | solution.py:24
  192.2 2.1 shard_map.211
  194.3 1.9 collective-permute-start.6
  196.2 0.5 shard_map.210.mine_ref
  196.7 0.8 collective-permute-done.6.other_ref
  197.5 0.7 shard_map.212
  198.2 7.4 %all-to-all-start.8 = ((bf16[16,32,256]{2,1,0:T(8,128)(2,1)}), bf16[16,32,256]{2,1,0:T(8,128)(2,1)S(1)}, u32[]{:S(2)}, u32[]{:S(2)}) async-start(bf16[16,32,256]{2,1,0:T(8,128)(2,1)} %shard_map.212), calls=%async_computation.8 | async-start | bytes 524288 | tf_op jit(solution)/shard_map/all_to_all | solution.py:24
  205.7 1.9 collective-permute-start.2
  207.6 16.4 %all-to-all-done.8 = bf16[16,32,256]{2,1,0:T(8,128)(2,1)S(1)} async-done(((bf16[16,32,256]{2,1,0:T(8,128)(2,1)}), bf16[16,32,256]{2,1,0:T(8,128)(2,1)S(1)}, u32[]{:S(2)}, u32[]{:S(2)}) %all-to-all-start.8) | async-done | bytes 262176 | tf_op jit(solution)/shard_map/all_to_all | solution.py:24
  224.0 0.6 add_convert_fusion.1
  (56 shorter events, 0.6 us)
Async XLA Ops:
  6.5 18.9 %copy-start.13 = (bf16[256,4,32]{0,2,1:T(8,128)(2,1)S(1)}, bf16[256,4,32]{0,2,1:T(8,128)(2,1)}, u32[]{:S(2)}) copy-start(bf16[256,4,32]{0,2,1:T(8,128)(2,1)} %param.24) | copy-start | bytes 196612
  6.5 18.9 %copy-start.15 = (bf16[256,4,2]{0,2,1:T(2,128)(2,1)S(1)}, bf16[256,4,2]{0,2,1:T(2,128)(2,1)}, u32[]{:S(2)}) copy-start(bf16[256,4,2]{0,2,1:T(2,128)(2,1)} %param.25) | copy-start | bytes 12292
  6.5 36.4 %copy-start.9 = (f32[256]{0:T(256)S(1)}, f32[256]{0:T(256)}, u32[]{:S(2)}) copy-start(f32[256]{0:T(256)} %param.22) | copy-start | bytes 3076
  6.5 115.0 %all-gather.3.cloned.1.call-start = ((), (), s32[]{:S(2)}) async-start(), calls=%async_computation.9 | async-start | bytes 4456448 | tf_op jit(solution)/shard_map/all_gather | solution.py:398
  7.3 0.7 copy-start.5
  8.7 34.2 %all-to-all-start = ((bf16[16,32,256]{2,1,0:T(8,128)(2,1)}), bf16[16,32,256]{2,1,0:T(8,128)(2,1)S(1)}, u32[]{:S(2)}, u32[]{:S(2)}) async-start(bf16[16,32,256]{2,1,0:T(8,128)(2,1)} %shard_map.199), calls=%async_computation | async-start | bytes 524288 | tf_op jit(solution)/shard_map/all_to_all | solution.py:24
  43.5 4.0 %collective-permute-start = (bf16[16,80,256]{2,1,0:T(8,128)(2,1)S(1)}, bf16[16,80,256]{2,1,0:T(8,128)(2,1)S(1)}, u32[]{:S(2)}, u32[]{:S(2)}) collective-permute-start(bf16[16,80,256]{2,1,0:T(8,128)(2,1)S(1)} %shard_map.201), channel_id=1, source_target_pairs={{0,16},{16,0},{32,48},{48,32},{64,80},{80,64},{96,112},{112,96},{1... | collective-permute-start | bytes 1966088 | tf_op jit(solution)/shard_map/ppermute | solution.py:407
  48.5 28.0 %copy-start.14 = (bf16[1,4,3,512]{3,1,2,0:T(4,128)(2,1)S(1)}, bf16[1,4,3,512]{3,1,2,0:T(4,128)(2,1)}, u32[]{:S(2)}) copy-start(bf16[1,4,3,512]{3,1,2,0:T(4,128)(2,1)} %param.32) | copy-start | bytes 36868
  48.5 28.1 %copy-start.16 = (bf16[1,4,3,128]{3,1,2,0:T(4,128)(2,1)S(1)}, bf16[1,4,3,128]{3,1,2,0:T(4,128)(2,1)}, u32[]{:S(2)}) copy-start(bf16[1,4,3,128]{3,1,2,0:T(4,128)(2,1)} %param.31) | copy-start | bytes 9220
  48.5 28.1 %copy-start.17 = (f32[4,2]{0,1:T(2,128)S(1)}, f32[4,2]{0,1:T(2,128)}, u32[]{:S(2)}) copy-start(f32[4,2]{0,1:T(2,128)} %param.26) | copy-start | bytes 100
  48.5 28.2 %copy-start.18 = (f32[4,2]{0,1:T(2,128)S(1)}, f32[4,2]{0,1:T(2,128)}, u32[]{:S(2)}) copy-start(f32[4,2]{0,1:T(2,128)} %param.27) | copy-start | bytes 100
  48.5 28.3 %copy-start.19 = (f32[4,2]{0,1:T(2,128)S(1)}, f32[4,2]{0,1:T(2,128)}, u32[]{:S(2)}) copy-start(f32[4,2]{0,1:T(2,128)} %param.28) | copy-start | bytes 100
  48.5 28.3 %copy-start.3 = (f32[1,4,2,64,256]{4,3,2,1,0:T(8,128)S(1)}, f32[1,4,2,64,256]{4,3,2,1,0:T(8,128)}, u32[]{:S(2)}) copy-start(f32[1,4,2,64,256]{4,3,2,1,0:T(8,128)} %state_ref.1) | copy-start | bytes 1572868
  48.5 28.3 %copy-start.4 = (s32[8,64,64]{2,1,0:T(8,128)S(1)}, s32[8,64,64]{2,1,0:T(8,128)}, u32[]{:S(2)}) copy-start(s32[8,64,64]{2,1,0:T(8,128)} %anc_ref.1) | copy-start | bytes 393220
  48.5 28.3 %copy-start.6 = (bf16[4,4,512]{2,1,0:T(4,128)(2,1)S(1)}, bf16[4,4,512]{2,1,0:T(4,128)(2,1)}, u32[]{:S(2)}) copy-start(bf16[4,4,512]{2,1,0:T(4,128)(2,1)} %bc_taps_ref.1) | copy-start | bytes 49156
  48.5 28.3 %copy-start.7 = (bf16[4,4,128]{2,1,0:T(4,128)(2,1)S(1)}, bf16[4,4,128]{2,1,0:T(4,128)(2,1)}, u32[]{:S(2)}) copy-start(bf16[4,4,128]{2,1,0:T(4,128)(2,1)} %x_taps_ref.1) | copy-start | bytes 12292
  48.5 28.3 %copy-start.8 = (s32[8,64]{1,0:T(8,128)S(1)}, s32[8,64]{1,0:T(8,128)}, u32[]{:S(2)}) copy-start(s32[8,64]{1,0:T(8,128)} %parents_ref.1) | copy-start | bytes 6148
  48.6 28.3 %copy-start.10 = (f32[4,128]{1,0:T(4,128)S(1)}, f32[4,128]{1,0:T(4,128)}, u32[]{:S(2)}) copy-start(f32[4,128]{1,0:T(4,128)} %gain_ref.1) | copy-start | bytes 6148
  48.6 28.3 %copy-start.12 = (s32[8]{0:T(128)S(1)}, s32[8]{0:T(128)}, u32[]{:S(2)}) copy-start(s32[8]{0:T(128)} %slot_ref.1) | copy-start | bytes 100
  48.6 20.5 %all-to-all-start.1 = ((bf16[16,80,256]{2,1,0:T(8,128)(2,1)}), bf16[16,80,256]{2,1,0:T(8,128)(2,1)S(1)}, u32[]{:S(2)}, u32[]{:S(2)}) async-start(bf16[16,80,256]{2,1,0:T(8,128)(2,1)} %add_convert_fusion), calls=%async_computation.1 | async-start | bytes 1310720 | tf_op jit(solution)/shard_map/all_to_all | solution.py:24
  69.8 19.0 %all-to-all-start.2 = ((bf16[16,16,128]{2,1,0:T(8,128)(2,1)}), bf16[16,16,128]{2,1,0:T(8,128)(2,1)S(1)}, u32[]{:S(2)}, u32[]{:S(2)}) async-start(bf16[16,16,128]{2,1,0:T(8,128)(2,1)} %get-tuple-element.21), calls=%async_computation.2 | async-start | bytes 131072 | tf_op jit(solution)/shard_map/all_to_all | solution.py:24
  79.1 30.7 %copy-start.1 = (bf16[256,2048]{1,0:T(8,128)(2,1)S(1)}, bf16[256,2048]{1,0:T(8,128)(2,1)}, u32[]{:S(2)}) copy-start(bf16[256,2048]{1,0:T(8,128)(2,1)} %weight_ref) | copy-start | bytes 3145732
  105.9 15.7 %all-to-all-start.4 = ((bf16[32,64,128]{2,1,0:T(8,128)(2,1)}), bf16[32,64,128]{2,1,0:T(8,128)(2,1)S(1)}, u32[]{:S(2)}, u32[]{:S(2)}) async-start(bf16[32,64,128]{2,1,0:T(8,128)(2,1)} %shard_map.205), calls=%async_computation.4 | async-start | bytes 1048576 | tf_op jit(solution)/shard_map/all_to_all | solution.py:24
  109.8 26.1 %collective-permute-start.4 = (bf16[256,2048]{1,0:T(8,128)(2,1)S(1)}, bf16[256,2048]{1,0:T(8,128)(2,1)S(1)}, u32[]{:S(2)}, u32[]{:S(2)}) collective-permute-start(bf16[256,2048]{1,0:T(8,128)(2,1)S(1)} %copy-done.1), channel_id=1, source_target_pairs={{0,16},{16,0},{32,48},{48,32},{64,80},{80,64},{96,112},{112,96},{1... | collective-permute-start | bytes 3145736 | tf_op jit(solution)/shard_map/ppermute | solution.py:473
  111.9 40.6 %collective-permute-start.5 = (bf16[2048,256]{1,0:T(8,128)(2,1)}, bf16[2048,256]{1,0:T(8,128)(2,1)}, u32[]{:S(2)}, u32[]{:S(2)}) collective-permute-start(bf16[2048,256]{1,0:T(8,128)(2,1)} %weight_ref.1), channel_id=1, source_target_pairs={{0,16},{16,0},{32,48},{48,32},{64,80},{80,64},{96,112},{112,96},{1... | collective-permute-start | bytes 3145736 | tf_op jit(solution)/shard_map/ppermute | solution.py:473
  121.6 2.2 copy-start
  123.8 9.2 %copy-start.11 = (f32[256]{0:T(256)S(1)}, f32[256]{0:T(256)}, u32[]{:S(2)}) copy-start(f32[256]{0:T(256)} %param.39) | copy-start | bytes 3076
  124.6 3.1 %collective-permute-start.1 = (bf16[16,256]{1,0:T(8,128)(2,1)S(1)}, bf16[16,256]{1,0:T(8,128)(2,1)S(1)}, u32[]{:S(2)}, u32[]{:S(2)}) collective-permute-start(bf16[16,256]{1,0:T(8,128)(2,1)S(1)} %get-tuple-element.27), channel_id=1, source_target_pairs={{0,16},{16,0},{32,48},{48,32},{64,80},{80,64},{96,112},{112,96},{1... | collective-permute-start | bytes 24584 | tf_op jit(solution)/shard_map/ppermute | solution.py:498
  128.3 23.4 %all-to-all-start.5 = ((bf16[16,16,512]{2,1,0:T(8,128)(2,1)}), bf16[16,16,512]{2,1,0:T(8,128)(2,1)S(1)}, u32[]{:S(2)}, u32[]{:S(2)}) async-start(bf16[16,16,512]{2,1,0:T(8,128)(2,1)} %shard_map.207), calls=%async_computation.5 | async-start | bytes 524288 | tf_op jit(solution)/shard_map/all_to_all | solution.py:24
  132.9 3.0 %collective-permute-start.3 = (f32[1,256]{1,0:T(1,128)S(1)}, f32[1,256]{1,0:T(1,128)S(1)}, u32[]{:S(2)}, u32[]{:S(2)}) collective-permute-start(f32[1,256]{1,0:T(1,128)S(1)} %bitcast.19), channel_id=1, source_target_pairs={{0,16},{16,0},{32,48},{48,32},{64,80},{80,64},{96,112},{112,96},{1... | collective-permute-start | bytes 3080 | tf_op jit(solution)/shard_map/ppermute | solution.py:473
  192.2 4.0 %copy-start.2 = (bf16[2048,256]{1,0:T(8,128)(2,1)S(1)}, bf16[2048,256]{1,0:T(8,128)(2,1)}, u32[]{:S(2)}) copy-start(bf16[2048,256]{1,0:T(8,128)(2,1)} %weight_ref.1) | copy-start | bytes 3145732
  194.3 3.2 %collective-permute-start.6 = (bf16[8,32,256]{2,1,0:T(8,128)(2,1)S(1)}, bf16[8,32,256]{2,1,0:T(8,128)(2,1)S(1)}, u32[]{:S(2)}, u32[]{:S(2)}) collective-permute-start(bf16[8,32,256]{2,1,0:T(8,128)(2,1)S(1)} %shard_map.211), channel_id=1, source_target_pairs={{0,16},{16,0},{32,48},{48,32},{64,80},{80,64},{96,112},{112,96},{1... | collective-permute-start | bytes 393224 | tf_op jit(solution)/shard_map/ppermute | solution.py:536
  198.2 25.8 %all-to-all-start.8 = ((bf16[16,32,256]{2,1,0:T(8,128)(2,1)}), bf16[16,32,256]{2,1,0:T(8,128)(2,1)S(1)}, u32[]{:S(2)}, u32[]{:S(2)}) async-start(bf16[16,32,256]{2,1,0:T(8,128)(2,1)} %shard_map.212), calls=%async_computation.8 | async-start | bytes 524288 | tf_op jit(solution)/shard_map/all_to_all | solution.py:24
  205.7 18.4 %collective-permute-start.2 = (bf16[32,256]{1,0:T(8,128)(2,1)S(1)}, bf16[32,256]{1,0:T(8,128)(2,1)S(1)}, u32[]{:S(2)}, u32[]{:S(2)}) collective-permute-start(bf16[32,256]{1,0:T(8,128)(2,1)S(1)} %slice.9), channel_id=1, source_target_pairs={{0,16},{16,0},{32,48},{48,32},{64,80},{80,64},{96,112},{112,96},{1... | collective-permute-start | bytes 49160 | tf_op jit(solution)/shard_map/ppermute | solution.py:556
Sparse Core Ops, SparseCore 0:
  9.4 88.1 all-gather.2

commit v9 on v6

--- a/solution.py
+++ b/solution.py
@@ -264,7 +264,9 @@
         out_ref[row] = heads
 
 
-def out_kernel(parity_ref, heads_ref, weight_ref, residual_ref, mine_ref, other_ref, left_ref):
+def out_kernel(
+    parity_ref, heads_ref, weight_ref, residual_ref, gain_ref, mine_ref, other_ref, left_ref
+):
     total = residual_ref[...].astype(F32)
     for group in range(G):
         for request in range(8):
@@ -279,13 +281,19 @@
     after = total.astype(BF16)
     first = parity_ref[0] == 0
     mine_ref[...] = jnp.where(first, after[0:16, :], after[16:32, :])
-    other_ref[...] = jnp.where(first, after[16:32, :], after[0:16, :])
-
-
-def pair_copies_kernel(mine_ref, other_ref, out_ref):
+    other_ref[0:16, :] = jnp.where(first, after[16:32, :], after[0:16, :])
+    gain = jnp.broadcast_to(gain_ref[...], (16, 256))
+    high = gain.astype(BF16).astype(F32)
+    top = lax.broadcasted_iota(jnp.int32, (16, 256), 0) < 8
+    other_ref[16:32, :] = jnp.where(top, high, gain - high).astype(BF16)
+
+
+def pair_copies_kernel(mine_ref, other_ref, out_ref, gain_ref):
     for col in range(out_ref.shape[0]):
         out_ref[col, :, 0:256] = mine_ref[...]
-        out_ref[col, :, 256:512] = other_ref[...]
+        out_ref[col, :, 256:512] = other_ref[0:16, :]
+    terms = other_ref[16:32, :].astype(F32)
+    gain_ref[...] = terms[0:1, :] + terms[8:9, :]
 
 
 def up_kernel(after_ref, gain_ref, other_gain_ref, weight_ref, other_weight_ref, out_ref):
@@ -305,7 +313,17 @@
         out_ref[part, :, 2048:2176] = stat[part * 16 : (part + 1) * 16, :]
 
 
-def act_kernel(parts_ref, out_ref):
+def act_kernel(parts_ref, far_ref, out_ref, near_ref, done_ref):
+    copies = [
+        pltpu.make_async_copy(
+            far_ref.at[pl.ds(part * 512, 512)],
+            near_ref.at[pl.ds(part * 512, 512)],
+            done_ref.at[part],
+        )
+        for part in range(4)
+    ]
+    for copy in copies:
+        copy.start()
     stat = parts_ref[0, :, 2048:2176].astype(F32)
     for part in range(1, parts_ref.shape[0]):
         stat = stat + parts_ref[part, :, 2048:2176].astype(F32)
@@ -319,17 +337,23 @@
         act = (act * act).astype(BF16)
         for part in range(out_ref.shape[0]):
             out_ref[part, :, lanes] = act
-
-
-def down_kernel(act_ref, weight_ref, out_ref, turn_ref):
-    term = jnp.dot(act_ref[...].reshape(256, -1), weight_ref[...], preferred_element_type=F32)
+    for copy in copies:
+        copy.wait()
+
+
+def turn(term, turn_ref):
     for col in range(16):
         for request in range(4):
             start = col * 16 + request * 4
             turn_ref[2 * request + col // 8, col % 8 * 4 : col % 8 * 4 + 4, :] = term[
                 start : start + 4, :
             ]
-    out_ref[...] = turn_ref[...].astype(BF16)
+    return turn_ref[...].astype(BF16)
+
+
+def down_kernel(act_ref, weight_ref, out_ref, turn_ref):
+    act = act_ref[...].reshape(256, -1)
+    out_ref[...] = turn(jnp.dot(act, weight_ref[...], preferred_element_type=F32), turn_ref)
 
 
 def join_kernel(parity_ref, mine_ref, other_ref, out_ref):
@@ -371,6 +395,7 @@
     halves = [[row for row in range(rows) if row % 2 == half] for half in range(2)]
     smem = pl.BlockSpec(memory_space=pltpu.SMEM)
     vmem = pl.BlockSpec(memory_space=pltpu.VMEM)
+    hbm = pl.BlockSpec(memory_space=pltpu.HBM)
     params = pltpu.CompilerParams(vmem_limit_bytes=VMEM_LIMIT)
 
     out_weights = lax.all_gather(out_proj, "col", axis=0, tiled=False)
@@ -395,12 +420,6 @@
         )(parity, hidden.reshape(512, 256), norm_mixer[None, :], main, side)
 
     parts = pair_sum(project_half)
-    parts, up_mine, down_mine, gain_mine = lax.optimization_barrier(
-        (parts, ffn_up, ffn_down, norm_ffn[None, :])
-    )
-    up_other, down_other, gain_other = [
-        lax.ppermute(weight, "row", swap) for weight in (up_mine, down_mine, gain_mine)
-    ]
     parts = exchange(parts, "row", halves)
 
     bc_own, local_sums = call(
@@ -450,6 +469,10 @@
     )(place, slot_ids, *[operand for operand, _ in operands])
 
     bc_new = exchange(bc_own, "col")
+    bc_new, up_mine, down_mine = lax.optimization_barrier((bc_new, ffn_up, ffn_down))
+    up_other, down_other = [
+        lax.ppermute(weight, "row", swap) for weight in (up_mine, down_mine)
+    ]
     mixed = pl.pallas_call(
         mixer_kernel,
         out_shape=jax.ShapeDtypeStruct((cols, 4, 256), BF16),
@@ -459,31 +482,34 @@
 
     mixed = exchange(mixed, "col")
     heads = call(scale_heads_kernel, jax.ShapeDtypeStruct((rows, cols * 4, 128), BF16), mixed)
-    heads, out_weights = lax.optimization_barrier((heads, out_weights))
     heads = exchange(heads, "row")
     residual = lax.dynamic_slice(
         hidden.reshape(8, 64, 256), (0, 4 * col_index, 0), (8, 4, 256)
     ).reshape(32, 256)
-    half_after = jax.ShapeDtypeStruct((16, 256), BF16)
+    gain_mine = norm_ffn[None, :]
     after_mine, after_other = pl.pallas_call(
         out_kernel,
-        out_shape=(half_after, half_after),
-        in_specs=[smem, vmem, vmem, vmem],
+        out_shape=(
+            jax.ShapeDtypeStruct((16, 256), BF16),
+            jax.ShapeDtypeStruct((32, 256), BF16),
+        ),
+        in_specs=[smem, vmem, vmem, vmem, vmem],
         out_specs=(vmem, vmem),
         scratch_shapes=[pltpu.VMEM((32, 2048), F32)],
         compiler_params=params,
-    )(parity, heads, out_weights, residual)
+    )(parity, heads, out_weights, residual, gain_mine)
 
     after_other = lax.ppermute(after_other, "row", swap)
-    after = exchange(
-        call(
-            pair_copies_kernel,
+    copies, gain_other = call(
+        pair_copies_kernel,
+        (
             jax.ShapeDtypeStruct((cols, 16, 512), BF16),
-            after_mine,
-            after_other,
+            jax.ShapeDtypeStruct((1, 256), F32),
         ),
-        "col",
-    )
+        after_mine,
+        after_other,
+    )
+    after = exchange(copies, "col")
     up_parts = call(
         up_kernel,
         jax.ShapeDtypeStruct((16, 16, 2176), BF16),
@@ -493,8 +519,19 @@
         up_mine,
         up_other,
     )
+    up_parts, down_other = lax.optimization_barrier((up_parts, down_other))
     up_parts = exchange(up_parts, "row", halves)
-    act = call(act_kernel, jax.ShapeDtypeStruct((16, 16, 2048), BF16), up_parts)
+    act, down_other = pl.pallas_call(
+        act_kernel,
+        out_shape=(
+            jax.ShapeDtypeStruct((16, 16, 2048), BF16),
+            jax.ShapeDtypeStruct((2048, 256), BF16),
+        ),
+        in_specs=[vmem, hbm],
+        out_specs=(vmem, vmem),
+        scratch_shapes=[pltpu.SemaphoreType.DMA((4,))],
+        compiler_params=params,
+    )(up_parts, down_other)
     act = exchange(act, "row", halves)
 
     def down_half(weight):

time: 236 us -> 232 us (0.983)
  blocking collectives: 15.4 us -> 54.9 us
  waiting for transfers between devices: 119 us -> 86.8 us
  starting transfers between devices: 67.1 us -> 57.1 us
    all_to_all x1 -> x3, blocking collectives: 15.4 us -> 54.9 us  [exchange(): lax.all_to_all(parts, axis, 0, 0, tiled=True, axis_index_groups=groups)]
    all_to_all x8 -> x6, waiting for transfers between devices: 114 us -> 82.6 us  [exchange(): lax.all_to_all(parts, axis, 0, 0, tiled=True, axis_index_groups=groups)]
    all_to_all x8 -> x6, starting transfers between devices: 53.5 us -> 45 us  [exchange(): lax.all_to_all(parts, axis, 0, 0, tiled=True, axis_index_groups=groups)]
    pallas_call x6 -> x5, Pallas kernels: 6.1 us -> 3.74 us  [call(): pl.pallas_call(kernel, out_shape=out_shape, compiler_params=pltpu.Compile...]
    ppermute x3 -> x2, starting transfers between devices: 5.91 us -> 4.33 us  [local(): lax.ppermute(weight, 'row', swap)]
  transfers between devices with their start and end apart: 16 -> 13, of which waited for: 12 -> 9; matrix products, arithmetic and copies ran while one was open for 1% -> 1% of each run, Pallas kernels for 4% -> 4%
where the time goes in v9:
time: 232 us; the launch traced here: 231 us
  waiting for transfers between devices  86.8 us (37%)
  starting transfers between devices  57.1 us (25%)
  blocking collectives  54.9 us (24%)
  between operations  13.8 us (6%)
  Pallas kernels  11.6 us (5%)
  local copies, waits for them, and re-layouts  4.84 us (2%)
    all_to_all x6, waiting for transfers between devices, exchange(): lax.all_to_all(parts, axis, 0, 0, tiled=True, axis_index_groups=groups)  82.6 us
    all_to_all x3, blocking collectives, exchange(): lax.all_to_all(parts, axis, 0, 0, tiled=True, axis_index_groups=groups)  54.9 us
    all_to_all x6, starting transfers between devices, exchange(): lax.all_to_all(parts, axis, 0, 0, tiled=True, axis_index_groups=groups)  45 us
  transfers between devices with their start and end apart: 13, of which 9 were waited for; matrix products, arithmetic and copies ran while one was open for 1% of the time, Pallas kernels for 4%

profile of v9, /device:TPU:32, one launch (start us, length us, event | category | flops | bytes accessed | tf_op | source)
XLA Modules:
  0.0 230.8 jit_solution(8305900366925741964)
XLA Ops:
  6.5 0.7 all-gather.3.cloned.1.call-update
  7.3 0.7 copy-done.5
  8.0 0.7 shard_map.199
  8.7 15.2 %all-to-all-start = ((bf16[16,32,256]{2,1,0:T(8,128)(2,1)}), bf16[16,32,256]{2,1,0:T(8,128)(2,1)S(1)}, u32[]{:S(2)}, u32[]{:S(2)}) async-start(bf16[16,32,256]{2,1,0:T(8,128)(2,1)} %shard_map.199), calls=%async_computation | async-start | bytes 524288 | tf_op jit(solution)/shard_map/all_to_all | solution.py:24
  23.9 1.4 reshape.20.main_ref
  25.4 0.1 maximum_maximum_fusion
  25.5 17.4 %all-to-all-done = bf16[16,32,256]{2,1,0:T(8,128)(2,1)S(1)} async-done(((bf16[16,32,256]{2,1,0:T(8,128)(2,1)}), bf16[16,32,256]{2,1,0:T(8,128)(2,1)S(1)}, u32[]{:S(2)}, u32[]{:S(2)}) %all-to-all-start) | async-done | bytes 262176 | tf_op jit(solution)/shard_map/all_to_all | solution.py:24
  42.9 0.6 shard_map.201
  43.5 1.9 collective-permute-start
  45.4 0.6 shard_map.200
  46.0 1.5 collective-permute-done
  47.5 1.0 add_convert_fusion
  48.6 7.2 %all-to-all-start.1 = ((bf16[16,80,256]{2,1,0:T(8,128)(2,1)}), bf16[16,80,256]{2,1,0:T(8,128)(2,1)S(1)}, u32[]{:S(2)}, u32[]{:S(2)}) async-start(bf16[16,80,256]{2,1,0:T(8,128)(2,1)} %add_convert_fusion), calls=%async_computation.1 | async-start | bytes 1310720 | tf_op jit(solution)/shard_map/all_to_all | solution.py:24
  55.9 13.1 %all-to-all-done.1.parts_ref = bf16[16,80,256]{2,1,0:T(8,128)(2,1)S(1)} async-done(((bf16[16,80,256]{2,1,0:T(8,128)(2,1)}), bf16[16,80,256]{2,1,0:T(8,128)(2,1)S(1)}, u32[]{:S(2)}, u32[]{:S(2)}) %all-to-all-start.1) | async-done | bytes 655392 | tf_op jit(solution)/shard_map/all_to_all | solution.py:24
  69.0 0.7 shard_map.202
  69.7 6.7 %all-to-all-start.2 = ((bf16[16,16,128]{2,1,0:T(8,128)(2,1)}), bf16[16,16,128]{2,1,0:T(8,128)(2,1)S(1)}, u32[]{:S(2)}, u32[]{:S(2)}) async-start(bf16[16,16,128]{2,1,0:T(8,128)(2,1)} %get-tuple-element.24), calls=%async_computation.2 | async-start | bytes 131072 | tf_op jit(solution)/shard_map/all_to_all | solution.py:24
  76.5 0.1 copy.29.offset_ref
  76.6 0.1 copy.30.rate_ref
  76.7 0.1 copy.31.skip_ref
  76.9 2.2 shard_map.203
  79.1 9.5 %all-to-all-done.2.bc_new_ref = bf16[16,16,128]{2,1,0:T(8,128)(2,1)S(1)} async-done(((bf16[16,16,128]{2,1,0:T(8,128)(2,1)}), bf16[16,16,128]{2,1,0:T(8,128)(2,1)S(1)}, u32[]{:S(2)}, u32[]{:S(2)}) %all-to-all-start.2) | async-done | bytes 65568 | tf_op jit(solution)/shard_map/all_to_all | solution.py:24
  88.6 0.8 shard_map.204
  89.5 15.6 %all_to_all.45.parts_ref = bf16[16,4,256]{2,1,0:T(4,128)(2,1)S(1)} all-to-all(bf16[16,4,256]{2,1,0:T(4,128)(2,1)S(1)} %shard_map.204), channel_id=1, replica_groups=mesh['row'=32,'col'=16] {'col'}, dimensions={0} | all-to-all | bytes 65536 | tf_op jit(solution)/shard_map/all_to_all | solution.py:24
  105.0 0.9 shard_map.205
  105.9 3.9 %all-to-all-start.4 = ((bf16[32,64,128]{2,1,0:T(8,128)(2,1)}), bf16[32,64,128]{2,1,0:T(8,128)(2,1)S(1)}, u32[]{:S(2)}, u32[]{:S(2)}) async-start(bf16[32,64,128]{2,1,0:T(8,128)(2,1)} %shard_map.205), calls=%async_computation.4 | async-start | bytes 1048576 | tf_op jit(solution)/shard_map/all_to_all | solution.py:24
  109.8 2.1 collective-permute-start.3
  111.9 2.3 collective-permute-start.4
  114.2 7.4 %all-to-all-done.4.heads_ref = bf16[32,64,128]{2,1,0:T(8,128)(2,1)S(1)} async-done(((bf16[32,64,128]{2,1,0:T(8,128)(2,1)}), bf16[32,64,128]{2,1,0:T(8,128)(2,1)S(1)}, u32[]{:S(2)}, u32[]{:S(2)}) %all-to-all-start.4) | async-done | bytes 524320 | tf_op jit(solution)/shard_map/all_to_all | solution.py:24
  121.5 2.2 copy-done
  123.7 0.8 shard_map.206
  124.5 2.0 collective-permute-start.1
  126.5 1.1 collective-permute-done.1.other_ref
  127.6 0.7 shard_map.207
  128.3 4.6 %all-to-all-start.5 = ((bf16[16,16,512]{2,1,0:T(8,128)(2,1)}), bf16[16,16,512]{2,1,0:T(8,128)(2,1)S(1)}, u32[]{:S(2)}, u32[]{:S(2)}) async-start(bf16[16,16,512]{2,1,0:T(8,128)(2,1)} %get-tuple-element.31), calls=%async_computation.5 | async-start | bytes 524288 | tf_op jit(solution)/shard_map/all_to_all | solution.py:24
  132.9 18.9 %all-to-all-done.5.after_ref = bf16[16,16,512]{2,1,0:T(8,128)(2,1)S(1)} async-done(((bf16[16,16,512]{2,1,0:T(8,128)(2,1)}), bf16[16,16,512]{2,1,0:T(8,128)(2,1)S(1)}, u32[]{:S(2)}, u32[]{:S(2)}) %all-to-all-start.5) | async-done | bytes 262176 | tf_op jit(solution)/shard_map/all_to_all | solution.py:24
  151.8 0.7 shard_map.208
  152.5 20.6 %all_to_all.46.parts_ref = bf16[16,16,2176]{2,1,0:T(8,128)(2,1)S(1)} all-to-all(bf16[16,16,2176]{2,1,0:T(8,128)(2,1)S(1)} %shard_map.208), channel_id=1, replica_groups={{0,32,64,96,128,160,192,224,256,288,320,352,384,416,448,480},{16,48,80,..., dimensions={0} | all-to-all | bytes 2228224 | tf_op jit(solution)/shard_map/all_to_all | solution.py:24
  173.1 1.2 shard_map.209
  174.4 18.8 %all_to_all.47.act_ref = bf16[16,16,2048]{2,1,0:T(8,128)(2,1)S(1)} all-to-all(bf16[16,16,2048]{2,1,0:T(8,128)(2,1)S(1)} %get-tuple-element.37), channel_id=1, replica_groups={{0,32,64,96,128,160,192,224,256,288,320,352,384,416,448,480},{16,48,80,..., dimensions={0} | all-to-all | bytes 2097152 | tf_op jit(solution)/shard_map/all_to_all | solution.py:24
  193.1 0.5 shard_map.211
  193.6 1.9 collective-permute-start.5
  195.5 0.5 shard_map.210.mine_ref
  196.0 0.8 collective-permute-done.5.other_ref
  196.8 0.7 shard_map.212
  197.6 7.4 %all-to-all-start.8 = ((bf16[16,32,256]{2,1,0:T(8,128)(2,1)}), bf16[16,32,256]{2,1,0:T(8,128)(2,1)S(1)}, u32[]{:S(2)}, u32[]{:S(2)}) async-start(bf16[16,32,256]{2,1,0:T(8,128)(2,1)} %shard_map.212), calls=%async_computation.8 | async-start | bytes 524288 | tf_op jit(solution)/shard_map/all_to_all | solution.py:24
  205.0 1.9 collective-permute-start.2
  206.9 16.4 %all-to-all-done.8 = bf16[16,32,256]{2,1,0:T(8,128)(2,1)S(1)} async-done(((bf16[16,32,256]{2,1,0:T(8,128)(2,1)}), bf16[16,32,256]{2,1,0:T(8,128)(2,1)S(1)}, u32[]{:S(2)}, u32[]{:S(2)}) %all-to-all-start.8) | async-done | bytes 262176 | tf_op jit(solution)/shard_map/all_to_all | solution.py:24
  223.4 0.6 add_convert_fusion.1
  (54 shorter events, 0.4 us)
Async XLA Ops:
  6.5 18.9 %copy-start.13 = (bf16[256,4,32]{0,2,1:T(8,128)(2,1)S(1)}, bf16[256,4,32]{0,2,1:T(8,128)(2,1)}, u32[]{:S(2)}) copy-start(bf16[256,4,32]{0,2,1:T(8,128)(2,1)} %param.24) | copy-start | bytes 196612
  6.5 18.9 %copy-start.15 = (bf16[256,4,2]{0,2,1:T(2,128)(2,1)S(1)}, bf16[256,4,2]{0,2,1:T(2,128)(2,1)}, u32[]{:S(2)}) copy-start(bf16[256,4,2]{0,2,1:T(2,128)(2,1)} %param.25) | copy-start | bytes 12292
  6.5 36.4 %copy-start.9 = (f32[256]{0:T(256)S(1)}, f32[256]{0:T(256)}, u32[]{:S(2)}) copy-start(f32[256]{0:T(256)} %param.22) | copy-start | bytes 3076
  6.5 115.0 %all-gather.3.cloned.1.call-start = ((), (), s32[]{:S(2)}) async-start(), calls=%async_computation.9 | async-start | bytes 4456448 | tf_op jit(solution)/shard_map/all_gather | solution.py:401
  7.3 0.7 copy-start.5
  8.7 34.2 %all-to-all-start = ((bf16[16,32,256]{2,1,0:T(8,128)(2,1)}), bf16[16,32,256]{2,1,0:T(8,128)(2,1)S(1)}, u32[]{:S(2)}, u32[]{:S(2)}) async-start(bf16[16,32,256]{2,1,0:T(8,128)(2,1)} %shard_map.199), calls=%async_computation | async-start | bytes 524288 | tf_op jit(solution)/shard_map/all_to_all | solution.py:24
  43.5 4.0 %collective-permute-start = (bf16[16,80,256]{2,1,0:T(8,128)(2,1)S(1)}, bf16[16,80,256]{2,1,0:T(8,128)(2,1)S(1)}, u32[]{:S(2)}, u32[]{:S(2)}) collective-permute-start(bf16[16,80,256]{2,1,0:T(8,128)(2,1)S(1)} %shard_map.201), channel_id=1, source_target_pairs={{0,16},{16,0},{32,48},{48,32},{64,80},{80,64},{96,112},{112,96},{1... | collective-permute-start | bytes 1966088 | tf_op jit(solution)/shard_map/ppermute | solution.py:410
  48.5 28.0 %copy-start.14 = (bf16[1,4,3,512]{3,1,2,0:T(4,128)(2,1)S(1)}, bf16[1,4,3,512]{3,1,2,0:T(4,128)(2,1)}, u32[]{:S(2)}) copy-start(bf16[1,4,3,512]{3,1,2,0:T(4,128)(2,1)} %param.32) | copy-start | bytes 36868
  48.5 28.0 %copy-start.16 = (bf16[1,4,3,128]{3,1,2,0:T(4,128)(2,1)S(1)}, bf16[1,4,3,128]{3,1,2,0:T(4,128)(2,1)}, u32[]{:S(2)}) copy-start(bf16[1,4,3,128]{3,1,2,0:T(4,128)(2,1)} %param.31) | copy-start | bytes 9220
  48.5 28.1 %copy-start.17 = (f32[4,2]{0,1:T(2,128)S(1)}, f32[4,2]{0,1:T(2,128)}, u32[]{:S(2)}) copy-start(f32[4,2]{0,1:T(2,128)} %param.26) | copy-start | bytes 100
  48.5 28.2 %copy-start.18 = (f32[4,2]{0,1:T(2,128)S(1)}, f32[4,2]{0,1:T(2,128)}, u32[]{:S(2)}) copy-start(f32[4,2]{0,1:T(2,128)} %param.27) | copy-start | bytes 100
  48.5 28.3 %copy-start.19 = (f32[4,2]{0,1:T(2,128)S(1)}, f32[4,2]{0,1:T(2,128)}, u32[]{:S(2)}) copy-start(f32[4,2]{0,1:T(2,128)} %param.28) | copy-start | bytes 100
  48.5 28.3 %copy-start.3 = (f32[1,4,2,64,256]{4,3,2,1,0:T(8,128)S(1)}, f32[1,4,2,64,256]{4,3,2,1,0:T(8,128)}, u32[]{:S(2)}) copy-start(f32[1,4,2,64,256]{4,3,2,1,0:T(8,128)} %state_ref.1) | copy-start | bytes 1572868
  48.5 28.3 %copy-start.4 = (s32[8,64,64]{2,1,0:T(8,128)S(1)}, s32[8,64,64]{2,1,0:T(8,128)}, u32[]{:S(2)}) copy-start(s32[8,64,64]{2,1,0:T(8,128)} %anc_ref.1) | copy-start | bytes 393220
  48.5 28.3 %copy-start.6 = (bf16[4,4,512]{2,1,0:T(4,128)(2,1)S(1)}, bf16[4,4,512]{2,1,0:T(4,128)(2,1)}, u32[]{:S(2)}) copy-start(bf16[4,4,512]{2,1,0:T(4,128)(2,1)} %bc_taps_ref.1) | copy-start | bytes 49156
  48.5 28.3 %copy-start.7 = (bf16[4,4,128]{2,1,0:T(4,128)(2,1)S(1)}, bf16[4,4,128]{2,1,0:T(4,128)(2,1)}, u32[]{:S(2)}) copy-start(bf16[4,4,128]{2,1,0:T(4,128)(2,1)} %x_taps_ref.1) | copy-start | bytes 12292
  48.5 28.3 %copy-start.8 = (s32[8,64]{1,0:T(8,128)S(1)}, s32[8,64]{1,0:T(8,128)}, u32[]{:S(2)}) copy-start(s32[8,64]{1,0:T(8,128)} %parents_ref.1) | copy-start | bytes 6148
  48.5 28.3 %copy-start.11 = (f32[4,128]{1,0:T(4,128)S(1)}, f32[4,128]{1,0:T(4,128)}, u32[]{:S(2)}) copy-start(f32[4,128]{1,0:T(4,128)} %gain_ref.1) | copy-start | bytes 6148
  48.6 28.3 %copy-start.12 = (s32[8]{0:T(128)S(1)}, s32[8]{0:T(128)}, u32[]{:S(2)}) copy-start(s32[8]{0:T(128)} %slot_ref.1) | copy-start | bytes 100
  48.6 20.4 %all-to-all-start.1 = ((bf16[16,80,256]{2,1,0:T(8,128)(2,1)}), bf16[16,80,256]{2,1,0:T(8,128)(2,1)S(1)}, u32[]{:S(2)}, u32[]{:S(2)}) async-start(bf16[16,80,256]{2,1,0:T(8,128)(2,1)} %add_convert_fusion), calls=%async_computation.1 | async-start | bytes 1310720 | tf_op jit(solution)/shard_map/all_to_all | solution.py:24
  69.7 18.9 %all-to-all-start.2 = ((bf16[16,16,128]{2,1,0:T(8,128)(2,1)}), bf16[16,16,128]{2,1,0:T(8,128)(2,1)S(1)}, u32[]{:S(2)}, u32[]{:S(2)}) async-start(bf16[16,16,128]{2,1,0:T(8,128)(2,1)} %get-tuple-element.24), calls=%async_computation.2 | async-start | bytes 131072 | tf_op jit(solution)/shard_map/all_to_all | solution.py:24
  79.1 30.7 %copy-start.1 = (bf16[256,2048]{1,0:T(8,128)(2,1)S(1)}, bf16[256,2048]{1,0:T(8,128)(2,1)}, u32[]{:S(2)}) copy-start(bf16[256,2048]{1,0:T(8,128)(2,1)} %weight_ref) | copy-start | bytes 3145732
  79.1 42.5 %copy-start.10 = (f32[256]{0:T(256)S(1)}, f32[256]{0:T(256)}, u32[]{:S(2)}) copy-start(f32[256]{0:T(256)} %param.39) | copy-start | bytes 3076
  105.9 15.7 %all-to-all-start.4 = ((bf16[32,64,128]{2,1,0:T(8,128)(2,1)}), bf16[32,64,128]{2,1,0:T(8,128)(2,1)S(1)}, u32[]{:S(2)}, u32[]{:S(2)}) async-start(bf16[32,64,128]{2,1,0:T(8,128)(2,1)} %shard_map.205), calls=%async_computation.4 | async-start | bytes 1048576 | tf_op jit(solution)/shard_map/all_to_all | solution.py:24
  109.8 23.1 %collective-permute-start.3 = (bf16[256,2048]{1,0:T(8,128)(2,1)S(1)}, bf16[256,2048]{1,0:T(8,128)(2,1)S(1)}, u32[]{:S(2)}, u32[]{:S(2)}) collective-permute-start(bf16[256,2048]{1,0:T(8,128)(2,1)S(1)} %copy-done.1), channel_id=1, source_target_pairs={{0,16},{16,0},{32,48},{48,32},{64,80},{80,64},{96,112},{112,96},{1... | collective-permute-start | bytes 3145736 | tf_op jit(solution)/shard_map/ppermute | solution.py:474
  111.9 40.7 %collective-permute-start.4 = (bf16[2048,256]{1,0:T(8,128)(2,1)}, bf16[2048,256]{1,0:T(8,128)(2,1)}, u32[]{:S(2)}, u32[]{:S(2)}) collective-permute-start(bf16[2048,256]{1,0:T(8,128)(2,1)} %weight_ref.1), channel_id=1, source_target_pairs={{0,16},{16,0},{32,48},{48,32},{64,80},{80,64},{96,112},{112,96},{1... | collective-permute-start | bytes 3145736 | tf_op jit(solution)/shard_map/ppermute | solution.py:474
  121.5 2.2 copy-start
  124.5 3.1 %collective-permute-start.1 = (bf16[32,256]{1,0:T(8,128)(2,1)S(1)}, bf16[32,256]{1,0:T(8,128)(2,1)S(1)}, u32[]{:S(2)}, u32[]{:S(2)}) collective-permute-start(bf16[32,256]{1,0:T(8,128)(2,1)S(1)} %get-tuple-element.30), channel_id=1, source_target_pairs={{0,16},{16,0},{32,48},{48,32},{64,80},{80,64},{96,112},{112,96},{1... | collective-permute-start | bytes 49160 | tf_op jit(solution)/shard_map/ppermute | solution.py:502
  128.3 23.5 %all-to-all-start.5 = ((bf16[16,16,512]{2,1,0:T(8,128)(2,1)}), bf16[16,16,512]{2,1,0:T(8,128)(2,1)S(1)}, u32[]{:S(2)}, u32[]{:S(2)}) async-start(bf16[16,16,512]{2,1,0:T(8,128)(2,1)} %get-tuple-element.31), calls=%async_computation.5 | async-start | bytes 524288 | tf_op jit(solution)/shard_map/all_to_all | solution.py:24
  193.1 2.4 %copy-start.2 = (bf16[2048,256]{1,0:T(8,128)(2,1)S(1)}, bf16[2048,256]{1,0:T(8,128)(2,1)}, u32[]{:S(2)}) copy-start(bf16[2048,256]{1,0:T(8,128)(2,1)} %weight_ref.1) | copy-start | bytes 3145732
  193.6 3.2 %collective-permute-start.5 = (bf16[8,32,256]{2,1,0:T(8,128)(2,1)S(1)}, bf16[8,32,256]{2,1,0:T(8,128)(2,1)S(1)}, u32[]{:S(2)}, u32[]{:S(2)}) collective-permute-start(bf16[8,32,256]{2,1,0:T(8,128)(2,1)S(1)} %shard_map.211), channel_id=1, source_target_pairs={{0,16},{16,0},{32,48},{48,32},{64,80},{80,64},{96,112},{112,96},{1... | collective-permute-start | bytes 393224 | tf_op jit(solution)/shard_map/ppermute | solution.py:545
  197.6 25.8 %all-to-all-start.8 = ((bf16[16,32,256]{2,1,0:T(8,128)(2,1)}), bf16[16,32,256]{2,1,0:T(8,128)(2,1)S(1)}, u32[]{:S(2)}, u32[]{:S(2)}) async-start(bf16[16,32,256]{2,1,0:T(8,128)(2,1)} %shard_map.212), calls=%async_computation.8 | async-start | bytes 524288 | tf_op jit(solution)/shard_map/all_to_all | solution.py:24
  205.0 18.4 %collective-permute-start.2 = (bf16[32,256]{1,0:T(8,128)(2,1)S(1)}, bf16[32,256]{1,0:T(8,128)(2,1)S(1)}, u32[]{:S(2)}, u32[]{:S(2)}) collective-permute-start(bf16[32,256]{1,0:T(8,128)(2,1)S(1)} %slice.9), channel_id=1, source_target_pairs={{0,16},{16,0},{32,48},{48,32},{64,80},{80,64},{96,112},{112,96},{1... | collective-permute-start | bytes 49160 | tf_op jit(solution)/shard_map/ppermute | solution.py:557
Sparse Core Ops, SparseCore 0:
  9.4 88.3 all-gather.2

commit v10 on v9

--- a/solution.py
+++ b/solution.py
@@ -37,8 +37,8 @@
         out_ref[part] = block_ref[...]
 
 
-def project_kernel(flip, parity_ref, hidden_ref, gain_ref, main_ref, side_ref, out_ref):
-    use = parity_ref[0] if not flip else 1 - parity_ref[0]
+def project_kernel(flip, place_ref, hidden_ref, gain_ref, main_ref, side_ref, out_ref):
+    use = place_ref[2] if not flip else 1 - place_ref[2]
     hidden = hidden_ref[...].astype(F32)
     normed = (hidden * gain_ref[...]).astype(BF16)
     squares = (hidden * hidden).astype(BF16)
@@ -265,7 +265,7 @@
 
 
 def out_kernel(
-    parity_ref, heads_ref, weight_ref, residual_ref, gain_ref, mine_ref, other_ref, left_ref
+    place_ref, heads_ref, weight_ref, residual_ref, gain_ref, mine_ref, other_ref, left_ref
 ):
     total = residual_ref[...].astype(F32)
     for group in range(G):
@@ -279,7 +279,7 @@
         weight = weight_ref[:, group].reshape(-1, 256)
         total = total + jnp.dot(left, weight, preferred_element_type=F32)
     after = total.astype(BF16)
-    first = parity_ref[0] == 0
+    first = place_ref[2] == 0
     mine_ref[...] = jnp.where(first, after[0:16, :], after[16:32, :])
     other_ref[0:16, :] = jnp.where(first, after[16:32, :], after[0:16, :])
     gain = jnp.broadcast_to(gain_ref[...], (16, 256))
@@ -356,8 +356,8 @@
     out_ref[...] = turn(jnp.dot(act, weight_ref[...], preferred_element_type=F32), turn_ref)
 
 
-def join_kernel(parity_ref, mine_ref, other_ref, out_ref):
-    parity = parity_ref[0]
+def join_kernel(place_ref, mine_ref, other_ref, out_ref):
+    parity = place_ref[2]
     out_ref[pl.ds(parity * 8, 8)] = mine_ref[...]
     out_ref[pl.ds(8 - parity * 8, 8)] = other_ref[...]
 
@@ -389,8 +389,7 @@
     cols = lax.axis_size("col")
     row_index = lax.axis_index("row")
     col_index = lax.axis_index("col")
-    place = jnp.stack([row_index // G, row_index % G]).astype(jnp.int32)
-    parity = (row_index % 2).astype(jnp.int32)[None]
+    place = jnp.stack([row_index // G, row_index % G, row_index % 2]).astype(jnp.int32)
     swap = [(row, row ^ 1) for row in range(rows)]
     halves = [[row for row in range(rows) if row % 2 == half] for half in range(2)]
     smem = pl.BlockSpec(memory_space=pltpu.SMEM)
@@ -417,7 +416,7 @@
             in_specs=[smem, vmem, vmem, vmem, vmem],
             out_specs=vmem,
             compiler_params=params,
-        )(parity, hidden.reshape(512, 256), norm_mixer[None, :], main, side)
+        )(place, hidden.reshape(512, 256), norm_mixer[None, :], main, side)
 
     parts = pair_sum(project_half)
     parts = exchange(parts, "row", halves)
@@ -427,7 +426,7 @@
         (jax.ShapeDtypeStruct((cols, 16, 128), BF16), jax.ShapeDtypeStruct((72, 256), F32)),
         parts,
     )
-    bc_own, place = lax.optimization_barrier((bc_own, place))
+    bc_own, place_later = lax.optimization_barrier((bc_own, place))
 
     def whole(array):
         shape = array.shape
@@ -466,7 +465,7 @@
             jax.ShapeDtypeStruct((2 * P_SIZE, N), BF16),
         ],
         compiler_params=params,
-    )(place, slot_ids, *[operand for operand, _ in operands])
+    )(place_later, slot_ids, *[operand for operand, _ in operands])
 
     bc_new = exchange(bc_own, "col")
     bc_new, up_mine, down_mine = lax.optimization_barrier((bc_new, ffn_up, ffn_down))
@@ -497,7 +496,7 @@
         out_specs=(vmem, vmem),
         scratch_shapes=[pltpu.VMEM((32, 2048), F32)],
         compiler_params=params,
-    )(parity, heads, out_weights, residual, gain_mine)
+    )(place, heads, out_weights, residual, gain_mine)
 
     after_other = lax.ppermute(after_other, "row", swap)
     copies, gain_other = call(
@@ -549,7 +548,7 @@
         in_specs=[smem, vmem, vmem],
         out_specs=vmem,
         compiler_params=params,
-    )(parity, down_half(down_mine), from_other)
+    )(place, down_half(down_mine), from_other)
     ffn_out = jnp.sum(exchange(down, "col").astype(F32), axis=0)
     own = lax.dynamic_slice(
         after, (8 * (col_index % 2), 4 * (col_index // 2 % 4), 0), (8, 4, 512)

time: 232 us -> 233 us (level)
  blocking collectives: 54.9 us -> 75.1 us
  waiting for transfers between devices: 86.8 us -> 73.1 us
  starting transfers between devices: 57.1 us -> 49.9 us
    all_to_all x3 -> x4, blocking collectives: 54.9 us -> 75.1 us  [exchange(): lax.all_to_all(parts, axis, 0, 0, tiled=True, axis_index_groups=groups)]
    all_to_all x6 -> x5, waiting for transfers between devices: 82.6 us -> 69.5 us  [exchange(): lax.all_to_all(parts, axis, 0, 0, tiled=True, axis_index_groups=groups)]
    all_to_all x6 -> x5, starting transfers between devices: 45 us -> 37.9 us  [exchange(): lax.all_to_all(parts, axis, 0, 0, tiled=True, axis_index_groups=groups)]
  transfers between devices with their start and end apart: 13 -> 12, of which waited for: 9 -> 8; matrix products, arithmetic and copies ran while one was open for 1% -> 1% of each run, Pallas kernels for 4% -> 5%
where the time goes in v10:
time: 233 us; the launch traced here: 231 us
  blocking collectives  75.1 us (32%)
  waiting for transfers between devices  73.1 us (31%)
  starting transfers between devices  49.9 us (21%)
  between operations  13.8 us (6%)
  Pallas kernels  13.7 us (6%)
  local copies, waits for them, and re-layouts  4.85 us (2%)
    all_to_all x4, blocking collectives, exchange(): lax.all_to_all(parts, axis, 0, 0, tiled=True, axis_index_groups=groups)  75.1 us
    all_to_all x5, waiting for transfers between devices, exchange(): lax.all_to_all(parts, axis, 0, 0, tiled=True, axis_index_groups=groups)  69.5 us
    all_to_all x5, starting transfers between devices, exchange(): lax.all_to_all(parts, axis, 0, 0, tiled=True, axis_index_groups=groups)  37.9 us
  transfers between devices with their start and end apart: 12, of which 8 were waited for; matrix products, arithmetic and copies ran while one was open for 1% of the time, Pallas kernels for 5%

profile of v10, /device:TPU:32, one launch (start us, length us, event | category | flops | bytes accessed | tf_op | source)
XLA Modules:
  0.0 231.5 jit_solution(10027933180570475993)
XLA Ops:
  6.5 0.7 all-gather.3.cloned.1.call-update
  7.3 0.7 copy-done.5
  8.0 0.7 shard_map.199
  8.7 15.2 %all-to-all-start = ((bf16[16,32,256]{2,1,0:T(8,128)(2,1)}), bf16[16,32,256]{2,1,0:T(8,128)(2,1)S(1)}, u32[]{:S(2)}, u32[]{:S(2)}) async-start(bf16[16,32,256]{2,1,0:T(8,128)(2,1)} %shard_map.199), calls=%async_computation | async-start | bytes 524288 | tf_op jit(solution)/shard_map/all_to_all | solution.py:24
  23.9 1.4 reshape.20.main_ref
  25.4 0.1 pad.2.clone
  25.5 0.1 maximum_maximum_fusion
  25.6 17.3 %all-to-all-done = bf16[16,32,256]{2,1,0:T(8,128)(2,1)S(1)} async-done(((bf16[16,32,256]{2,1,0:T(8,128)(2,1)}), bf16[16,32,256]{2,1,0:T(8,128)(2,1)S(1)}, u32[]{:S(2)}, u32[]{:S(2)}) %all-to-all-start) | async-done | bytes 262176 | tf_op jit(solution)/shard_map/all_to_all | solution.py:24
  42.9 1.1 shard_map.201
  44.0 1.9 collective-permute-start
  45.9 1.1 shard_map.200
  47.0 1.0 collective-permute-done
  48.0 0.2 add_convert_fusion
  48.3 20.2 %all_to_all.45.parts_ref = bf16[16,80,256]{2,1,0:T(8,128)(2,1)S(1)} all-to-all(bf16[16,80,256]{2,1,0:T(8,128)(2,1)S(1)} %add_convert_fusion), channel_id=1, replica_groups={{0,32,64,96,128,160,192,224,256,288,320,352,384,416,448,480},{16,48,80,..., dimensions={0} | all-to-all | bytes 1310720 | tf_op jit(solution)/shard_map/all_to_all | solution.py:24
  68.5 0.7 shard_map.202
  69.3 6.7 %all-to-all-start.2 = ((bf16[16,16,128]{2,1,0:T(8,128)(2,1)}), bf16[16,16,128]{2,1,0:T(8,128)(2,1)S(1)}, u32[]{:S(2)}, u32[]{:S(2)}) async-start(bf16[16,16,128]{2,1,0:T(8,128)(2,1)} %get-tuple-element.24), calls=%async_computation.2 | async-start | bytes 131072 | tf_op jit(solution)/shard_map/all_to_all | solution.py:24
  76.1 0.1 copy.29.offset_ref
  76.2 0.1 copy.30.rate_ref
  76.2 0.1 copy.31.skip_ref
  76.4 2.2 shard_map.203
  78.6 9.6 %all-to-all-done.2.bc_new_ref = bf16[16,16,128]{2,1,0:T(8,128)(2,1)S(1)} async-done(((bf16[16,16,128]{2,1,0:T(8,128)(2,1)}), bf16[16,16,128]{2,1,0:T(8,128)(2,1)S(1)}, u32[]{:S(2)}, u32[]{:S(2)}) %all-to-all-start.2) | async-done | bytes 65568 | tf_op jit(solution)/shard_map/all_to_all | solution.py:24
  88.2 0.8 shard_map.204
  89.0 15.5 %all_to_all.46.parts_ref = bf16[16,4,256]{2,1,0:T(4,128)(2,1)S(1)} all-to-all(bf16[16,4,256]{2,1,0:T(4,128)(2,1)S(1)} %shard_map.204), channel_id=1, replica_groups=mesh['row'=32,'col'=16] {'col'}, dimensions={0} | all-to-all | bytes 65536 | tf_op jit(solution)/shard_map/all_to_all | solution.py:24
  104.5 0.9 shard_map.205
  105.4 3.9 %all-to-all-start.4 = ((bf16[32,64,128]{2,1,0:T(8,128)(2,1)}), bf16[32,64,128]{2,1,0:T(8,128)(2,1)S(1)}, u32[]{:S(2)}, u32[]{:S(2)}) async-start(bf16[32,64,128]{2,1,0:T(8,128)(2,1)} %shard_map.205), calls=%async_computation.4 | async-start | bytes 1048576 | tf_op jit(solution)/shard_map/all_to_all | solution.py:24
  109.3 2.1 collective-permute-start.3
  111.4 2.3 collective-permute-start.4
  113.7 7.4 %all-to-all-done.4.heads_ref = bf16[32,64,128]{2,1,0:T(8,128)(2,1)S(1)} async-done(((bf16[32,64,128]{2,1,0:T(8,128)(2,1)}), bf16[32,64,128]{2,1,0:T(8,128)(2,1)S(1)}, u32[]{:S(2)}, u32[]{:S(2)}) %all-to-all-start.4) | async-done | bytes 524320 | tf_op jit(solution)/shard_map/all_to_all | solution.py:24
  121.1 2.2 copy-done
  123.3 1.3 shard_map.206
  124.6 2.0 collective-permute-start.1
  126.6 1.1 collective-permute-done.1.other_ref
  127.7 0.7 shard_map.207
  128.4 4.6 %all-to-all-start.5 = ((bf16[16,16,512]{2,1,0:T(8,128)(2,1)}), bf16[16,16,512]{2,1,0:T(8,128)(2,1)S(1)}, u32[]{:S(2)}, u32[]{:S(2)}) async-start(bf16[16,16,512]{2,1,0:T(8,128)(2,1)} %get-tuple-element.31), calls=%async_computation.5 | async-start | bytes 524288 | tf_op jit(solution)/shard_map/all_to_all | solution.py:24
  133.0 18.9 %all-to-all-done.5.after_ref = bf16[16,16,512]{2,1,0:T(8,128)(2,1)S(1)} async-done(((bf16[16,16,512]{2,1,0:T(8,128)(2,1)}), bf16[16,16,512]{2,1,0:T(8,128)(2,1)S(1)}, u32[]{:S(2)}, u32[]{:S(2)}) %all-to-all-start.5) | async-done | bytes 262176 | tf_op jit(solution)/shard_map/all_to_all | solution.py:24
  151.9 0.7 shard_map.208
  152.6 20.6 %all_to_all.47.parts_ref = bf16[16,16,2176]{2,1,0:T(8,128)(2,1)S(1)} all-to-all(bf16[16,16,2176]{2,1,0:T(8,128)(2,1)S(1)} %shard_map.208), channel_id=1, replica_groups={{0,32,64,96,128,160,192,224,256,288,320,352,384,416,448,480},{16,48,80,..., dimensions={0} | all-to-all | bytes 2228224 | tf_op jit(solution)/shard_map/all_to_all | solution.py:24
  173.2 1.2 shard_map.209
  174.4 18.8 %all_to_all.48.act_ref = bf16[16,16,2048]{2,1,0:T(8,128)(2,1)S(1)} all-to-all(bf16[16,16,2048]{2,1,0:T(8,128)(2,1)S(1)} %get-tuple-element.37), channel_id=1, replica_groups={{0,32,64,96,128,160,192,224,256,288,320,352,384,416,448,480},{16,48,80,..., dimensions={0} | all-to-all | bytes 2097152 | tf_op jit(solution)/shard_map/all_to_all | solution.py:24
  193.2 0.5 shard_map.211
  193.7 1.9 collective-permute-start.5
  195.6 0.5 shard_map.210.mine_ref
  196.1 0.8 collective-permute-done.5.other_ref
  196.9 1.3 shard_map.212
  198.2 7.4 %all-to-all-start.8 = ((bf16[16,32,256]{2,1,0:T(8,128)(2,1)}), bf16[16,32,256]{2,1,0:T(8,128)(2,1)S(1)}, u32[]{:S(2)}, u32[]{:S(2)}) async-start(bf16[16,32,256]{2,1,0:T(8,128)(2,1)} %shard_map.212), calls=%async_computation.8 | async-start | bytes 524288 | tf_op jit(solution)/shard_map/all_to_all | solution.py:24
  205.6 1.9 collective-permute-start.2
  207.6 16.4 %all-to-all-done.8 = bf16[16,32,256]{2,1,0:T(8,128)(2,1)S(1)} async-done(((bf16[16,32,256]{2,1,0:T(8,128)(2,1)}), bf16[16,32,256]{2,1,0:T(8,128)(2,1)S(1)}, u32[]{:S(2)}, u32[]{:S(2)}) %all-to-all-start.8) | async-done | bytes 262176 | tf_op jit(solution)/shard_map/all_to_all | solution.py:24
  224.0 0.6 add_convert_fusion.1
  (53 shorter events, 0.3 us)
Async XLA Ops:
  6.5 19.0 %copy-start.13 = (bf16[256,4,32]{0,2,1:T(8,128)(2,1)S(1)}, bf16[256,4,32]{0,2,1:T(8,128)(2,1)}, u32[]{:S(2)}) copy-start(bf16[256,4,32]{0,2,1:T(8,128)(2,1)} %param.24) | copy-start | bytes 196612
  6.5 19.0 %copy-start.15 = (bf16[256,4,2]{0,2,1:T(2,128)(2,1)S(1)}, bf16[256,4,2]{0,2,1:T(2,128)(2,1)}, u32[]{:S(2)}) copy-start(bf16[256,4,2]{0,2,1:T(2,128)(2,1)} %param.25) | copy-start | bytes 12292
  6.5 36.4 %copy-start.9 = (f32[256]{0:T(256)S(1)}, f32[256]{0:T(256)}, u32[]{:S(2)}) copy-start(f32[256]{0:T(256)} %param.22) | copy-start | bytes 3076
  6.5 114.5 %all-gather.3.cloned.1.call-start = ((), (), s32[]{:S(2)}) async-start(), calls=%async_computation.9 | async-start | bytes 4456448 | tf_op jit(solution)/shard_map/all_gather | solution.py:400
  7.3 0.7 copy-start.5
  8.7 34.2 %all-to-all-start = ((bf16[16,32,256]{2,1,0:T(8,128)(2,1)}), bf16[16,32,256]{2,1,0:T(8,128)(2,1)S(1)}, u32[]{:S(2)}, u32[]{:S(2)}) async-start(bf16[16,32,256]{2,1,0:T(8,128)(2,1)} %shard_map.199), calls=%async_computation | async-start | bytes 524288 | tf_op jit(solution)/shard_map/all_to_all | solution.py:24
  44.0 4.0 %collective-permute-start = (bf16[16,80,256]{2,1,0:T(8,128)(2,1)S(1)}, bf16[16,80,256]{2,1,0:T(8,128)(2,1)S(1)}, u32[]{:S(2)}, u32[]{:S(2)}) collective-permute-start(bf16[16,80,256]{2,1,0:T(8,128)(2,1)S(1)} %shard_map.201), channel_id=1, source_target_pairs={{0,16},{16,0},{32,48},{48,32},{64,80},{80,64},{96,112},{112,96},{1... | collective-permute-start | bytes 1966088 | tf_op jit(solution)/shard_map/ppermute | solution.py:409
  48.2 27.8 %copy-start.14 = (bf16[1,4,3,512]{3,1,2,0:T(4,128)(2,1)S(1)}, bf16[1,4,3,512]{3,1,2,0:T(4,128)(2,1)}, u32[]{:S(2)}) copy-start(bf16[1,4,3,512]{3,1,2,0:T(4,128)(2,1)} %param.32) | copy-start | bytes 36868
  48.2 27.8 %copy-start.16 = (bf16[1,4,3,128]{3,1,2,0:T(4,128)(2,1)S(1)}, bf16[1,4,3,128]{3,1,2,0:T(4,128)(2,1)}, u32[]{:S(2)}) copy-start(bf16[1,4,3,128]{3,1,2,0:T(4,128)(2,1)} %param.31) | copy-start | bytes 9220
  48.2 27.9 %copy-start.17 = (f32[4,2]{0,1:T(2,128)S(1)}, f32[4,2]{0,1:T(2,128)}, u32[]{:S(2)}) copy-start(f32[4,2]{0,1:T(2,128)} %param.26) | copy-start | bytes 100
  48.2 27.9 %copy-start.18 = (f32[4,2]{0,1:T(2,128)S(1)}, f32[4,2]{0,1:T(2,128)}, u32[]{:S(2)}) copy-start(f32[4,2]{0,1:T(2,128)} %param.27) | copy-start | bytes 100
  48.2 28.0 %copy-start.19 = (f32[4,2]{0,1:T(2,128)S(1)}, f32[4,2]{0,1:T(2,128)}, u32[]{:S(2)}) copy-start(f32[4,2]{0,1:T(2,128)} %param.28) | copy-start | bytes 100
  48.2 28.1 %copy-start.3 = (f32[1,4,2,64,256]{4,3,2,1,0:T(8,128)S(1)}, f32[1,4,2,64,256]{4,3,2,1,0:T(8,128)}, u32[]{:S(2)}) copy-start(f32[1,4,2,64,256]{4,3,2,1,0:T(8,128)} %state_ref.1) | copy-start | bytes 1572868
  48.2 28.1 %copy-start.4 = (s32[8,64,64]{2,1,0:T(8,128)S(1)}, s32[8,64,64]{2,1,0:T(8,128)}, u32[]{:S(2)}) copy-start(s32[8,64,64]{2,1,0:T(8,128)} %anc_ref.1) | copy-start | bytes 393220
  48.3 28.1 %copy-start.6 = (bf16[4,4,512]{2,1,0:T(4,128)(2,1)S(1)}, bf16[4,4,512]{2,1,0:T(4,128)(2,1)}, u32[]{:S(2)}) copy-start(bf16[4,4,512]{2,1,0:T(4,128)(2,1)} %bc_taps_ref.1) | copy-start | bytes 49156
  48.3 28.1 %copy-start.7 = (bf16[4,4,128]{2,1,0:T(4,128)(2,1)S(1)}, bf16[4,4,128]{2,1,0:T(4,128)(2,1)}, u32[]{:S(2)}) copy-start(bf16[4,4,128]{2,1,0:T(4,128)(2,1)} %x_taps_ref.1) | copy-start | bytes 12292
  48.3 28.1 %copy-start.8 = (s32[8,64]{1,0:T(8,128)S(1)}, s32[8,64]{1,0:T(8,128)}, u32[]{:S(2)}) copy-start(s32[8,64]{1,0:T(8,128)} %parents_ref.1) | copy-start | bytes 6148
  48.3 28.1 %copy-start.11 = (f32[4,128]{1,0:T(4,128)S(1)}, f32[4,128]{1,0:T(4,128)}, u32[]{:S(2)}) copy-start(f32[4,128]{1,0:T(4,128)} %gain_ref.1) | copy-start | bytes 6148
  48.3 28.1 %copy-start.12 = (s32[8]{0:T(128)S(1)}, s32[8]{0:T(128)}, u32[]{:S(2)}) copy-start(s32[8]{0:T(128)} %slot_ref.1) | copy-start | bytes 100
  69.3 18.9 %all-to-all-start.2 = ((bf16[16,16,128]{2,1,0:T(8,128)(2,1)}), bf16[16,16,128]{2,1,0:T(8,128)(2,1)S(1)}, u32[]{:S(2)}, u32[]{:S(2)}) async-start(bf16[16,16,128]{2,1,0:T(8,128)(2,1)} %get-tuple-element.24), calls=%async_computation.2 | async-start | bytes 131072 | tf_op jit(solution)/shard_map/all_to_all | solution.py:24
  78.6 30.7 %copy-start.1 = (bf16[256,2048]{1,0:T(8,128)(2,1)S(1)}, bf16[256,2048]{1,0:T(8,128)(2,1)}, u32[]{:S(2)}) copy-start(bf16[256,2048]{1,0:T(8,128)(2,1)} %weight_ref) | copy-start | bytes 3145732
  78.6 42.5 %copy-start.10 = (f32[256]{0:T(256)S(1)}, f32[256]{0:T(256)}, u32[]{:S(2)}) copy-start(f32[256]{0:T(256)} %param.39) | copy-start | bytes 3076
  105.4 15.7 %all-to-all-start.4 = ((bf16[32,64,128]{2,1,0:T(8,128)(2,1)}), bf16[32,64,128]{2,1,0:T(8,128)(2,1)S(1)}, u32[]{:S(2)}, u32[]{:S(2)}) async-start(bf16[32,64,128]{2,1,0:T(8,128)(2,1)} %shard_map.205), calls=%async_computation.4 | async-start | bytes 1048576 | tf_op jit(solution)/shard_map/all_to_all | solution.py:24
  109.3 23.7 %collective-permute-start.3 = (bf16[256,2048]{1,0:T(8,128)(2,1)S(1)}, bf16[256,2048]{1,0:T(8,128)(2,1)S(1)}, u32[]{:S(2)}, u32[]{:S(2)}) collective-permute-start(bf16[256,2048]{1,0:T(8,128)(2,1)S(1)} %copy-done.1), channel_id=1, source_target_pairs={{0,16},{16,0},{32,48},{48,32},{64,80},{80,64},{96,112},{112,96},{1... | collective-permute-start | bytes 3145736 | tf_op jit(solution)/shard_map/ppermute | solution.py:473
  111.4 41.2 %collective-permute-start.4 = (bf16[2048,256]{1,0:T(8,128)(2,1)}, bf16[2048,256]{1,0:T(8,128)(2,1)}, u32[]{:S(2)}, u32[]{:S(2)}) collective-permute-start(bf16[2048,256]{1,0:T(8,128)(2,1)} %weight_ref.1), channel_id=1, source_target_pairs={{0,16},{16,0},{32,48},{48,32},{64,80},{80,64},{96,112},{112,96},{1... | collective-permute-start | bytes 3145736 | tf_op jit(solution)/shard_map/ppermute | solution.py:473
  121.1 2.2 copy-start
  124.6 3.1 %collective-permute-start.1 = (bf16[32,256]{1,0:T(8,128)(2,1)S(1)}, bf16[32,256]{1,0:T(8,128)(2,1)S(1)}, u32[]{:S(2)}, u32[]{:S(2)}) collective-permute-start(bf16[32,256]{1,0:T(8,128)(2,1)S(1)} %get-tuple-element.30), channel_id=1, source_target_pairs={{0,16},{16,0},{32,48},{48,32},{64,80},{80,64},{96,112},{112,96},{1... | collective-permute-start | bytes 49160 | tf_op jit(solution)/shard_map/ppermute | solution.py:501
  128.4 23.5 %all-to-all-start.5 = ((bf16[16,16,512]{2,1,0:T(8,128)(2,1)}), bf16[16,16,512]{2,1,0:T(8,128)(2,1)S(1)}, u32[]{:S(2)}, u32[]{:S(2)}) async-start(bf16[16,16,512]{2,1,0:T(8,128)(2,1)} %get-tuple-element.31), calls=%async_computation.5 | async-start | bytes 524288 | tf_op jit(solution)/shard_map/all_to_all | solution.py:24
  193.2 2.4 %copy-start.2 = (bf16[2048,256]{1,0:T(8,128)(2,1)S(1)}, bf16[2048,256]{1,0:T(8,128)(2,1)}, u32[]{:S(2)}) copy-start(bf16[2048,256]{1,0:T(8,128)(2,1)} %weight_ref.1) | copy-start | bytes 3145732
  193.7 3.2 %collective-permute-start.5 = (bf16[8,32,256]{2,1,0:T(8,128)(2,1)S(1)}, bf16[8,32,256]{2,1,0:T(8,128)(2,1)S(1)}, u32[]{:S(2)}, u32[]{:S(2)}) collective-permute-start(bf16[8,32,256]{2,1,0:T(8,128)(2,1)S(1)} %shard_map.211), channel_id=1, source_target_pairs={{0,16},{16,0},{32,48},{48,32},{64,80},{80,64},{96,112},{112,96},{1... | collective-permute-start | bytes 393224 | tf_op jit(solution)/shard_map/ppermute | solution.py:544
  198.2 25.8 %all-to-all-start.8 = ((bf16[16,32,256]{2,1,0:T(8,128)(2,1)}), bf16[16,32,256]{2,1,0:T(8,128)(2,1)S(1)}, u32[]{:S(2)}, u32[]{:S(2)}) async-start(bf16[16,32,256]{2,1,0:T(8,128)(2,1)} %shard_map.212), calls=%async_computation.8 | async-start | bytes 524288 | tf_op jit(solution)/shard_map/all_to_all | solution.py:24
  205.6 18.4 %collective-permute-start.2 = (bf16[32,256]{1,0:T(8,128)(2,1)S(1)}, bf16[32,256]{1,0:T(8,128)(2,1)S(1)}, u32[]{:S(2)}, u32[]{:S(2)}) collective-permute-start(bf16[32,256]{1,0:T(8,128)(2,1)S(1)} %slice.9), channel_id=1, source_target_pairs={{0,16},{16,0},{32,48},{48,32},{64,80},{80,64},{96,112},{112,96},{1... | collective-permute-start | bytes 49160 | tf_op jit(solution)/shard_map/ppermute | solution.py:556
Sparse Core Ops, SparseCore 0:
  9.4 88.2 all-gather.2

commit v11 on v9

--- a/solution.py
+++ b/solution.py
@@ -87,7 +87,8 @@
 
 
 def prepare_kernel(
-    place_ref,
+    request_ref,
+    group_ref,
     slot_ref,
     x_hist_ref,
     bc_hist_ref,
@@ -103,8 +104,8 @@
     pack_ref,
     state_out_ref,
 ):
-    request = place_ref[0]
-    group = place_ref[1]
+    request = request_ref[0]
+    group = group_ref[0]
 
     def of_group(ref):
         table = ref[...]
@@ -389,8 +390,10 @@
     cols = lax.axis_size("col")
     row_index = lax.axis_index("row")
     col_index = lax.axis_index("col")
-    place = jnp.stack([row_index // G, row_index % G]).astype(jnp.int32)
+    request = (row_index // G).astype(jnp.int32)[None]
+    group = (row_index % G).astype(jnp.int32)[None]
     parity = (row_index % 2).astype(jnp.int32)[None]
+    request, group, parity = lax.optimization_barrier((request, group, parity))
     swap = [(row, row ^ 1) for row in range(rows)]
     halves = [[row for row in range(rows) if row % 2 == half] for half in range(2)]
     smem = pl.BlockSpec(memory_space=pltpu.SMEM)
@@ -427,15 +430,17 @@
         (jax.ShapeDtypeStruct((cols, 16, 128), BF16), jax.ShapeDtypeStruct((72, 256), F32)),
         parts,
     )
-    bc_own, place = lax.optimization_barrier((bc_own, place))
+    bc_own, request = lax.optimization_barrier((bc_own, request))
 
     def whole(array):
         shape = array.shape
-        return pl.BlockSpec(shape, lambda step, place, slots: (0,) * len(shape))
+        return pl.BlockSpec(shape, lambda step, request, group, slots: (0,) * len(shape))
 
     def slot_block(*shape):
         zeros = (0,) * (len(shape) - 2)
-        return pl.BlockSpec(shape, lambda step, place, slots: (0, slots[place[0]]) + zeros)
+        return pl.BlockSpec(
+            shape, lambda step, request, group, slots: (0, slots[request[0]]) + zeros
+        )
 
     operands = [
         (x_cache, slot_block(1, 1, 3, 128)),
@@ -448,17 +453,20 @@
         (skip_d, whole(skip_d)),
         (norm_gated, whole(norm_gated)),
         (parents, whole(parents)),
-        (ancestors, pl.BlockSpec((1, 64, 64), lambda step, place, slots: (place[0], 0, 0))),
+        (
+            ancestors,
+            pl.BlockSpec((1, 64, 64), lambda step, request, group, slots: (request[0], 0, 0)),
+        ),
     ]
     pack, state = pl.pallas_call(
         prepare_kernel,
         grid_spec=pltpu.PrefetchScalarGridSpec(
-            num_scalar_prefetch=2,
+            num_scalar_prefetch=3,
             grid=(1,),
             in_specs=[spec for _, spec in operands],
             out_specs=[
-                pl.BlockSpec((PACK, 128), lambda step, place, slots: (0, 0)),
-                pl.BlockSpec((2 * P_SIZE, N), lambda step, place, slots: (0, 0)),
+                pl.BlockSpec((PACK, 128), lambda step, request, group, slots: (0, 0)),
+                pl.BlockSpec((2 * P_SIZE, N), lambda step, request, group, slots: (0, 0)),
             ],
         ),
         out_shape=[
@@ -466,7 +474,7 @@
             jax.ShapeDtypeStruct((2 * P_SIZE, N), BF16),
         ],
         compiler_params=params,
-    )(place, slot_ids, *[operand for operand, _ in operands])
+    )(request, group, slot_ids, *[operand for operand, _ in operands])
 
     bc_new = exchange(bc_own, "col")
     bc_new, up_mine, down_mine = lax.optimization_barrier((bc_new, ffn_up, ffn_down))

time: 232 us -> 231 us (level)
  blocking collectives: 54.9 us -> 75.1 us
  waiting for transfers between devices: 86.8 us -> 73.7 us
  starting transfers between devices: 57.1 us -> 49.9 us
    all_to_all x3 -> x4, blocking collectives: 54.9 us -> 75.1 us  [exchange(): lax.all_to_all(parts, axis, 0, 0, tiled=True, axis_index_groups=groups)]
    all_to_all x6 -> x5, waiting for transfers between devices: 82.6 us -> 69.5 us  [exchange(): lax.all_to_all(parts, axis, 0, 0, tiled=True, axis_index_groups=groups)]
    all_to_all x6 -> x5, starting transfers between devices: 45 us -> 37.9 us  [exchange(): lax.all_to_all(parts, axis, 0, 0, tiled=True, axis_index_groups=groups)]
  transfers between devices with their start and end apart: 13 -> 12, of which waited for: 9 -> 8; matrix products, arithmetic and copies ran while one was open for 1% -> 1% of each run, Pallas kernels for 4% -> 4%
where the time goes in v11:
time: 231 us; the launch traced here: 230 us
  blocking collectives  75.1 us (33%)
  waiting for transfers between devices  73.7 us (32%)
  starting transfers between devices  49.9 us (22%)
  between operations  13.8 us (6%)
  Pallas kernels  11.6 us (5%)
  local copies, waits for them, and re-layouts  4.85 us (2%)
    all_to_all x4, blocking collectives, exchange(): lax.all_to_all(parts, axis, 0, 0, tiled=True, axis_index_groups=groups)  75.1 us
    all_to_all x5, waiting for transfers between devices, exchange(): lax.all_to_all(parts, axis, 0, 0, tiled=True, axis_index_groups=groups)  69.5 us
    all_to_all x5, starting transfers between devices, exchange(): lax.all_to_all(parts, axis, 0, 0, tiled=True, axis_index_groups=groups)  37.9 us
  transfers between devices with their start and end apart: 12, of which 8 were waited for; matrix products, arithmetic and copies ran while one was open for 1% of the time, Pallas kernels for 4%

profile of v11, /device:TPU:32, one launch (start us, length us, event | category | flops | bytes accessed | tf_op | source)
XLA Modules:
  0.0 229.8 jit_solution(15488765438929950788)
XLA Ops:
  6.5 0.7 all-gather.3.cloned.1.call-update
  7.3 0.7 copy-done.5
  8.0 0.7 shard_map.199
  8.7 15.2 %all-to-all-start = ((bf16[16,32,256]{2,1,0:T(8,128)(2,1)}), bf16[16,32,256]{2,1,0:T(8,128)(2,1)S(1)}, u32[]{:S(2)}, u32[]{:S(2)}) async-start(bf16[16,32,256]{2,1,0:T(8,128)(2,1)} %shard_map.199), calls=%async_computation | async-start | bytes 524288 | tf_op jit(solution)/shard_map/all_to_all | solution.py:24
  23.9 1.4 reshape.20.main_ref
  25.3 0.1 pad.2.clone
  25.4 0.1 maximum_maximum_fusion
  25.5 17.4 %all-to-all-done = bf16[16,32,256]{2,1,0:T(8,128)(2,1)S(1)} async-done(((bf16[16,32,256]{2,1,0:T(8,128)(2,1)}), bf16[16,32,256]{2,1,0:T(8,128)(2,1)S(1)}, u32[]{:S(2)}, u32[]{:S(2)}) %all-to-all-start) | async-done | bytes 262176 | tf_op jit(solution)/shard_map/all_to_all | solution.py:24
  42.9 0.6 shard_map.201
  43.5 1.9 collective-permute-start
  45.4 0.6 shard_map.200
  46.0 1.5 collective-permute-done
  47.5 0.2 add_convert_fusion
  47.8 20.2 %all_to_all.45.parts_ref = bf16[16,80,256]{2,1,0:T(8,128)(2,1)S(1)} all-to-all(bf16[16,80,256]{2,1,0:T(8,128)(2,1)S(1)} %add_convert_fusion), channel_id=1, replica_groups={{0,32,64,96,128,160,192,224,256,288,320,352,384,416,448,480},{16,48,80,..., dimensions={0} | all-to-all | bytes 1310720 | tf_op jit(solution)/shard_map/all_to_all | solution.py:24
  68.0 0.7 shard_map.202
  68.7 6.7 %all-to-all-start.2 = ((bf16[16,16,128]{2,1,0:T(8,128)(2,1)}), bf16[16,16,128]{2,1,0:T(8,128)(2,1)S(1)}, u32[]{:S(2)}, u32[]{:S(2)}) async-start(bf16[16,16,128]{2,1,0:T(8,128)(2,1)} %get-tuple-element.29), calls=%async_computation.2 | async-start | bytes 131072 | tf_op jit(solution)/shard_map/all_to_all | solution.py:24
  75.5 0.1 copy.29.offset_ref
  75.6 0.1 copy.30.rate_ref
  75.7 0.1 copy.31.skip_ref
  75.8 2.2 shard_map.203
  78.1 9.5 %all-to-all-done.2.bc_new_ref = bf16[16,16,128]{2,1,0:T(8,128)(2,1)S(1)} async-done(((bf16[16,16,128]{2,1,0:T(8,128)(2,1)}), bf16[16,16,128]{2,1,0:T(8,128)(2,1)S(1)}, u32[]{:S(2)}, u32[]{:S(2)}) %all-to-all-start.2) | async-done | bytes 65568 | tf_op jit(solution)/shard_map/all_to_all | solution.py:24
  87.6 0.8 shard_map.204
  88.5 15.5 %all_to_all.46.parts_ref = bf16[16,4,256]{2,1,0:T(4,128)(2,1)S(1)} all-to-all(bf16[16,4,256]{2,1,0:T(4,128)(2,1)S(1)} %shard_map.204), channel_id=1, replica_groups=mesh['row'=32,'col'=16] {'col'}, dimensions={0} | all-to-all | bytes 65536 | tf_op jit(solution)/shard_map/all_to_all | solution.py:24
  104.0 0.9 shard_map.205
  104.8 3.9 %all-to-all-start.4 = ((bf16[32,64,128]{2,1,0:T(8,128)(2,1)}), bf16[32,64,128]{2,1,0:T(8,128)(2,1)S(1)}, u32[]{:S(2)}, u32[]{:S(2)}) async-start(bf16[32,64,128]{2,1,0:T(8,128)(2,1)} %shard_map.205), calls=%async_computation.4 | async-start | bytes 1048576 | tf_op jit(solution)/shard_map/all_to_all | solution.py:24
  108.7 2.1 collective-permute-start.3
  110.8 2.3 collective-permute-start.4
  113.1 7.4 %all-to-all-done.4.heads_ref = bf16[32,64,128]{2,1,0:T(8,128)(2,1)S(1)} async-done(((bf16[32,64,128]{2,1,0:T(8,128)(2,1)}), bf16[32,64,128]{2,1,0:T(8,128)(2,1)S(1)}, u32[]{:S(2)}, u32[]{:S(2)}) %all-to-all-start.4) | async-done | bytes 524320 | tf_op jit(solution)/shard_map/all_to_all | solution.py:24
  120.5 2.2 copy-done
  122.7 0.8 shard_map.206
  123.5 2.0 collective-permute-start.1
  125.5 1.1 collective-permute-done.1.other_ref
  126.6 0.7 shard_map.207
  127.3 4.6 %all-to-all-start.5 = ((bf16[16,16,512]{2,1,0:T(8,128)(2,1)}), bf16[16,16,512]{2,1,0:T(8,128)(2,1)S(1)}, u32[]{:S(2)}, u32[]{:S(2)}) async-start(bf16[16,16,512]{2,1,0:T(8,128)(2,1)} %get-tuple-element.37), calls=%async_computation.5 | async-start | bytes 524288 | tf_op jit(solution)/shard_map/all_to_all | solution.py:24
  131.9 18.9 %all-to-all-done.5.after_ref = bf16[16,16,512]{2,1,0:T(8,128)(2,1)S(1)} async-done(((bf16[16,16,512]{2,1,0:T(8,128)(2,1)}), bf16[16,16,512]{2,1,0:T(8,128)(2,1)S(1)}, u32[]{:S(2)}, u32[]{:S(2)}) %all-to-all-start.5) | async-done | bytes 262176 | tf_op jit(solution)/shard_map/all_to_all | solution.py:24
  150.8 0.7 shard_map.208
  151.5 20.6 %all_to_all.47.parts_ref = bf16[16,16,2176]{2,1,0:T(8,128)(2,1)S(1)} all-to-all(bf16[16,16,2176]{2,1,0:T(8,128)(2,1)S(1)} %shard_map.208), channel_id=1, replica_groups={{0,32,64,96,128,160,192,224,256,288,320,352,384,416,448,480},{16,48,80,..., dimensions={0} | all-to-all | bytes 2228224 | tf_op jit(solution)/shard_map/all_to_all | solution.py:24
  172.1 1.2 shard_map.209
  173.3 18.8 %all_to_all.48.act_ref = bf16[16,16,2048]{2,1,0:T(8,128)(2,1)S(1)} all-to-all(bf16[16,16,2048]{2,1,0:T(8,128)(2,1)S(1)} %get-tuple-element.43), channel_id=1, replica_groups={{0,32,64,96,128,160,192,224,256,288,320,352,384,416,448,480},{16,48,80,..., dimensions={0} | all-to-all | bytes 2097152 | tf_op jit(solution)/shard_map/all_to_all | solution.py:24
  192.1 0.5 shard_map.211
  192.6 1.9 collective-permute-start.5
  194.5 0.5 shard_map.210.mine_ref
  195.0 0.8 collective-permute-done.5.other_ref
  195.8 0.7 shard_map.212
  196.5 7.4 %all-to-all-start.8 = ((bf16[16,32,256]{2,1,0:T(8,128)(2,1)}), bf16[16,32,256]{2,1,0:T(8,128)(2,1)S(1)}, u32[]{:S(2)}, u32[]{:S(2)}) async-start(bf16[16,32,256]{2,1,0:T(8,128)(2,1)} %shard_map.212), calls=%async_computation.8 | async-start | bytes 524288 | tf_op jit(solution)/shard_map/all_to_all | solution.py:24
  204.0 1.9 collective-permute-start.2
  205.9 16.4 %all-to-all-done.8 = bf16[16,32,256]{2,1,0:T(8,128)(2,1)S(1)} async-done(((bf16[16,32,256]{2,1,0:T(8,128)(2,1)}), bf16[16,32,256]{2,1,0:T(8,128)(2,1)S(1)}, u32[]{:S(2)}, u32[]{:S(2)}) %all-to-all-start.8) | async-done | bytes 262176 | tf_op jit(solution)/shard_map/all_to_all | solution.py:24
  222.4 0.6 add_convert_fusion.1
  (52 shorter events, 0.2 us)
Async XLA Ops:
  6.5 18.9 %copy-start.13 = (bf16[256,4,32]{0,2,1:T(8,128)(2,1)S(1)}, bf16[256,4,32]{0,2,1:T(8,128)(2,1)}, u32[]{:S(2)}) copy-start(bf16[256,4,32]{0,2,1:T(8,128)(2,1)} %param.24) | copy-start | bytes 196612
  6.5 18.9 %copy-start.15 = (bf16[256,4,2]{0,2,1:T(2,128)(2,1)S(1)}, bf16[256,4,2]{0,2,1:T(2,128)(2,1)}, u32[]{:S(2)}) copy-start(bf16[256,4,2]{0,2,1:T(2,128)(2,1)} %param.25) | copy-start | bytes 12292
  6.5 36.4 %copy-start.9 = (f32[256]{0:T(256)S(1)}, f32[256]{0:T(256)}, u32[]{:S(2)}) copy-start(f32[256]{0:T(256)} %param.22) | copy-start | bytes 3076
  6.5 113.9 %all-gather.3.cloned.1.call-start = ((), (), s32[]{:S(2)}) async-start(), calls=%async_computation.9 | async-start | bytes 4456448 | tf_op jit(solution)/shard_map/all_gather | solution.py:404
  7.3 0.7 copy-start.5
  8.7 34.2 %all-to-all-start = ((bf16[16,32,256]{2,1,0:T(8,128)(2,1)}), bf16[16,32,256]{2,1,0:T(8,128)(2,1)S(1)}, u32[]{:S(2)}, u32[]{:S(2)}) async-start(bf16[16,32,256]{2,1,0:T(8,128)(2,1)} %shard_map.199), calls=%async_computation | async-start | bytes 524288 | tf_op jit(solution)/shard_map/all_to_all | solution.py:24
  43.5 4.0 %collective-permute-start = (bf16[16,80,256]{2,1,0:T(8,128)(2,1)S(1)}, bf16[16,80,256]{2,1,0:T(8,128)(2,1)S(1)}, u32[]{:S(2)}, u32[]{:S(2)}) collective-permute-start(bf16[16,80,256]{2,1,0:T(8,128)(2,1)S(1)} %shard_map.201), channel_id=1, source_target_pairs={{0,16},{16,0},{32,48},{48,32},{64,80},{80,64},{96,112},{112,96},{1... | collective-permute-start | bytes 1966088 | tf_op jit(solution)/shard_map/ppermute | solution.py:413
  47.6 27.8 %copy-start.14 = (bf16[1,4,3,512]{3,1,2,0:T(4,128)(2,1)S(1)}, bf16[1,4,3,512]{3,1,2,0:T(4,128)(2,1)}, u32[]{:S(2)}) copy-start(bf16[1,4,3,512]{3,1,2,0:T(4,128)(2,1)} %param.32) | copy-start | bytes 36868
  47.6 27.8 %copy-start.16 = (bf16[1,4,3,128]{3,1,2,0:T(4,128)(2,1)S(1)}, bf16[1,4,3,128]{3,1,2,0:T(4,128)(2,1)}, u32[]{:S(2)}) copy-start(bf16[1,4,3,128]{3,1,2,0:T(4,128)(2,1)} %param.31) | copy-start | bytes 9220
  47.7 27.9 %copy-start.17 = (f32[4,2]{0,1:T(2,128)S(1)}, f32[4,2]{0,1:T(2,128)}, u32[]{:S(2)}) copy-start(f32[4,2]{0,1:T(2,128)} %param.26) | copy-start | bytes 100
  47.7 27.9 %copy-start.18 = (f32[4,2]{0,1:T(2,128)S(1)}, f32[4,2]{0,1:T(2,128)}, u32[]{:S(2)}) copy-start(f32[4,2]{0,1:T(2,128)} %param.27) | copy-start | bytes 100
  47.7 28.0 %copy-start.19 = (f32[4,2]{0,1:T(2,128)S(1)}, f32[4,2]{0,1:T(2,128)}, u32[]{:S(2)}) copy-start(f32[4,2]{0,1:T(2,128)} %param.28) | copy-start | bytes 100
  47.7 28.1 %copy-start.3 = (f32[1,4,2,64,256]{4,3,2,1,0:T(8,128)S(1)}, f32[1,4,2,64,256]{4,3,2,1,0:T(8,128)}, u32[]{:S(2)}) copy-start(f32[1,4,2,64,256]{4,3,2,1,0:T(8,128)} %state_ref.1) | copy-start | bytes 1572868
  47.7 28.1 %copy-start.4 = (s32[8,64,64]{2,1,0:T(8,128)S(1)}, s32[8,64,64]{2,1,0:T(8,128)}, u32[]{:S(2)}) copy-start(s32[8,64,64]{2,1,0:T(8,128)} %anc_ref.1) | copy-start | bytes 393220
  47.7 28.1 %copy-start.6 = (bf16[4,4,512]{2,1,0:T(4,128)(2,1)S(1)}, bf16[4,4,512]{2,1,0:T(4,128)(2,1)}, u32[]{:S(2)}) copy-start(bf16[4,4,512]{2,1,0:T(4,128)(2,1)} %bc_taps_ref.1) | copy-start | bytes 49156
  47.7 28.1 %copy-start.7 = (bf16[4,4,128]{2,1,0:T(4,128)(2,1)S(1)}, bf16[4,4,128]{2,1,0:T(4,128)(2,1)}, u32[]{:S(2)}) copy-start(bf16[4,4,128]{2,1,0:T(4,128)(2,1)} %x_taps_ref.1) | copy-start | bytes 12292
  47.7 28.1 %copy-start.8 = (s32[8,64]{1,0:T(8,128)S(1)}, s32[8,64]{1,0:T(8,128)}, u32[]{:S(2)}) copy-start(s32[8,64]{1,0:T(8,128)} %parents_ref.1) | copy-start | bytes 6148
  47.7 28.1 %copy-start.11 = (f32[4,128]{1,0:T(4,128)S(1)}, f32[4,128]{1,0:T(4,128)}, u32[]{:S(2)}) copy-start(f32[4,128]{1,0:T(4,128)} %gain_ref.1) | copy-start | bytes 6148
  47.8 28.1 %copy-start.12 = (s32[8]{0:T(128)S(1)}, s32[8]{0:T(128)}, u32[]{:S(2)}) copy-start(s32[8]{0:T(128)} %slot_ref.1) | copy-start | bytes 100
  68.7 18.9 %all-to-all-start.2 = ((bf16[16,16,128]{2,1,0:T(8,128)(2,1)}), bf16[16,16,128]{2,1,0:T(8,128)(2,1)S(1)}, u32[]{:S(2)}, u32[]{:S(2)}) async-start(bf16[16,16,128]{2,1,0:T(8,128)(2,1)} %get-tuple-element.29), calls=%async_computation.2 | async-start | bytes 131072 | tf_op jit(solution)/shard_map/all_to_all | solution.py:24
  78.1 30.7 %copy-start.1 = (bf16[256,2048]{1,0:T(8,128)(2,1)S(1)}, bf16[256,2048]{1,0:T(8,128)(2,1)}, u32[]{:S(2)}) copy-start(bf16[256,2048]{1,0:T(8,128)(2,1)} %weight_ref) | copy-start | bytes 3145732
  78.1 42.4 %copy-start.10 = (f32[256]{0:T(256)S(1)}, f32[256]{0:T(256)}, u32[]{:S(2)}) copy-start(f32[256]{0:T(256)} %param.39) | copy-start | bytes 3076
  104.8 15.7 %all-to-all-start.4 = ((bf16[32,64,128]{2,1,0:T(8,128)(2,1)}), bf16[32,64,128]{2,1,0:T(8,128)(2,1)S(1)}, u32[]{:S(2)}, u32[]{:S(2)}) async-start(bf16[32,64,128]{2,1,0:T(8,128)(2,1)} %shard_map.205), calls=%async_computation.4 | async-start | bytes 1048576 | tf_op jit(solution)/shard_map/all_to_all | solution.py:24
  108.7 23.2 %collective-permute-start.3 = (bf16[256,2048]{1,0:T(8,128)(2,1)S(1)}, bf16[256,2048]{1,0:T(8,128)(2,1)S(1)}, u32[]{:S(2)}, u32[]{:S(2)}) collective-permute-start(bf16[256,2048]{1,0:T(8,128)(2,1)S(1)} %copy-done.1), channel_id=1, source_target_pairs={{0,16},{16,0},{32,48},{48,32},{64,80},{80,64},{96,112},{112,96},{1... | collective-permute-start | bytes 3145736 | tf_op jit(solution)/shard_map/ppermute | solution.py:482
  110.8 40.7 %collective-permute-start.4 = (bf16[2048,256]{1,0:T(8,128)(2,1)}, bf16[2048,256]{1,0:T(8,128)(2,1)}, u32[]{:S(2)}, u32[]{:S(2)}) collective-permute-start(bf16[2048,256]{1,0:T(8,128)(2,1)} %weight_ref.1), channel_id=1, source_target_pairs={{0,16},{16,0},{32,48},{48,32},{64,80},{80,64},{96,112},{112,96},{1... | collective-permute-start | bytes 3145736 | tf_op jit(solution)/shard_map/ppermute | solution.py:482
  120.5 2.2 copy-start
  123.5 3.1 %collective-permute-start.1 = (bf16[32,256]{1,0:T(8,128)(2,1)S(1)}, bf16[32,256]{1,0:T(8,128)(2,1)S(1)}, u32[]{:S(2)}, u32[]{:S(2)}) collective-permute-start(bf16[32,256]{1,0:T(8,128)(2,1)S(1)} %get-tuple-element.36), channel_id=1, source_target_pairs={{0,16},{16,0},{32,48},{48,32},{64,80},{80,64},{96,112},{112,96},{1... | collective-permute-start | bytes 49160 | tf_op jit(solution)/shard_map/ppermute | solution.py:510
  127.3 23.5 %all-to-all-start.5 = ((bf16[16,16,512]{2,1,0:T(8,128)(2,1)}), bf16[16,16,512]{2,1,0:T(8,128)(2,1)S(1)}, u32[]{:S(2)}, u32[]{:S(2)}) async-start(bf16[16,16,512]{2,1,0:T(8,128)(2,1)} %get-tuple-element.37), calls=%async_computation.5 | async-start | bytes 524288 | tf_op jit(solution)/shard_map/all_to_all | solution.py:24
  192.1 2.4 %copy-start.2 = (bf16[2048,256]{1,0:T(8,128)(2,1)S(1)}, bf16[2048,256]{1,0:T(8,128)(2,1)}, u32[]{:S(2)}) copy-start(bf16[2048,256]{1,0:T(8,128)(2,1)} %weight_ref.1) | copy-start | bytes 3145732
  192.6 3.2 %collective-permute-start.5 = (bf16[8,32,256]{2,1,0:T(8,128)(2,1)S(1)}, bf16[8,32,256]{2,1,0:T(8,128)(2,1)S(1)}, u32[]{:S(2)}, u32[]{:S(2)}) collective-permute-start(bf16[8,32,256]{2,1,0:T(8,128)(2,1)S(1)} %shard_map.211), channel_id=1, source_target_pairs={{0,16},{16,0},{32,48},{48,32},{64,80},{80,64},{96,112},{112,96},{1... | collective-permute-start | bytes 393224 | tf_op jit(solution)/shard_map/ppermute | solution.py:553
  196.5 25.8 %all-to-all-start.8 = ((bf16[16,32,256]{2,1,0:T(8,128)(2,1)}), bf16[16,32,256]{2,1,0:T(8,128)(2,1)S(1)}, u32[]{:S(2)}, u32[]{:S(2)}) async-start(bf16[16,32,256]{2,1,0:T(8,128)(2,1)} %shard_map.212), calls=%async_computation.8 | async-start | bytes 524288 | tf_op jit(solution)/shard_map/all_to_all | solution.py:24
  204.0 18.4 %collective-permute-start.2 = (bf16[32,256]{1,0:T(8,128)(2,1)S(1)}, bf16[32,256]{1,0:T(8,128)(2,1)S(1)}, u32[]{:S(2)}, u32[]{:S(2)}) collective-permute-start(bf16[32,256]{1,0:T(8,128)(2,1)S(1)} %slice.9), channel_id=1, source_target_pairs={{0,16},{16,0},{32,48},{48,32},{64,80},{80,64},{96,112},{112,96},{1... | collective-permute-start | bytes 49160 | tf_op jit(solution)/shard_map/ppermute | solution.py:565
Sparse Core Ops, SparseCore 0:
  9.4 88.2 all-gather.2

commit v12 on v11

--- a/solution.py
+++ b/solution.py
@@ -297,7 +297,43 @@
     gain_ref[...] = terms[0:1, :] + terms[8:9, :]
 
 
-def up_kernel(after_ref, gain_ref, other_gain_ref, weight_ref, other_weight_ref, out_ref):
+def fetch(far_ref, near_ref, done_ref, half):
+    copies = []
+    for part in range(4):
+        rows = pl.ds(half * 1024 + part * 256, 256)
+        near = pl.ds(part * 256, 256)
+        copies.append(
+            pltpu.make_async_copy(far_ref.at[rows], near_ref.at[near], done_ref.at[part])
+        )
+    for copy in copies:
+        copy.start()
+    return copies
+
+
+def up_kernel(
+    after_ref,
+    gain_ref,
+    other_gain_ref,
+    weight_ref,
+    other_weight_ref,
+    far_ref,
+    out_ref,
+    near_ref,
+    done_ref,
+    block_ref,
+    block_done_ref,
+):
+    blocks = [
+        pltpu.make_async_copy(
+            other_weight_ref.at[:, pl.ds(block * 512, 512)],
+            block_ref.at[block],
+            block_done_ref.at[block],
+        )
+        for block in range(4)
+    ]
+    for copy in blocks:
+        copy.start()
+    copies = fetch(far_ref, near_ref, done_ref, 0)
     after = after_ref[...].reshape(256, 512).astype(F32)
     stat = jnp.broadcast_to(jnp.sum(after * after, axis=1, keepdims=True), (256, 128))
     stat = stat.astype(BF16)
@@ -306,25 +342,19 @@
     for block in range(4):
         lanes = slice(block * 512, (block + 1) * 512)
         term = jnp.dot(mine, weight_ref[:, lanes], preferred_element_type=F32)
-        term = term + jnp.dot(other, other_weight_ref[:, lanes], preferred_element_type=F32)
+        blocks[block].wait()
+        term = term + jnp.dot(other, block_ref[block], preferred_element_type=F32)
         term = term.astype(BF16)
         for part in range(16):
             out_ref[part, :, lanes] = term[part * 16 : (part + 1) * 16, :]
     for part in range(16):
         out_ref[part, :, 2048:2176] = stat[part * 16 : (part + 1) * 16, :]
+    for copy in copies:
+        copy.wait()
 
 
 def act_kernel(parts_ref, far_ref, out_ref, near_ref, done_ref):
-    copies = [
-        pltpu.make_async_copy(
-            far_ref.at[pl.ds(part * 512, 512)],
-            near_ref.at[pl.ds(part * 512, 512)],
-            done_ref.at[part],
-        )
-        for part in range(4)
-    ]
-    for copy in copies:
-        copy.start()
+    copies = fetch(far_ref, near_ref, done_ref, 1)
     stat = parts_ref[0, :, 2048:2176].astype(F32)
     for part in range(1, parts_ref.shape[0]):
         stat = stat + parts_ref[part, :, 2048:2176].astype(F32)
@@ -352,9 +382,16 @@
     return turn_ref[...].astype(BF16)
 
 
-def down_kernel(act_ref, weight_ref, out_ref, turn_ref):
+def down_mine_kernel(act_ref, weight_ref, out_ref, turn_ref):
     act = act_ref[...].reshape(256, -1)
     out_ref[...] = turn(jnp.dot(act, weight_ref[...], preferred_element_type=F32), turn_ref)
+
+
+def down_other_kernel(act_ref, upper_ref, lower_ref, out_ref, turn_ref):
+    act = act_ref[...].reshape(256, -1)
+    term = jnp.dot(act[:, 0:1024], upper_ref[...], preferred_element_type=F32)
+    term = term + jnp.dot(act[:, 1024:2048], lower_ref[...], preferred_element_type=F32)
+    out_ref[...] = turn(term, turn_ref)
 
 
 def join_kernel(parity_ref, mine_ref, other_ref, out_ref):
@@ -518,46 +555,44 @@
         after_other,
     )
     after = exchange(copies, "col")
-    up_parts = call(
+    half_shape = jax.ShapeDtypeStruct((1024, 256), BF16)
+    fetches = [pltpu.SemaphoreType.DMA((4,))]
+    up_parts, upper = pl.pallas_call(
         up_kernel,
-        jax.ShapeDtypeStruct((16, 16, 2176), BF16),
-        after,
-        gain_mine,
-        gain_other,
-        up_mine,
-        up_other,
-    )
-    up_parts, down_other = lax.optimization_barrier((up_parts, down_other))
+        out_shape=(jax.ShapeDtypeStruct((16, 16, 2176), BF16), half_shape),
+        in_specs=[vmem, vmem, vmem, vmem, hbm, hbm],
+        out_specs=(vmem, vmem),
+        scratch_shapes=fetches
+        + [pltpu.VMEM((4, 256, 512), BF16), pltpu.SemaphoreType.DMA((4,))],
+        compiler_params=params,
+    )(after, gain_mine, gain_other, up_mine, up_other, down_other)
     up_parts = exchange(up_parts, "row", halves)
-    act, down_other = pl.pallas_call(
+    act, lower = pl.pallas_call(
         act_kernel,
-        out_shape=(
-            jax.ShapeDtypeStruct((16, 16, 2048), BF16),
-            jax.ShapeDtypeStruct((2048, 256), BF16),
-        ),
+        out_shape=(jax.ShapeDtypeStruct((16, 16, 2048), BF16), half_shape),
         in_specs=[vmem, hbm],
         out_specs=(vmem, vmem),
-        scratch_shapes=[pltpu.SemaphoreType.DMA((4,))],
+        scratch_shapes=fetches,
         compiler_params=params,
     )(up_parts, down_other)
     act = exchange(act, "row", halves)
 
-    def down_half(weight):
+    def down_half(kernel, *weights):
         return pl.pallas_call(
-            down_kernel,
+            kernel,
             out_shape=jax.ShapeDtypeStruct((8, 32, 256), BF16),
             scratch_shapes=[pltpu.VMEM((8, 32, 256), F32)],
             compiler_params=params,
-        )(act, weight)
-
-    from_other = lax.ppermute(down_half(down_other), "row", swap)
+        )(act, *weights)
+
+    from_other = lax.ppermute(down_half(down_other_kernel, upper, lower), "row", swap)
     down = pl.pallas_call(
         join_kernel,
         out_shape=jax.ShapeDtypeStruct((cols, 32, 256), BF16),
         in_specs=[smem, vmem, vmem],
         out_specs=vmem,
         compiler_params=params,
-    )(parity, down_half(down_mine), from_other)
+    )(parity, down_half(down_mine_kernel, down_mine), from_other)
     ffn_out = jnp.sum(exchange(down, "col").astype(F32), axis=0)
     own = lax.dynamic_slice(
         after, (8 * (col_index % 2), 4 * (col_index // 2 % 4), 0), (8, 4, 512)

time: 231 us -> 232 us (level)
  no operation moved by 1% of the time
where the time goes in v12:
time: 232 us; the launch traced here: 231 us
  blocking collectives  75.1 us (32%)
  waiting for transfers between devices  73.7 us (32%)
  starting transfers between devices  49.9 us (22%)
  between operations  13.8 us (6%)
  Pallas kernels  12.9 us (6%)
  local copies, waits for them, and re-layouts  4.85 us (2%)
    all_to_all x4, blocking collectives, exchange(): lax.all_to_all(parts, axis, 0, 0, tiled=True, axis_index_groups=groups)  75.1 us
    all_to_all x5, waiting for transfers between devices, exchange(): lax.all_to_all(parts, axis, 0, 0, tiled=True, axis_index_groups=groups)  69.5 us
    all_to_all x5, starting transfers between devices, exchange(): lax.all_to_all(parts, axis, 0, 0, tiled=True, axis_index_groups=groups)  37.9 us
  transfers between devices with their start and end apart: 12, of which 8 were waited for; matrix products, arithmetic and copies ran while one was open for 1% of the time, Pallas kernels for 4%

profile of v12, /device:TPU:32, one launch (start us, length us, event | category | flops | bytes accessed | tf_op | source)
XLA Modules:
  0.0 231.2 jit_solution(4065257340695028888)
XLA Ops:
  6.5 0.7 all-gather.3.cloned.1.call-update
  7.3 0.7 copy-done.5
  8.0 0.7 shard_map.199
  8.7 15.2 %all-to-all-start = ((bf16[16,32,256]{2,1,0:T(8,128)(2,1)}), bf16[16,32,256]{2,1,0:T(8,128)(2,1)S(1)}, u32[]{:S(2)}, u32[]{:S(2)}) async-start(bf16[16,32,256]{2,1,0:T(8,128)(2,1)} %shard_map.199), calls=%async_computation | async-start | bytes 524288 | tf_op jit(solution)/shard_map/all_to_all | solution.py:24
  23.9 1.4 reshape.20.main_ref
  25.3 0.1 pad.2.clone
  25.4 0.1 maximum_maximum_fusion
  25.5 17.4 %all-to-all-done = bf16[16,32,256]{2,1,0:T(8,128)(2,1)S(1)} async-done(((bf16[16,32,256]{2,1,0:T(8,128)(2,1)}), bf16[16,32,256]{2,1,0:T(8,128)(2,1)S(1)}, u32[]{:S(2)}, u32[]{:S(2)}) %all-to-all-start) | async-done | bytes 262176 | tf_op jit(solution)/shard_map/all_to_all | solution.py:24
  42.9 0.6 shard_map.201
  43.5 1.9 collective-permute-start
  45.4 0.6 shard_map.200
  46.0 1.5 collective-permute-done
  47.5 0.2 add_convert_fusion
  47.8 20.2 %all_to_all.45.parts_ref = bf16[16,80,256]{2,1,0:T(8,128)(2,1)S(1)} all-to-all(bf16[16,80,256]{2,1,0:T(8,128)(2,1)S(1)} %add_convert_fusion), channel_id=1, replica_groups={{0,32,64,96,128,160,192,224,256,288,320,352,384,416,448,480},{16,48,80,..., dimensions={0} | all-to-all | bytes 1310720 | tf_op jit(solution)/shard_map/all_to_all | solution.py:24
  68.0 0.7 shard_map.202
  68.7 6.7 %all-to-all-start.2 = ((bf16[16,16,128]{2,1,0:T(8,128)(2,1)}), bf16[16,16,128]{2,1,0:T(8,128)(2,1)S(1)}, u32[]{:S(2)}, u32[]{:S(2)}) async-start(bf16[16,16,128]{2,1,0:T(8,128)(2,1)} %get-tuple-element.29), calls=%async_computation.2 | async-start | bytes 131072 | tf_op jit(solution)/shard_map/all_to_all | solution.py:24
  75.5 0.1 copy.29.offset_ref
  75.6 0.1 copy.30.rate_ref
  75.7 0.1 copy.31.skip_ref
  75.9 2.2 shard_map.203
  78.1 9.6 %all-to-all-done.2.bc_new_ref = bf16[16,16,128]{2,1,0:T(8,128)(2,1)S(1)} async-done(((bf16[16,16,128]{2,1,0:T(8,128)(2,1)}), bf16[16,16,128]{2,1,0:T(8,128)(2,1)S(1)}, u32[]{:S(2)}, u32[]{:S(2)}) %all-to-all-start.2) | async-done | bytes 65568 | tf_op jit(solution)/shard_map/all_to_all | solution.py:24
  87.6 0.8 shard_map.204
  88.5 15.5 %all_to_all.46.parts_ref = bf16[16,4,256]{2,1,0:T(4,128)(2,1)S(1)} all-to-all(bf16[16,4,256]{2,1,0:T(4,128)(2,1)S(1)} %shard_map.204), channel_id=1, replica_groups=mesh['row'=32,'col'=16] {'col'}, dimensions={0} | all-to-all | bytes 65536 | tf_op jit(solution)/shard_map/all_to_all | solution.py:24
  104.0 0.9 shard_map.205
  104.9 3.9 %all-to-all-start.4 = ((bf16[32,64,128]{2,1,0:T(8,128)(2,1)}), bf16[32,64,128]{2,1,0:T(8,128)(2,1)S(1)}, u32[]{:S(2)}, u32[]{:S(2)}) async-start(bf16[32,64,128]{2,1,0:T(8,128)(2,1)} %shard_map.205), calls=%async_computation.4 | async-start | bytes 1048576 | tf_op jit(solution)/shard_map/all_to_all | solution.py:24
  108.8 2.1 collective-permute-start.3
  110.9 2.3 collective-permute-start.4
  113.2 7.4 %all-to-all-done.4.heads_ref = bf16[32,64,128]{2,1,0:T(8,128)(2,1)S(1)} async-done(((bf16[32,64,128]{2,1,0:T(8,128)(2,1)}), bf16[32,64,128]{2,1,0:T(8,128)(2,1)S(1)}, u32[]{:S(2)}, u32[]{:S(2)}) %all-to-all-start.4) | async-done | bytes 524320 | tf_op jit(solution)/shard_map/all_to_all | solution.py:24
  120.5 2.2 copy-done
  122.7 0.8 shard_map.206
  123.5 2.0 collective-permute-start.1
  125.5 1.1 collective-permute-done.1.other_ref
  126.6 0.7 shard_map.207
  127.3 4.6 %all-to-all-start.5 = ((bf16[16,16,512]{2,1,0:T(8,128)(2,1)}), bf16[16,16,512]{2,1,0:T(8,128)(2,1)S(1)}, u32[]{:S(2)}, u32[]{:S(2)}) async-start(bf16[16,16,512]{2,1,0:T(8,128)(2,1)} %get-tuple-element.37), calls=%async_computation.5 | async-start | bytes 524288 | tf_op jit(solution)/shard_map/all_to_all | solution.py:24
  132.0 18.9 %all-to-all-done.5.after_ref = bf16[16,16,512]{2,1,0:T(8,128)(2,1)S(1)} async-done(((bf16[16,16,512]{2,1,0:T(8,128)(2,1)}), bf16[16,16,512]{2,1,0:T(8,128)(2,1)S(1)}, u32[]{:S(2)}, u32[]{:S(2)}) %all-to-all-start.5) | async-done | bytes 262176 | tf_op jit(solution)/shard_map/all_to_all | solution.py:24
  150.8 2.3 shard_map.208
  153.1 20.6 %all_to_all.47.parts_ref = bf16[16,16,2176]{2,1,0:T(8,128)(2,1)S(1)} all-to-all(bf16[16,16,2176]{2,1,0:T(8,128)(2,1)S(1)} %get-tuple-element.41), channel_id=1, replica_groups={{0,32,64,96,128,160,192,224,256,288,320,352,384,416,448,480},{16,48,80,..., dimensions={0} | all-to-all | bytes 2228224 | tf_op jit(solution)/shard_map/all_to_all | solution.py:24
  173.7 1.0 shard_map.209
  174.7 18.8 %all_to_all.48.act_ref = bf16[16,16,2048]{2,1,0:T(8,128)(2,1)S(1)} all-to-all(bf16[16,16,2048]{2,1,0:T(8,128)(2,1)S(1)} %get-tuple-element.42), channel_id=1, replica_groups={{0,32,64,96,128,160,192,224,256,288,320,352,384,416,448,480},{16,48,80,..., dimensions={0} | all-to-all | bytes 2097152 | tf_op jit(solution)/shard_map/all_to_all | solution.py:24
  193.5 0.5 shard_map.211
  193.9 1.9 collective-permute-start.5
  195.9 0.5 shard_map.210.mine_ref
  196.3 0.8 collective-permute-done.5.other_ref
  197.2 0.7 shard_map.212
  197.9 7.4 %all-to-all-start.8 = ((bf16[16,32,256]{2,1,0:T(8,128)(2,1)}), bf16[16,32,256]{2,1,0:T(8,128)(2,1)S(1)}, u32[]{:S(2)}, u32[]{:S(2)}) async-start(bf16[16,32,256]{2,1,0:T(8,128)(2,1)} %shard_map.212), calls=%async_computation.8 | async-start | bytes 524288 | tf_op jit(solution)/shard_map/all_to_all | solution.py:24
  205.3 1.9 collective-permute-start.2
  207.3 16.4 %all-to-all-done.8 = bf16[16,32,256]{2,1,0:T(8,128)(2,1)S(1)} async-done(((bf16[16,32,256]{2,1,0:T(8,128)(2,1)}), bf16[16,32,256]{2,1,0:T(8,128)(2,1)S(1)}, u32[]{:S(2)}, u32[]{:S(2)}) %all-to-all-start.8) | async-done | bytes 262176 | tf_op jit(solution)/shard_map/all_to_all | solution.py:24
  223.7 0.6 add_convert_fusion.1
  (52 shorter events, 0.2 us)
Async XLA Ops:
  6.5 18.9 %copy-start.13 = (bf16[256,4,32]{0,2,1:T(8,128)(2,1)S(1)}, bf16[256,4,32]{0,2,1:T(8,128)(2,1)}, u32[]{:S(2)}) copy-start(bf16[256,4,32]{0,2,1:T(8,128)(2,1)} %param.24) | copy-start | bytes 196612
  6.5 18.9 %copy-start.15 = (bf16[256,4,2]{0,2,1:T(2,128)(2,1)S(1)}, bf16[256,4,2]{0,2,1:T(2,128)(2,1)}, u32[]{:S(2)}) copy-start(bf16[256,4,2]{0,2,1:T(2,128)(2,1)} %param.25) | copy-start | bytes 12292
  6.5 36.4 %copy-start.9 = (f32[256]{0:T(256)S(1)}, f32[256]{0:T(256)}, u32[]{:S(2)}) copy-start(f32[256]{0:T(256)} %param.22) | copy-start | bytes 3076
  6.5 114.0 %all-gather.3.cloned.1.call-start = ((), (), s32[]{:S(2)}) async-start(), calls=%async_computation.9 | async-start | bytes 4456448 | tf_op jit(solution)/shard_map/all_gather | solution.py:441
  7.3 0.7 copy-start.5
  8.7 34.2 %all-to-all-start = ((bf16[16,32,256]{2,1,0:T(8,128)(2,1)}), bf16[16,32,256]{2,1,0:T(8,128)(2,1)S(1)}, u32[]{:S(2)}, u32[]{:S(2)}) async-start(bf16[16,32,256]{2,1,0:T(8,128)(2,1)} %shard_map.199), calls=%async_computation | async-start | bytes 524288 | tf_op jit(solution)/shard_map/all_to_all | solution.py:24
  43.5 4.0 %collective-permute-start = (bf16[16,80,256]{2,1,0:T(8,128)(2,1)S(1)}, bf16[16,80,256]{2,1,0:T(8,128)(2,1)S(1)}, u32[]{:S(2)}, u32[]{:S(2)}) collective-permute-start(bf16[16,80,256]{2,1,0:T(8,128)(2,1)S(1)} %shard_map.201), channel_id=1, source_target_pairs={{0,16},{16,0},{32,48},{48,32},{64,80},{80,64},{96,112},{112,96},{1... | collective-permute-start | bytes 1966088 | tf_op jit(solution)/shard_map/ppermute | solution.py:450
  47.6 27.9 %copy-start.14 = (bf16[1,4,3,512]{3,1,2,0:T(4,128)(2,1)S(1)}, bf16[1,4,3,512]{3,1,2,0:T(4,128)(2,1)}, u32[]{:S(2)}) copy-start(bf16[1,4,3,512]{3,1,2,0:T(4,128)(2,1)} %param.32) | copy-start | bytes 36868
  47.6 27.9 %copy-start.16 = (bf16[1,4,3,128]{3,1,2,0:T(4,128)(2,1)S(1)}, bf16[1,4,3,128]{3,1,2,0:T(4,128)(2,1)}, u32[]{:S(2)}) copy-start(bf16[1,4,3,128]{3,1,2,0:T(4,128)(2,1)} %param.31) | copy-start | bytes 9220
  47.7 27.9 %copy-start.17 = (f32[4,2]{0,1:T(2,128)S(1)}, f32[4,2]{0,1:T(2,128)}, u32[]{:S(2)}) copy-start(f32[4,2]{0,1:T(2,128)} %param.26) | copy-start | bytes 100
  47.7 28.0 %copy-start.18 = (f32[4,2]{0,1:T(2,128)S(1)}, f32[4,2]{0,1:T(2,128)}, u32[]{:S(2)}) copy-start(f32[4,2]{0,1:T(2,128)} %param.27) | copy-start | bytes 100
  47.7 28.0 %copy-start.19 = (f32[4,2]{0,1:T(2,128)S(1)}, f32[4,2]{0,1:T(2,128)}, u32[]{:S(2)}) copy-start(f32[4,2]{0,1:T(2,128)} %param.28) | copy-start | bytes 100
  47.7 28.1 %copy-start.3 = (f32[1,4,2,64,256]{4,3,2,1,0:T(8,128)S(1)}, f32[1,4,2,64,256]{4,3,2,1,0:T(8,128)}, u32[]{:S(2)}) copy-start(f32[1,4,2,64,256]{4,3,2,1,0:T(8,128)} %state_ref.1) | copy-start | bytes 1572868
  47.7 28.1 %copy-start.4 = (s32[8,64,64]{2,1,0:T(8,128)S(1)}, s32[8,64,64]{2,1,0:T(8,128)}, u32[]{:S(2)}) copy-start(s32[8,64,64]{2,1,0:T(8,128)} %anc_ref.1) | copy-start | bytes 393220
  47.7 28.1 %copy-start.6 = (bf16[4,4,512]{2,1,0:T(4,128)(2,1)S(1)}, bf16[4,4,512]{2,1,0:T(4,128)(2,1)}, u32[]{:S(2)}) copy-start(bf16[4,4,512]{2,1,0:T(4,128)(2,1)} %bc_taps_ref.1) | copy-start | bytes 49156
  47.7 28.1 %copy-start.7 = (bf16[4,4,128]{2,1,0:T(4,128)(2,1)S(1)}, bf16[4,4,128]{2,1,0:T(4,128)(2,1)}, u32[]{:S(2)}) copy-start(bf16[4,4,128]{2,1,0:T(4,128)(2,1)} %x_taps_ref.1) | copy-start | bytes 12292
  47.7 28.1 %copy-start.8 = (s32[8,64]{1,0:T(8,128)S(1)}, s32[8,64]{1,0:T(8,128)}, u32[]{:S(2)}) copy-start(s32[8,64]{1,0:T(8,128)} %parents_ref.1) | copy-start | bytes 6148
  47.7 28.1 %copy-start.11 = (f32[4,128]{1,0:T(4,128)S(1)}, f32[4,128]{1,0:T(4,128)}, u32[]{:S(2)}) copy-start(f32[4,128]{1,0:T(4,128)} %gain_ref.1) | copy-start | bytes 6148
  47.8 28.1 %copy-start.12 = (s32[8]{0:T(128)S(1)}, s32[8]{0:T(128)}, u32[]{:S(2)}) copy-start(s32[8]{0:T(128)} %slot_ref.1) | copy-start | bytes 100
  68.7 18.9 %all-to-all-start.2 = ((bf16[16,16,128]{2,1,0:T(8,128)(2,1)}), bf16[16,16,128]{2,1,0:T(8,128)(2,1)S(1)}, u32[]{:S(2)}, u32[]{:S(2)}) async-start(bf16[16,16,128]{2,1,0:T(8,128)(2,1)} %get-tuple-element.29), calls=%async_computation.2 | async-start | bytes 131072 | tf_op jit(solution)/shard_map/all_to_all | solution.py:24
  78.1 30.7 %copy-start.1 = (bf16[256,2048]{1,0:T(8,128)(2,1)S(1)}, bf16[256,2048]{1,0:T(8,128)(2,1)}, u32[]{:S(2)}) copy-start(bf16[256,2048]{1,0:T(8,128)(2,1)} %weight_ref) | copy-start | bytes 3145732
  78.1 42.5 %copy-start.10 = (f32[256]{0:T(256)S(1)}, f32[256]{0:T(256)}, u32[]{:S(2)}) copy-start(f32[256]{0:T(256)} %param.39) | copy-start | bytes 3076
  104.9 15.7 %all-to-all-start.4 = ((bf16[32,64,128]{2,1,0:T(8,128)(2,1)}), bf16[32,64,128]{2,1,0:T(8,128)(2,1)S(1)}, u32[]{:S(2)}, u32[]{:S(2)}) async-start(bf16[32,64,128]{2,1,0:T(8,128)(2,1)} %shard_map.205), calls=%async_computation.4 | async-start | bytes 1048576 | tf_op jit(solution)/shard_map/all_to_all | solution.py:24
  108.8 23.1 %collective-permute-start.3 = (bf16[256,2048]{1,0:T(8,128)(2,1)S(1)}, bf16[256,2048]{1,0:T(8,128)(2,1)}, u32[]{:S(2)}, u32[]{:S(2)}) collective-permute-start(bf16[256,2048]{1,0:T(8,128)(2,1)S(1)} %copy-done.1), channel_id=1, source_target_pairs={{0,16},{16,0},{32,48},{48,32},{64,80},{80,64},{96,112},{112,96},{1... | collective-permute-start | bytes 3145736 | tf_op jit(solution)/shard_map/ppermute | solution.py:519
  110.9 21.1 %collective-permute-start.4 = (bf16[2048,256]{1,0:T(8,128)(2,1)}, bf16[2048,256]{1,0:T(8,128)(2,1)S(1)}, u32[]{:S(2)}, u32[]{:S(2)}) collective-permute-start(bf16[2048,256]{1,0:T(8,128)(2,1)} %weight_ref.1), channel_id=1, source_target_pairs={{0,16},{16,0},{32,48},{48,32},{64,80},{80,64},{96,112},{112,96},{1... | collective-permute-start | bytes 3145736 | tf_op jit(solution)/shard_map/ppermute | solution.py:519
  120.5 2.2 copy-start
  123.5 3.1 %collective-permute-start.1 = (bf16[32,256]{1,0:T(8,128)(2,1)S(1)}, bf16[32,256]{1,0:T(8,128)(2,1)S(1)}, u32[]{:S(2)}, u32[]{:S(2)}) collective-permute-start(bf16[32,256]{1,0:T(8,128)(2,1)S(1)} %get-tuple-element.36), channel_id=1, source_target_pairs={{0,16},{16,0},{32,48},{48,32},{64,80},{80,64},{96,112},{112,96},{1... | collective-permute-start | bytes 49160 | tf_op jit(solution)/shard_map/ppermute | solution.py:547
  127.3 23.5 %all-to-all-start.5 = ((bf16[16,16,512]{2,1,0:T(8,128)(2,1)}), bf16[16,16,512]{2,1,0:T(8,128)(2,1)S(1)}, u32[]{:S(2)}, u32[]{:S(2)}) async-start(bf16[16,16,512]{2,1,0:T(8,128)(2,1)} %get-tuple-element.37), calls=%async_computation.5 | async-start | bytes 524288 | tf_op jit(solution)/shard_map/all_to_all | solution.py:24
  193.5 2.4 %copy-start.2 = (bf16[2048,256]{1,0:T(8,128)(2,1)S(1)}, bf16[2048,256]{1,0:T(8,128)(2,1)}, u32[]{:S(2)}) copy-start(bf16[2048,256]{1,0:T(8,128)(2,1)} %weight_ref.1) | copy-start | bytes 3145732
  193.9 3.2 %collective-permute-start.5 = (bf16[8,32,256]{2,1,0:T(8,128)(2,1)S(1)}, bf16[8,32,256]{2,1,0:T(8,128)(2,1)S(1)}, u32[]{:S(2)}, u32[]{:S(2)}) collective-permute-start(bf16[8,32,256]{2,1,0:T(8,128)(2,1)S(1)} %shard_map.211), channel_id=1, source_target_pairs={{0,16},{16,0},{32,48},{48,32},{64,80},{80,64},{96,112},{112,96},{1... | collective-permute-start | bytes 393224 | tf_op jit(solution)/shard_map/ppermute | solution.py:588
  197.9 25.8 %all-to-all-start.8 = ((bf16[16,32,256]{2,1,0:T(8,128)(2,1)}), bf16[16,32,256]{2,1,0:T(8,128)(2,1)S(1)}, u32[]{:S(2)}, u32[]{:S(2)}) async-start(bf16[16,32,256]{2,1,0:T(8,128)(2,1)} %shard_map.212), calls=%async_computation.8 | async-start | bytes 524288 | tf_op jit(solution)/shard_map/all_to_all | solution.py:24
  205.3 18.4 %collective-permute-start.2 = (bf16[32,256]{1,0:T(8,128)(2,1)S(1)}, bf16[32,256]{1,0:T(8,128)(2,1)S(1)}, u32[]{:S(2)}, u32[]{:S(2)}) collective-permute-start(bf16[32,256]{1,0:T(8,128)(2,1)S(1)} %slice.9), channel_id=1, source_target_pairs={{0,16},{16,0},{32,48},{48,32},{64,80},{80,64},{96,112},{112,96},{1... | collective-permute-start | bytes 49160 | tf_op jit(solution)/shard_map/ppermute | solution.py:600
Sparse Core Ops, SparseCore 0:
  9.4 88.4 all-gather.2
